TPU v7x, 512 devices: a whole 4x8x8 slice. The times are simulated.
512 devices in a mesh: row: 16 (over z, core), col: 32 (over x, y).
Axes of the slice: x: 4, y: 8, z: 8, core: 2. Of those that a mesh axis runs over, the one named last changes fastest.
Arguments:
- tokens_in: bfloat16 [320, 6144], P('col', 'row'), may hold values from -6 to 6
- layer_norm_gain: float32 [6144], P('row'), may hold values from 0.5 to 1.5
- w_qkv: bfloat16 [6144, 3, 4096], P('row', None, 'col'), may hold values from -0.063788795 to 0.063788795
- qk_gain: float32 [2, 4096], P(None, 'col'), may hold values from 0.6 to 3.75
- w_up: bfloat16 [6144, 24576], P('row', 'col'), may hold values from -0.078125 to 0.078125
- w_attn_out: bfloat16 [4096, 6144], P('col', 'row'), may hold values from -0.09375 to 0.09375
- w_down: bfloat16 [24576, 6144], P('col', 'row'), may hold values from -0.0390625 to 0.0390625
- cotangent: bfloat16 [320, 6144], P('col', 'row'), may hold values from -6 to 6
Outputs:
- layer_out: bfloat16 [320, 6144], P('col', 'row')
- token_input_gradient: bfloat16 [320, 6144], P('col', 'row')
- layer_norm_gain_gradient: float32 [6144], P('row')
- d_w_qkv: bfloat16 [6144, 3, 4096], P('row', None, 'col')
- d_qk_gain: float32 [2, 4096], P(None, 'col')
- d_w_up: bfloat16 [6144, 24576], P('row', 'col')
- d_w_attn_out: bfloat16 [4096, 6144], P('col', 'row')
- d_w_down: bfloat16 [24576, 6144], P('col', 'row')
All inputs are finite; a program needn't handle non-finite values.
Results may differ from a plain program's by a relative error of at most 0.022.
Values may be sent and summed in bfloat16 or wider, within the bound.
No kernel may reach another device: no remote copies, remote signals or barrier semaphores. Data moves between devices by JAX's collectives and lax.ppermute only.
A program may use at most 64 MiB of HBM per device.

v0:
```python
import jax
import jax.numpy as jnp
from jax import lax
from jax.sharding import PartitionSpec as P

HEAD_DIM = 128


def qk_norm(values, gain_vec):
    centred = values - jnp.mean(values, -1, keepdims=True)
    variance = jnp.mean(centred * centred, -1, keepdims=True)
    return (
        centred * lax.rsqrt(variance + 1e-06) * gain_vec.reshape(values.shape[1], values.shape[2])
    )


def shards(tokens_in, layer_norm_gain, w_qkv, qk_gain, w_up, w_attn_out, w_down, cotangent):
    rows_c, width_r = tokens_in.shape
    n_row = lax.axis_size("row")
    tokens = rows_c * lax.axis_size("col")
    rows_r = tokens // n_row
    model_width_value = width_r * n_row
    head_w = w_qkv.shape[2]
    local_heads = head_w // HEAD_DIM
    score_scale = HEAD_DIM ** (-0.5)
    contract_rows = (((0,), (0,)), ((), ()))
    contract_cols = (((1,), (1,)), ((), ()))
    input_single_precision = tokens_in.astype(jnp.float32)
    row_sum, row_square = lax.psum(
        (
            jnp.sum(input_single_precision, 1),
            jnp.sum(input_single_precision * input_single_precision, 1),
        ),
        "row",
    )
    token_row_average = row_sum / model_width_value
    variance = row_square / model_width_value - token_row_average * token_row_average
    inverse_deviation = lax.rsqrt(variance + 1e-06)
    centered_scaled_input = (
        input_single_precision - token_row_average[:, None]
    ) * inverse_deviation[:, None]
    normalized_tokens = (centered_scaled_input * layer_norm_gain).astype(jnp.bfloat16)
    normed_all = lax.all_gather(normalized_tokens, "col", axis=0, tiled=True)
    w_in = jnp.concatenate([w_qkv.reshape(width_r, 3 * head_w), w_up], 1)
    merged = lax.psum_scatter(
        jnp.dot(normed_all, w_in, preferred_element_type=jnp.float32),
        "row",
        scatter_dimension=0,
        tiled=True,
    )
    query = merged[:, :head_w]
    up_rows = merged[:, 3 * head_w :]
    k_normed, k_back = jax.vjp(
        qk_norm, merged[:, head_w : 2 * head_w].reshape(rows_r, local_heads, HEAD_DIM), qk_gain[1]
    )
    v_local = (
        merged[:, 2 * head_w : 3 * head_w]
        .astype(jnp.bfloat16)
        .reshape(rows_r, local_heads, HEAD_DIM)
    )
    k_all, v_all = (
        lax.all_gather(k_normed.astype(jnp.bfloat16), "row", axis=0, tiled=True),
        lax.all_gather(v_local, "row", axis=0, tiled=True),
    )
    q_normed, q_back = jax.vjp(qk_norm, query.reshape(rows_r, local_heads, HEAD_DIM), qk_gain[0])
    q_rows = q_normed.astype(jnp.bfloat16)
    scores = (
        jnp.einsum("qhd,khd->hqk", q_rows, k_all, preferred_element_type=jnp.float32) * score_scale
    )
    probs = jax.nn.softmax(scores, -1)
    prob_low = probs.astype(jnp.bfloat16)
    attended = jnp.einsum("hqk,khd->qhd", prob_low, v_all, preferred_element_type=jnp.float32)
    attended = attended.astype(jnp.bfloat16).reshape(rows_r, head_w)
    hidden_f, gelu_back = jax.vjp(jax.nn.gelu, up_rows)
    hidden = hidden_f.astype(jnp.bfloat16)
    joined = jnp.concatenate([attended, hidden], 1)
    joined_all = lax.all_gather(joined, "row", axis=0, tiled=True)
    w_cat = jnp.concatenate([w_attn_out, w_down], 0)
    branch = lax.psum_scatter(
        jnp.dot(joined_all, w_cat, preferred_element_type=jnp.float32).astype(jnp.bfloat16),
        "col",
        scatter_dimension=0,
        tiled=True,
    ).astype(jnp.float32)
    layer_out = (input_single_precision + branch).astype(jnp.bfloat16)
    cot_all = lax.all_gather(cotangent, "col", axis=0, tiled=True)
    d_cat = lax.dot_general(joined_all, cot_all, contract_rows, preferred_element_type=jnp.float32)
    d_w_attn_out = d_cat[:head_w].astype(jnp.bfloat16)
    d_w_down = d_cat[head_w:].astype(jnp.bfloat16)
    d_joined = lax.psum_scatter(
        lax.dot_general(cot_all, w_cat, contract_cols, preferred_element_type=jnp.float32),
        "row",
        scatter_dimension=0,
        tiled=True,
    )
    d_attended = d_joined[:, :head_w].astype(jnp.bfloat16).reshape(rows_r, local_heads, HEAD_DIM)
    d_hidden = d_joined[:, head_w:].astype(jnp.bfloat16)
    d_up = gelu_back(d_hidden.astype(jnp.float32))[0].astype(jnp.bfloat16)
    d_probs = jnp.einsum("qhd,khd->hqk", d_attended, v_all, preferred_element_type=jnp.float32)
    row_delta = jnp.sum(probs * d_probs, -1, keepdims=True)
    d_scores = (probs * (d_probs - row_delta)).astype(jnp.bfloat16)
    d_qn = (
        jnp.einsum("hqk,khd->qhd", d_scores, k_all, preferred_element_type=jnp.float32)
        * score_scale
    )
    d_kn_part = (
        jnp.einsum("hqk,qhd->khd", d_scores, q_rows, preferred_element_type=jnp.float32)
        * score_scale
    )
    d_value_part = jnp.einsum(
        "hqk,qhd->khd", prob_low, d_attended, preferred_element_type=jnp.float32
    )
    d_query, d_q_gain = q_back(d_qn)
    d_query_low = d_query.astype(jnp.bfloat16).reshape(rows_r, head_w)
    d_kn_rows, d_value_rows = (
        lax.psum_scatter(
            d_kn_part.astype(jnp.bfloat16), "row", scatter_dimension=0, tiled=True
        ).astype(jnp.float32),
        lax.psum_scatter(
            d_value_part.astype(jnp.bfloat16), "row", scatter_dimension=0, tiled=True
        ).astype(jnp.float32),
    )
    d_key, d_k_gain = k_back(d_kn_rows)
    gain_q, gain_k = lax.psum((d_q_gain, d_k_gain), "row")
    d_qk_gain = jnp.stack([gain_q, gain_k])
    d_merged = jnp.concatenate(
        [
            d_query_low,
            d_key.astype(jnp.bfloat16).reshape(rows_r, head_w),
            d_value_rows.astype(jnp.bfloat16).reshape(rows_r, head_w),
            d_up,
        ],
        1,
    )
    d_merged_all = lax.all_gather(d_merged, "row", axis=0, tiled=True)
    d_w_in = lax.dot_general(
        normed_all, d_merged_all, contract_rows, preferred_element_type=jnp.float32
    )
    d_w_qkv = d_w_in[:, : 3 * head_w].reshape(width_r, 3, head_w).astype(jnp.bfloat16)
    d_w_up = d_w_in[:, 3 * head_w :].astype(jnp.bfloat16)
    normalized_rows_gradient = lax.psum_scatter(
        lax.dot_general(
            d_merged_all, w_in, contract_cols, preferred_element_type=jnp.float32
        ).astype(jnp.bfloat16),
        "col",
        scatter_dimension=0,
        tiled=True,
    ).astype(jnp.float32)
    partial_gain_gradient = jnp.sum(normalized_rows_gradient * centered_scaled_input, 0)
    centered_scaled_gradient = normalized_rows_gradient * layer_norm_gain
    gradient_row_total, gradient_dot_product = lax.psum(
        (
            jnp.sum(centered_scaled_gradient, 1),
            jnp.sum(centered_scaled_gradient * centered_scaled_input, 1),
        ),
        "row",
    )
    layer_norm_gain_gradient = lax.psum(partial_gain_gradient, "col")
    token_input_gradient = (
        cotangent.astype(jnp.float32)
        + (
            centered_scaled_gradient
            - gradient_row_total[:, None] / model_width_value
            - centered_scaled_input * gradient_dot_product[:, None] / model_width_value
        )
        * inverse_deviation[:, None]
    ).astype(jnp.bfloat16)
    return (
        layer_out,
        token_input_gradient,
        layer_norm_gain_gradient,
        d_w_qkv,
        d_qk_gain,
        d_w_up,
        d_w_attn_out,
        d_w_down,
    )


def solution(mesh):
    in_specs = (
        P("col", "row"),
        P("row"),
        P("row", None, "col"),
        P(None, "col"),
        P("row", "col"),
        P("col", "row"),
        P("col", "row"),
        P("col", "row"),
    )
    out_specs = (
        P("col", "row"),
        P("col", "row"),
        P("row"),
        P("row", None, "col"),
        P(None, "col"),
        P("row", "col"),
        P("col", "row"),
        P("col", "row"),
    )
    return jax.shard_map(shards, mesh=mesh, in_specs=in_specs, out_specs=out_specs, check_vma=False)
```

profile of v0, /device:TPU:1, one launch (start us, length us, event | category | flops | bytes accessed | tf_op | source)
XLA Modules:
  0.0 743.2 jit_solution(16288707024005902092)
XLA Ops:
  7.2 0.0 all-reduce.15.cloned.1.call-start
  7.2 0.9 convert_reduce_fusion
  8.1 1.2 copy.22
  9.3 0.2 copy.23
  9.5 39.6 %all-gather.6 = bf16[32,10,384]{2,1,0:T(8,128)(2,1)S(1)} all-gather(bf16[1,10,384]{2,1,0:T(8,128)(2,1)} %bitcast.104), channel_id=1, replica_groups=mesh['row'=16,'col'=32] {'col'}, dimensions={0}, use_global_device_ids=true | all-gather | bytes 253440 | tf_op jit(solution)/shard_map/all_gather | solution.py:86
  49.1 0.1 reshape.255
  49.3 0.1 constant_dynamic-update-slice_fusion
  49.4 0.0 copy-start.1
  49.4 0.0 copy-start.4
  49.4 0.5 convolution_bitcast_fusion
  49.9 71.8 %all-reduce.20 = (f32[10]{0:T(128)S(1)}, f32[10]{0:T(128)S(1)}, bf16[320,896]{1,0:T(8,128)(2,1)}) all-reduce(f32[10]{0:T(128)S(1)} %get-tuple-element.45, f32[10]{0:T(128)S(1)} %get-tuple-element.44, f32[320,896]{1,0:T(8,128)S(1)} %convolution_bitcast_fusion), channel_id=1, replica_groups=mesh['row'=16,'col'=32] {'row'}, use_global_device_ids=true, to_apply=%region_3.0 | all-reduce | flops 286740 | bytes 1720480 | tf_op jit(solution)/shard_map/psum | solution.py:29
  121.7 0.1 fusion.37
  121.8 35.8 %all-gather.2 = bf16[32,10,384]{2,1,0:T(8,128)(2,1)S(1)} all-gather(bf16[1,10,384]{2,1,0:T(8,128)(2,1)S(1)} %fusion.37), channel_id=1, replica_groups=mesh['row'=16,'col'=32] {'col'}, dimensions={0}, use_global_device_ids=true | all-gather | bytes 253440 | tf_op jit(solution)/shard_map/all_gather | solution.py:43
  157.6 0.1 reshape.247
  157.7 0.0 copy-start.5
  157.7 2.8 fusion.4
  160.5 0.0 all-reduce.15.cloned.1.call-update
  160.5 0.0 all-reduce.19.cloned.1.call-start
  160.5 1.3 dynamic-slice.2
  161.8 1.3 dynamic-slice
  164.4 0.8 dynamic-slice_convert_fusion
  165.3 123.8 %all-reduce.15.cloned.1.call-done = f32[320,1152]{1,0:T(8,128)} async-done(((f32[320,1152]{1,0:T(8,128)}), f32[320,1152]{1,0:T(8,128)}) %all-reduce.15.cloned.1.call-update) | async-done | bytes 1474576
  289.1 1.0 dynamic-slice_reduce_fusion
  290.1 1.0 multiply_reduce_fusion.2
  291.1 0.8 fusion.42
  291.9 16.5 %all-gather.4 = bf16[16,20,128]{2,1,0:T(8,128)(2,1)S(1)} all-gather(bf16[1,20,128]{2,1,0:T(8,128)(2,1)S(1)} %fusion.42), channel_id=3, replica_groups=mesh['row'=16,'col'=32] {'row'}, dimensions={0}, use_global_device_ids=true | all-gather | bytes 87040 | tf_op jit(solution)/shard_map/all_gather | solution.py:62
  308.4 0.8 fusion.45
  309.3 16.0 %all-gather.3 = bf16[16,20,128]{2,1,0:T(8,128)(2,1)S(1)} all-gather(bf16[1,20,128]{2,1,0:T(8,128)(2,1)S(1)} %fusion.45), channel_id=2, replica_groups=mesh['row'=16,'col'=32] {'row'}, dimensions={0}, use_global_device_ids=true | all-gather | bytes 87040 | tf_op jit(solution)/shard_map/all_gather | solution.py:63
  325.3 1.0 fusion.57
  326.3 0.2 fusion.16
  326.5 0.9 fusion.2
  327.4 0.3 multiply_reduce_fusion
  327.7 0.2 fusion.3
  327.9 1.0 fusion.7
  329.0 16.4 %all-gather.5 = bf16[16,20,896]{2,1,0:T(8,128)(2,1)S(1)} all-gather(bf16[1,20,896]{2,1,0:T(8,128)(2,1)S(1)} %maximum_bitcast_fusion.1), channel_id=1, replica_groups=mesh['row'=16,'col'=32] {'row'}, dimensions={0}, use_global_device_ids=true | all-gather | bytes 609280 | tf_op jit(solution)/shard_map/all_gather | solution.py:77
  345.4 0.1 reshape.253
  345.6 1.2 convolution_convert_fusion.3
  346.8 0.1 multiply_convert_fusion.1
  346.8 1.6 fusion.1
  348.5 0.0 all-reduce.19.cloned.1.call-update
  348.5 0.0 all-reduce.17.cloned.1.call-start
  348.5 1.0 fusion.39
  349.5 105.5 %all-reduce.19.cloned.1.call-done = (bf16[320,1,128]{2,0,1:T(8,128)(2,1)}, bf16[320,1,128]{2,0,1:T(8,128)(2,1)}) async-done(((bf16[320,1,128]{2,0,1:T(8,128)(2,1)}, bf16[320,1,128]{2,0,1:T(8,128)(2,1)}), (bf16[320,1,128]{2,0,1:T(8,128)(2,1)}, bf16[320,1,128]{2,0,1:T(8,128)(2,1)})) %all-reduce.19.cloned.1.call-update) | async-done | bytes 163856
  455.0 0.7 dynamic-slice_bitcast_fusion
  455.7 1.0 fusion.38
  456.7 1.0 fusion.36
  457.7 0.9 fusion.44
  458.6 18.0 %all-gather.7 = bf16[16,20,1152]{2,1,0:T(8,128)(2,1)S(1)} all-gather(bf16[1,20,1152]{2,1,0:T(8,128)(2,1)S(1)} %maximum_bitcast_fusion), channel_id=1, replica_groups=mesh['row'=16,'col'=32] {'row'}, dimensions={0}, use_global_device_ids=true | all-gather | bytes 783360 | tf_op jit(solution)/shard_map/all_gather | solution.py:135
  476.5 0.1 reshape.257
  476.7 2.3 convolution_convert_fusion.2
  479.0 0.0 all-reduce.17.cloned.1.call-update
  479.1 0.6 convolution_convert_fusion.1
  479.7 0.7 slice.59
  480.3 0.9 slice.60
  481.2 0.7 convolution_convert_fusion
  481.9 0.9 slice.58
  482.8 0.2 copy.24
  483.0 0.9 copy.25
  483.9 147.8 %all-reduce.17.cloned.1.call-done = (bf16[320,384]{1,0:T(8,128)(2,1)}, bf16[320,384]{1,0:T(8,128)(2,1)}) async-done(((bf16[320,384]{1,0:T(8,128)(2,1)}, bf16[320,384]{1,0:T(8,128)(2,1)}), (bf16[320,384]{1,0:T(8,128)(2,1)}, bf16[320,384]{1,0:T(8,128)(2,1)})) %all-reduce.17.cloned.1.call-update) | async-done | bytes 491536
  631.6 0.9 fusion.25
  632.6 59.9 %psum.53 = f32[384]{0:T(512)} all-reduce(f32[384]{0:T(512)S(1)} %get-tuple-element.41), channel_id=1, replica_groups=mesh['row'=16,'col'=32] {'col'}, use_global_device_ids=true, to_apply=%region_26.0 | all-reduce | flops 384 | bytes 3072 | tf_op jit(solution)/shard_map/psum | solution.py:158
  692.4 42.3 %all-reduce.6 = (f32[10]{0:T(128)S(1)}, f32[10]{0:T(128)S(1)}, f32[1,128]{1,0:T(1,128)S(1)}, f32[1,128]{1,0:T(1,128)S(1)}) all-reduce(f32[10]{0:T(128)S(1)} %get-tuple-element.42, f32[10]{0:T(128)S(1)} %get-tuple-element.43, f32[1,128]{1,0:T(1,128)S(1)} %bitcast.106, ...), channel_id=1, replica_groups=mesh['row'=16,'col'=32] {'row'}, use_global_device_ids=true, to_apply=%region_24.0 | all-reduce | flops 276 | bytes 2208 | tf_op jit(solution)/shard_map/psum | solution.py:151
  734.7 0.6 pad_maximum_fusion.3
  735.3 1.4 fusion.23
  (26 shorter events, 0.2 us)
Async XLA Ops:
  7.2 42.1 %copy-start.2 = (bf16[128,384]{1,0:T(8,128)(2,1)S(1)}, bf16[128,384]{1,0:T(8,128)(2,1)}, u32[]{:S(2)}) copy-start(bf16[128,384]{1,0:T(8,128)(2,1)} %param.13) | copy-start | bytes 294916
  7.2 42.1 %copy-start = (bf16[768,384]{1,0:T(8,128)(2,1)S(1)}, bf16[768,384]{1,0:T(8,128)(2,1)}, u32[]{:S(2)}) copy-start(bf16[768,384]{1,0:T(8,128)(2,1)} %param.14) | copy-start | bytes 1769476
  7.2 281.9 %all-reduce.15.cloned.1.call-start = ((), (), s32[]{:S(2)}) async-start(), calls=%async_computation | async-start | bytes 2949120
  49.4 72.4 %copy-start.1 = (bf16[10,384]{1,0:T(8,128)(2,1)S(1)}, bf16[10,384]{1,0:T(8,128)(2,1)}, u32[]{:S(2)}) copy-start(bf16[10,384]{1,0:T(8,128)(2,1)} %param.8) | copy-start | bytes 23044
  49.4 72.4 %copy-start.4 = (f32[384]{0:T(512)S(1)}, f32[384]{0:T(512)}, u32[]{:S(2)}) copy-start(f32[384]{0:T(512)} %param.9) | copy-start | bytes 4612
  157.7 7.5 %copy-start.5 = (f32[2,128]{1,0:T(2,128)S(1)}, f32[2,128]{1,0:T(2,128)}, u32[]{:S(2)}) copy-start(f32[2,128]{1,0:T(2,128)} %param.11) | copy-start | bytes 3076
  160.5 294.5 %all-reduce.19.cloned.1.call-start = ((), (), s32[]{:S(2)}) async-start(), calls=%async_computation.2 | async-start | bytes 327680
  348.5 283.2 %all-reduce.17.cloned.1.call-start = ((), (), s32[]{:S(2)}) async-start(), calls=%async_computation.1 | async-start | bytes 983040
  481.9 253.4 %copy-start.3 = (bf16[10,384]{1,0:T(8,128)(2,1)S(1)}, bf16[10,384]{1,0:T(8,128)(2,1)}, u32[]{:S(2)}) copy-start(bf16[10,384]{1,0:T(8,128)(2,1)} %param.15) | copy-start | bytes 23044
Sparse Core Ops, SparseCore 0:
  160.6 128.4 all-reduce.14
  348.6 106.3 all-reduce.18
  479.2 152.4 all-reduce.16
where the time goes:
time: 745 us; the launch traced here: 743 us
  waiting for transfers between devices  377 us (51%)
  blocking collectives  316 us (42%)
  between operations  15.3 us (2%)
  matrix products  13.1 us (2%)
  other arithmetic  10.9 us (1%)
  local copies, waits for them, and re-layouts  10.5 us (1%)
    unnamed x6, waiting for transfers between devices  377 us
    psum x1, blocking collectives, shards(): lax.psum((jnp.sum(input_single_precision, 1), jnp.sum(input_single_precis...  71.8 us
    psum x1, blocking collectives, shards(): layer_norm_gain_gradient = lax.psum(partial_gain_gradient, 'col')  59.9 us
    psum x1, blocking collectives, shards(): lax.psum((jnp.sum(centered_scaled_gradient, 1), jnp.sum(centered_scaled_g...  42.3 us
    all_gather x1, blocking collectives, shards(): cot_all = lax.all_gather(cotangent, 'col', axis=0, tiled=True)  39.6 us
    all_gather x1, blocking collectives, shards(): normed_all = lax.all_gather(normalized_tokens, 'col', axis=0, tiled=True)  35.8 us
    all_gather x1, blocking collectives, shards(): d_merged_all = lax.all_gather(d_merged, 'row', axis=0, tiled=True)  18 us
    all_gather x1, blocking collectives, shards(): lax.all_gather(k_normed.astype(jnp.bfloat16), 'row', axis=0, tiled=True)  16.5 us
  transfers between devices with their start and end apart: 3, of which 3 were waited for; matrix products, arithmetic and copies ran while one was open for 1% of the time, Pallas kernels for 0%

commit v1 on v0

v1 whole, which is shorter than its diff:
```python
import jax
import jax.numpy as jnp
from jax import lax
from jax.sharding import Mesh
from jax.sharding import PartitionSpec as P

HEAD_DIM = 128
EPS = 1e-06
ROW = ("z", "core")
COL = ("x", "y")
F32 = jnp.float32
BF16 = jnp.bfloat16


def split(values, parts):
    out = []
    for _ in range(parts):
        high = lax.reduce_precision(values, 8, 7)
        out.append(high.astype(BF16))
        values = values - high
    return out


def dot(a, b, dims):
    return lax.dot_general(a, b, (dims, ((), ())), preferred_element_type=F32)


NN = ((1,), (0,))
NT = ((1,), (1,))
TN = ((0,), (0,))


def lane_pad(values, width):
    return jnp.pad(values, [(0, 0)] * (values.ndim - 1) + [(0, width - values.shape[-1])])


def shards(tokens_in, gain, w_qkv, qk_gain, w_up, w_attn_out, w_down, cotangent):
    rows_c, width = tokens_in.shape
    n_col = lax.axis_size(COL)
    n_z = lax.axis_size("z")
    tokens = rows_c * n_col
    rows_z = tokens // n_z
    model_width = width * lax.axis_size(ROW)
    core = lax.axis_index("core")
    first = core == 0
    swap = [(0, 1), (1, 0)]
    scale = HEAD_DIM ** (-0.5)
    w_qkv2 = w_qkv.reshape(width, 3 * HEAD_DIM)

    mine = jnp.concatenate([tokens_in, cotangent], 0)
    got = lax.all_to_all(jnp.broadcast_to(mine, (n_col,) + mine.shape), COL, 0, 0)
    x_all = got[:, :rows_c].reshape(tokens, width)
    cot_all = got[:, rows_c:].reshape(tokens, width)

    x_f = x_all.astype(F32)
    sum_1 = jnp.sum(x_f, 1)
    sum_2 = jnp.sum(x_f * x_f, 1)
    gain_parts = jnp.stack(split(gain, 3) + [jnp.zeros((width,), BF16)] * 5)
    xg = jnp.concatenate([(x_f * gain).astype(BF16), gain_parts], 0)
    p_qkv = dot(xg, w_qkv2, NN)
    p_up = dot(xg, w_up, NN)
    p_da = dot(cot_all, w_attn_out, NT)
    p_dh = dot(cot_all, w_down, NT)
    c_qkv = jnp.sum(p_qkv[tokens:], 0)
    c_up = jnp.sum(p_up[tokens:], 0)
    p_qkv, p_up = p_qkv[:tokens], p_up[:tokens]
    q4 = 2 * HEAD_DIM
    zero = jnp.zeros((q4,), F32)
    lay_0 = jnp.concatenate([p_qkv, p_da, p_up[:, :q4], p_dh[:, :q4]], 1)
    lay_1 = jnp.concatenate(
        [p_up[:, q4 : 2 * q4], p_dh[:, q4 : 2 * q4], p_up[:, 2 * q4 :], p_dh[:, 2 * q4 :]], 1
    )
    c_0 = jnp.concatenate([c_qkv, zero[:HEAD_DIM], c_up[:q4], zero])
    c_1 = jnp.concatenate([c_up[q4 : 2 * q4], zero, c_up[2 * q4 :], zero])
    wide = lay_0.shape[1]

    def extras(c_vec, s_1, s_2, c_h):
        rows = split(c_vec, 2)
        for s, c in zip(split(s_1, 3), split(c_h, 3)):
            rows.append(
                jnp.concatenate(
                    [lane_pad(s, 512), lane_pad(c, wide - 512)]
                )
            )
        rows += [lane_pad(s, wide) for s in split(s_2, 3)]
        return jnp.stack(rows)

    def unpack(block):
        block = block.astype(F32)
        h = jnp.sum(block[2:5], 0)
        return (
            jnp.sum(block[0:2], 0),
            h[:tokens],
            jnp.sum(block[5:8], 0)[:tokens],
            h[512 : 512 + 3 * HEAD_DIM],
        )

    own = jnp.where(first, lay_0, lay_1)
    other = jnp.where(first, lay_1, lay_0).astype(BF16)
    c_own = jnp.where(first, c_0, c_1)
    c_other = jnp.where(first, c_1, c_0)

    sent = jnp.concatenate([other, extras(c_other, sum_1, sum_2, c_qkv)], 0)
    came = lax.ppermute(sent, "core", swap)
    half = (own + came[:tokens].astype(F32)).astype(BF16)
    o_c, o_1, o_2, o_h = unpack(came[tokens:])
    extra = extras(c_own + o_c, sum_1 + o_1, sum_2 + o_2, c_qkv + o_h)
    sent = jnp.concatenate(
        [half.reshape(n_z, rows_z, wide), jnp.broadcast_to(extra, (n_z,) + extra.shape)], 1
    )
    total = jnp.sum(lax.all_to_all(sent, "z", 0, 0).astype(F32), 0)
    c_tot, s_1, s_2, c_h = unpack(total[rows_z:])
    total = total[:rows_z]

    mean = s_1 / model_width
    inv = lax.rsqrt(s_2 / model_width - mean * mean + EPS)
    at = lax.axis_index("z") * rows_z
    mean_z = lax.dynamic_slice(mean, (at,), (rows_z,))[:, None]
    inv_z = lax.dynamic_slice(inv, (at,), (rows_z,))[:, None]
    merged = (total - mean_z * c_tot) * inv_z

    def mlp(up, d_hidden, c_vec):
        hidden, back = jax.vjp(jax.nn.gelu, up)
        d_up = back(d_hidden.astype(BF16).astype(F32))[0].astype(BF16)
        d_f = d_up.astype(F32)
        return hidden.astype(BF16), d_up, jnp.sum(d_f * c_vec, 1), jnp.sum(d_f * up, 1)

    def norm(values, g):
        average = jnp.mean(values, -1, keepdims=True)
        centred = values - average
        rstd = lax.rsqrt(jnp.mean(centred * centred, -1, keepdims=True) + EPS)
        return (centred * rstd * g).astype(BF16), rstd[:, 0], average[:, 0]

    h_a, u_a, s1_a, s2_a = mlp(merged[:, :q4], total[:, q4 : 2 * q4], c_tot[:q4])
    h_b, u_b, s1_b, s2_b = mlp(merged[:, 2 * q4 : 3 * q4], total[:, 3 * q4 :], c_tot[2 * q4 : 3 * q4])
    q_z, rstd_q, mean_q = norm(merged[:, :HEAD_DIM], qk_gain[0])
    k_z, rstd_k, mean_k = norm(merged[:, HEAD_DIM : 2 * HEAD_DIM], qk_gain[1])
    v_z = merged[:, 2 * HEAD_DIM : 3 * HEAD_DIM].astype(BF16)
    da_z = total[:, 3 * HEAD_DIM : 4 * HEAD_DIM].astype(BF16)
    left = jnp.where(
        first, jnp.concatenate([q_z, k_z, v_z, da_z], 1), jnp.concatenate([h_a, u_a], 1)
    )
    e_cols = jnp.stack(
        [rstd_q, rstd_k, mean_q, mean_k, jnp.where(first, 0, s1_a) + s1_b, jnp.where(first, 0, s2_a) + s2_b],
        1,
    )
    e_cols = lane_pad(jnp.concatenate(split(e_cols, 2), 1), HEAD_DIM)
    sent = jnp.concatenate([left, h_b, u_b, e_cols], 1)

    mine = lax.all_to_all(jnp.broadcast_to(sent, (n_z,) + sent.shape), "z", 0, 0)
    mine = mine.reshape(tokens, sent.shape[1])
    theirs = lax.ppermute(mine, "core", swap)
    a0 = jnp.where(first, mine, theirs)
    a1 = jnp.where(first, theirs, mine)
    q_rows, k_rows, v_rows, d_att = (
        a0[:, i * HEAD_DIM : (i + 1) * HEAD_DIM] for i in range(4)
    )
    hidden = jnp.concatenate([a0[:, 2 * q4 : 3 * q4], a1[:, :q4], a1[:, 2 * q4 : 3 * q4]], 1)
    d_up = jnp.concatenate([a0[:, 3 * q4 : 4 * q4], a1[:, q4 : 2 * q4], a1[:, 3 * q4 : 4 * q4]], 1)
    e0 = a0[:, wide:].astype(F32)
    e1 = a1[:, wide:].astype(F32)
    e0 = e0[:, :6] + e0[:, 6:12]
    e1 = e1[:, :6] + e1[:, 6:12]
    rstd_q, rstd_k, mean_q, mean_k = (e0[:, i : i + 1] for i in range(4))

    probs = jax.nn.softmax(dot(q_rows, k_rows, NT) * scale, -1)
    prob_low = probs.astype(BF16)
    attended = dot(prob_low, v_rows, NN).astype(BF16)
    branch = dot(attended, w_attn_out, NN) + dot(hidden, w_down, NN)
    d_probs = dot(d_att, v_rows, NT)
    row_delta = jnp.sum(probs * d_probs, -1, keepdims=True)
    d_scores = (probs * (d_probs - row_delta)).astype(BF16)
    d_qn = dot(d_scores, k_rows, NN) * scale
    d_kn = dot(d_scores, q_rows, TN) * scale
    d_value = dot(prob_low, d_att, TN)

    def norm_back(rows, rstd, average, g, d_rows):
        unit = rows.astype(F32) / g
        d_unit = d_rows * g
        d_values = (
            d_unit
            - jnp.mean(d_unit, -1, keepdims=True)
            - unit * jnp.mean(d_unit * unit, -1, keepdims=True)
        ) * rstd
        return d_values.astype(BF16), jnp.sum(d_rows * unit, 0), unit / rstd + average

    d_q, d_q_gain, query = norm_back(q_rows, rstd_q, mean_q, qk_gain[0], d_qn)
    d_k, d_k_gain, key = norm_back(k_rows, rstd_k, mean_k, qk_gain[1], d_kn)
    d_qk_gain = jnp.stack([d_q_gain, d_k_gain])
    d_qkv = jnp.concatenate([d_q, d_k, d_value.astype(BF16)], 1)
    d_f = d_qkv.astype(F32)
    t_1 = jnp.sum(d_f * c_h, 1) + e0[:, 4] + e1[:, 4]
    t_2 = (
        jnp.sum(d_f * jnp.concatenate([query, key, v_rows.astype(F32)], 1), 1) + e0[:, 5] + e1[:, 5]
    )
    d_normed = dot(d_qkv, w_qkv2, NT) + dot(d_up, w_up, NT)
    xhat = (x_f - mean[:, None]) * inv[:, None]
    normed = (xhat * gain).astype(BF16)
    part_gain = jnp.sum(d_normed * xhat, 0)
    d_w_qkv = dot(normed, d_qkv, TN).astype(BF16).reshape(w_qkv.shape)
    d_w_up = dot(normed, d_up, TN).astype(BF16)
    d_w_attn_out = dot(attended, cot_all, TN).astype(BF16)
    d_w_down = dot(hidden, cot_all, TN).astype(BF16)

    send = jnp.concatenate([branch.astype(BF16), d_normed.astype(BF16)], 1)
    send = send.reshape(n_col, rows_c, 2 * width)
    rows = [
        jnp.concatenate([g, lane_pad(s, width)])
        for g, s in zip(split(part_gain, 3), split(t_1, 3))
    ] + [jnp.concatenate([jnp.zeros((width,), BF16), lane_pad(s, width)]) for s in split(t_2, 3)]
    rows = jnp.stack(rows)
    send = jnp.concatenate([send, jnp.broadcast_to(rows, (n_col,) + rows.shape)], 1)
    total = jnp.sum(lax.all_to_all(send, COL, 0, 0).astype(F32), 0)
    layer_out = (tokens_in.astype(F32) + total[:rows_c, :width]).astype(BF16)
    d_gain = jnp.sum(total[rows_c : rows_c + 3, :width], 0)
    t_1 = jnp.sum(total[rows_c : rows_c + 3, width:], 0)
    t_2 = jnp.sum(total[rows_c + 3 : rows_c + 6, width:], 0)
    at = lax.axis_index(COL) * rows_c
    t_1, t_2, mean_c, inv_c = (
        lax.dynamic_slice(v, (at,), (rows_c,))[:, None] for v in (t_1, t_2, mean, inv)
    )
    xhat_c = (tokens_in.astype(F32) - mean_c) * inv_c
    d_xhat = total[:rows_c, width:] * gain
    token_grad = (
        cotangent.astype(F32) + (d_xhat - t_1 / model_width - xhat_c * t_2 / model_width) * inv_c
    ).astype(BF16)
    return (
        layer_out,
        token_grad,
        d_gain,
        d_w_qkv,
        d_qk_gain,
        d_w_up,
        d_w_attn_out,
        d_w_down,
    )


def solution(mesh):
    fine = Mesh(mesh.devices.reshape(-1, 2, 4, 8), ("z", "core", "x", "y"))
    in_specs = (
        P(COL, ROW),
        P(ROW),
        P(ROW, None, COL),
        P(None, COL),
        P(ROW, COL),
        P(COL, ROW),
        P(COL, ROW),
        P(COL, ROW),
    )
    out_specs = (
        P(COL, ROW),
        P(COL, ROW),
        P(ROW),
        P(ROW, None, COL),
        P(None, COL),
        P(ROW, COL),
        P(COL, ROW),
        P(COL, ROW),
    )
    return jax.shard_map(shards, mesh=fine, in_specs=in_specs, out_specs=out_specs, check_vma=False)
```

time: 745 us -> 168 us (0.23)
  the two profiles are of different devices: /device:TPU:1 before, /device:TPU:8 now
where the time goes in v1:
time: 168 us; the launch traced here: 167 us
  waiting for transfers between devices  63.4 us (38%)
  starting transfers between devices  29.4 us (18%)
  blocking collectives  24.9 us (15%)
  local copies, waits for them, and re-layouts  21.8 us (13%)
  other arithmetic  16.7 us (10%)
  matrix products  8.76 us (5%)
    all_to_all x1, blocking collectives, shards(): lax.all_to_all(jnp.broadcast_to(sent, (n_z,) + sent.shape), 'z', 0, 0)  24.9 us
    all_to_all x1, waiting for transfers between devices, shards(): total = jnp.sum(lax.all_to_all(sent, 'z', 0, 0).astype(F32), 0)  23.4 us
    all_to_all x1, waiting for transfers between devices, shards(): lax.all_to_all(jnp.broadcast_to(mine, (n_col,) + mine.shape), COL, 0, 0)  18 us
    all_to_all x1, waiting for transfers between devices, shards(): total = jnp.sum(lax.all_to_all(send, COL, 0, 0).astype(F32), 0)  17.4 us
    all_to_all x1, starting transfers between devices, shards(): total = jnp.sum(lax.all_to_all(sent, 'z', 0, 0).astype(F32), 0)  10.5 us
    all_to_all x1, starting transfers between devices, shards(): lax.all_to_all(jnp.broadcast_to(mine, (n_col,) + mine.shape), COL, 0, 0)  10.2 us
    dot_general x18, matrix products, dot(): return lax.dot_general(a, b, (dims, ((), ())), preferred_element_type=F32)  8.76 us
    another operation x13, local copies, waits for them, and re-layouts, extras(): return jnp.stack(rows)  8.56 us
  transfers between devices with their start and end apart: 5, of which 5 were waited for; matrix products, arithmetic and copies ran while one was open for 4% of the time, Pallas kernels for 0%

profile of v1, /device:TPU:8, one launch (start us, length us, event | category | flops | bytes accessed | tf_op | source)
XLA Modules:
  0.0 166.6 jit_solution(8748207464168844074)
XLA Ops:
  0.7 0.8 pad_maximum_fusion.12
  1.5 0.9 broadcast_in_dim.15
  2.3 10.2 %all-to-all-start = ((bf16[32,20,384]{2,1,0:T(8,128)(2,1)}), bf16[32,20,384]{2,1,0:T(8,128)(2,1)S(1)}, u32[]{:S(2)}, u32[]{:S(2)}) async-start(bf16[32,20,384]{2,1,0:T(8,128)(2,1)} %broadcast_in_dim.15), calls=%async_computation | async-start | bytes 1179648 | tf_op jit(solution)/shard_map/all_to_all | solution.py:51
  12.8 0.7 pad.159.clone
  13.5 18.0 %all-to-all-done = bf16[32,20,384]{2,1,0:T(8,128)(2,1)S(1)} async-done(((bf16[32,20,384]{2,1,0:T(8,128)(2,1)}), bf16[32,20,384]{2,1,0:T(8,128)(2,1)S(1)}, u32[]{:S(2)}, u32[]{:S(2)}) %all-to-all-start) | async-done | bytes 491552 | tf_op jit(solution)/shard_map/all_to_all | solution.py:51
  31.5 0.9 slice_convert_fusion
  32.7 0.4 fusion.134
  33.3 0.6 concatenate.153
  33.9 0.4 fusion.136
  35.0 0.6 stack.95
  35.6 0.6 stack.94
  36.2 0.6 stack.93
  36.9 0.6 stack.90
  37.5 0.6 stack.91
  38.1 0.6 stack.92
  38.9 0.4 fusion.137
  39.5 0.6 copy-done.25
  40.1 0.6 fusion.58
  40.7 0.6 copy-done.19
  41.3 0.6 reduce-precision_convert_fusion.2
  41.9 1.0 select_convert_fusion
  42.8 5.0 %concatenate.159 = bf16[328,1024]{1,0:T(8,128)(2,1)} concatenate(bf16[320,1024]{1,0:T(8,128)(2,1)} %select_convert_fusion, bf16[1,1024]{1,0:T(2,128)(2,1)} %reduce-precision_convert_fusion.2, bf16[1,1024]{1,0:T(2,128)(2,1)} %get-tuple-element.67, bf16[1,1024]{1,0:T(2,128)(2,1)} %stack.90, bf16[1,1024]{1,0:T(2,128)(2,1)} %stack.91, bf16[1,1024]{1,0:T(2,128)(2,1)} %stack.92, ...), dimensions={0} | concatenate | bytes 1343488 | tf_op jit(solution)/shard_map/concatenate | solution.py:103
  47.8 1.9 %collective-permute-start = (bf16[328,1024]{1,0:T(8,128)(2,1)}, bf16[328,1024]{1,0:T(8,128)(2,1)}, u32[]{:S(2)}, u32[]{:S(2)}) collective-permute-start(bf16[328,1024]{1,0:T(8,128)(2,1)} %concatenate.159), channel_id=1, source_target_pairs={{0,32},{32,0},{1,33},{33,1},{2,34},{34,2},{3,35},{35,3},{4,36},{36... | collective-permute-start | bytes 2015240 | tf_op jit(solution)/shard_map/ppermute | solution.py:104
  49.7 2.4 %collective-permute-done = bf16[328,1024]{1,0:T(8,128)(2,1)} collective-permute-done((bf16[328,1024]{1,0:T(8,128)(2,1)}, bf16[328,1024]{1,0:T(8,128)(2,1)}, u32[]{:S(2)}, u32[]{:S(2)}) %collective-permute-start) | collective-permute-done | bytes 671776 | tf_op jit(solution)/shard_map/ppermute | solution.py:104
  52.2 0.7 slice_convert_fusion.5
  52.9 0.7 fusion.88
  53.6 0.7 fusion.90
  54.3 0.7 fusion.92
  55.0 1.3 fusion.60
  56.3 0.6 stack.96
  56.9 0.6 stack.97
  57.5 0.6 stack.98
  58.1 0.6 stack.101
  58.7 0.6 stack.100
  59.3 0.6 stack.99
  59.9 0.6 reduce-precision_convert_fusion.1
  60.5 1.4 stack.102
  61.9 1.3 add_convert_fusion
  63.3 0.9 pad_maximum_fusion.2
  64.2 10.5 %all-to-all-start.1 = ((bf16[8,48,1024]{2,1,0:T(8,128)(2,1)}), bf16[8,48,1024]{2,1,0:T(8,128)(2,1)S(1)}, u32[]{:S(2)}, u32[]{:S(2)}) async-start(bf16[8,48,1024]{2,1,0:T(8,128)(2,1)} %pad_maximum_fusion.2), calls=%async_computation.1 | async-start | bytes 1572864 | tf_op jit(solution)/shard_map/all_to_all | solution.py:111
  74.7 23.4 %all-to-all-done.1 = bf16[8,48,1024]{2,1,0:T(8,128)(2,1)S(1)} async-done(((bf16[8,48,1024]{2,1,0:T(8,128)(2,1)}), bf16[8,48,1024]{2,1,0:T(8,128)(2,1)S(1)}, u32[]{:S(2)}, u32[]{:S(2)}) %all-to-all-start.1) | async-done | bytes 786464 | tf_op jit(solution)/shard_map/all_to_all | solution.py:111
  99.5 24.9 %all_to_all.20 = bf16[8,40,1152]{2,1,0:T(8,128)(2,1)S(1)} all-to-all(bf16[8,40,1152]{2,1,0:T(8,128)(2,1)S(1)} %broadcast_in_dim.19), channel_id=1, replica_groups=mesh['z'=8,'core'=2,'x'=4,'y'=8] {'z'}, dimensions={0} | all-to-all | bytes 1474560 | tf_op jit(solution)/shard_map/all_to_all | solution.py:150
  124.4 1.9 %collective-permute-start.1 = (bf16[320,1152]{1,0:T(8,128)(2,1)S(1)}, bf16[320,1152]{1,0:T(8,128)(2,1)S(1)}, u32[]{:S(2)}, u32[]{:S(2)}) collective-permute-start(bf16[320,1152]{1,0:T(8,128)(2,1)S(1)} %bitcast.51), channel_id=1, source_target_pairs={{0,32},{32,0},{1,33},{33,1},{2,34},{34,2},{3,35},{35,3},{4,36},{36... | collective-permute-start | bytes 2211848 | tf_op jit(solution)/shard_map/ppermute | solution.py:152
  126.4 2.2 %collective-permute-done.1 = bf16[320,1152]{1,0:T(8,128)(2,1)S(1)} collective-permute-done((bf16[320,1152]{1,0:T(8,128)(2,1)S(1)}, bf16[320,1152]{1,0:T(8,128)(2,1)S(1)}, u32[]{:S(2)}, u32[]{:S(2)}) %collective-permute-start.1) | collective-permute-done | bytes 737312 | tf_op jit(solution)/shard_map/ppermute | solution.py:152
  129.5 0.3 convolution_convert_fusion.5
  130.6 0.6 slice_reduce_fusion.1
  131.8 0.4 multiply_reduce_fusion.4
  132.3 0.4 multiply_convert_fusion.4
  132.7 0.5 copy-done.2
  133.2 0.3 fusion.120
  133.9 0.5 fusion.130
  134.5 0.5 copy-done.7
  135.0 0.4 fusion
  135.7 1.1 pad_maximum_fusion.3
  136.8 5.0 %all-to-all-start.3 = ((bf16[32,16,768]{2,1,0:T(8,128)(2,1)}), bf16[32,16,768]{2,1,0:T(8,128)(2,1)S(1)}, u32[]{:S(2)}, u32[]{:S(2)}) async-start(bf16[32,16,768]{2,1,0:T(8,128)(2,1)} %pad_maximum_fusion.3), calls=%async_computation.3 | async-start | bytes 1572864 | tf_op jit(solution)/shard_map/all_to_all | solution.py:213
  142.0 0.5 convolution_convert_fusion.2
  142.5 0.9 copy.20
  143.4 0.6 pad_maximum_fusion.16
  143.9 0.9 convolution_convert_fusion.3
  144.8 1.4 convolution_convert_fusion
  146.2 1.4 convolution_convert_fusion.1
  147.7 17.4 %all-to-all-done.3 = bf16[32,16,768]{2,1,0:T(8,128)(2,1)S(1)} async-done(((bf16[32,16,768]{2,1,0:T(8,128)(2,1)}), bf16[32,16,768]{2,1,0:T(8,128)(2,1)S(1)}, u32[]{:S(2)}, u32[]{:S(2)}) %all-to-all-start.3) | async-done | bytes 786464 | tf_op jit(solution)/shard_map/all_to_all | solution.py:213
  165.2 0.6 slice_reduce_fusion.18
  165.9 0.7 fusion.55
  (176 shorter events, 6.5 us)
Async XLA Ops:
  0.6 33.3 %copy-start = (bf16[384,768]{1,0:T(8,128)(2,1)S(1)}, bf16[384,768]{1,0:T(8,128)(2,1)}, u32[]{:S(2)}) copy-start(bf16[384,768]{1,0:T(8,128)(2,1)} %param.12) | copy-start | bytes 1769476
  0.6 11.9 %copy-start.21 = (f32[384]{0:T(512)S(1)}, f32[384]{0:T(512)}, u32[]{:S(2)}) copy-start(f32[384]{0:T(512)} %param.9) | copy-start | bytes 4612
  0.7 11.9 %copy-start.9 = (bf16[384,3,128]{2,0,1:T(8,128)(2,1)S(1)}, bf16[384,3,128]{2,0,1:T(8,128)(2,1)}, u32[]{:S(2)}) copy-start(bf16[384,3,128]{2,0,1:T(8,128)(2,1)} %param.10) | copy-start | bytes 884740
  2.3 29.2 %all-to-all-start = ((bf16[32,20,384]{2,1,0:T(8,128)(2,1)}), bf16[32,20,384]{2,1,0:T(8,128)(2,1)S(1)}, u32[]{:S(2)}, u32[]{:S(2)}) async-start(bf16[32,20,384]{2,1,0:T(8,128)(2,1)} %broadcast_in_dim.15), calls=%async_computation | async-start | bytes 1179648 | tf_op jit(solution)/shard_map/all_to_all | solution.py:51
  12.8 19.9 %copy-start.1 = (bf16[384,3,128]{0,2,1:T(8,128)(2,1)}, bf16[384,3,128]{0,2,1:T(8,128)(2,1)S(1)}, u32[]{:S(2)}) copy-start(bf16[384,3,128]{0,2,1:T(8,128)(2,1)S(1)} %copy.18) | copy-start | bytes 884740
  32.5 0.8 copy-start.3
  33.3 1.0 copy-start.20
  34.3 2.4 %copy-start.5 = (bf16[32,10,384]{2,1,0:T(8,128)(2,1)S(1)}, bf16[32,10,384]{2,1,0:T(8,128)(2,1)}, u32[]{:S(2)}) copy-start(bf16[32,10,384]{2,1,0:T(8,128)(2,1)} %get-tuple-element.93) | copy-start | bytes 737284
  34.4 4.2 %copy-start.8 = (bf16[128,384]{1,0:T(8,128)(2,1)S(1)}, bf16[128,384]{1,0:T(8,128)(2,1)}, u32[]{:S(2)}) copy-start(bf16[128,384]{1,0:T(8,128)(2,1)} %param.13) | copy-start | bytes 294916
  34.7 4.3 %copy-start.6 = (bf16[768,384]{1,0:T(8,128)(2,1)S(1)}, bf16[768,384]{1,0:T(8,128)(2,1)}, u32[]{:S(2)}) copy-start(bf16[768,384]{1,0:T(8,128)(2,1)} %param.14) | copy-start | bytes 1769476
  34.8 3.9 %copy-start.23 = (f32[320]{0:T(512)}, f32[320]{0:T(512)S(1)}, u32[]{:S(2)}) copy-start(f32[320]{0:T(512)S(1)} %reduce_sum.317) | copy-start | bytes 3844
  34.9 3.8 %copy-start.24 = (f32[320]{0:T(512)}, f32[320]{0:T(512)S(1)}, u32[]{:S(2)}) copy-start(f32[320]{0:T(512)S(1)} %reduce_sum.315) | copy-start | bytes 3844
  39.4 0.7 copy-start.25
  39.4 0.7 copy-start.26
  40.7 0.6 copy-start.19
  47.8 4.3 %collective-permute-start = (bf16[328,1024]{1,0:T(8,128)(2,1)}, bf16[328,1024]{1,0:T(8,128)(2,1)}, u32[]{:S(2)}, u32[]{:S(2)}) collective-permute-start(bf16[328,1024]{1,0:T(8,128)(2,1)} %concatenate.159), channel_id=1, source_target_pairs={{0,32},{32,0},{1,33},{33,1},{2,34},{34,2},{3,35},{35,3},{4,36},{36... | collective-permute-start | bytes 2015240 | tf_op jit(solution)/shard_map/ppermute | solution.py:104
  61.9 1.3 copy-start.16
  64.2 10.5 %copy-start.27 = (f32[2,128]{1,0:T(2,128)S(1)}, f32[2,128]{1,0:T(2,128)}, u32[]{:S(2)}) copy-start(f32[2,128]{1,0:T(2,128)} %param.11) | copy-start | bytes 3076
  64.2 33.9 %all-to-all-start.1 = ((bf16[8,48,1024]{2,1,0:T(8,128)(2,1)}), bf16[8,48,1024]{2,1,0:T(8,128)(2,1)S(1)}, u32[]{:S(2)}, u32[]{:S(2)}) async-start(bf16[8,48,1024]{2,1,0:T(8,128)(2,1)} %pad_maximum_fusion.2), calls=%async_computation.1 | async-start | bytes 1572864 | tf_op jit(solution)/shard_map/all_to_all | solution.py:111
  98.3 35.5 %copy-start.28 = (f32[320]{0:T(512)}, f32[320]{0:T(512)S(1)}, u32[]{:S(2)}) copy-start(f32[320]{0:T(512)S(1)} %get-tuple-element.115) | copy-start | bytes 3844
  98.3 35.5 %copy-start.30 = (f32[320]{0:T(512)}, f32[320]{0:T(512)S(1)}, u32[]{:S(2)}) copy-start(f32[320]{0:T(512)S(1)} %get-tuple-element.116) | copy-start | bytes 3844
  124.4 4.1 %collective-permute-start.1 = (bf16[320,1152]{1,0:T(8,128)(2,1)S(1)}, bf16[320,1152]{1,0:T(8,128)(2,1)S(1)}, u32[]{:S(2)}, u32[]{:S(2)}) collective-permute-start(bf16[320,1152]{1,0:T(8,128)(2,1)S(1)} %bitcast.51), channel_id=1, source_target_pairs={{0,32},{32,0},{1,33},{33,1},{2,34},{34,2},{3,35},{35,3},{4,36},{36... | collective-permute-start | bytes 2211848 | tf_op jit(solution)/shard_map/ppermute | solution.py:152
  128.8 5.6 %copy-start.10 = (bf16[320,256]{1,0:T(8,128)(2,1)}, bf16[320,256]{1,0:T(8,128)(2,1)S(1)}, u32[]{:S(2)}) copy-start(bf16[320,256]{1,0:T(8,128)(2,1)S(1)} %get-tuple-element.87) | copy-start | bytes 491524
  128.9 5.0 %copy-start.12 = (bf16[320,256]{1,0:T(8,128)(2,1)}, bf16[320,256]{1,0:T(8,128)(2,1)S(1)}, u32[]{:S(2)}) copy-start(bf16[320,256]{1,0:T(8,128)(2,1)S(1)} %get-tuple-element.83) | copy-start | bytes 491524
  128.9 5.6 %copy-start.14 = (bf16[320,256]{1,0:T(8,128)(2,1)}, bf16[320,256]{1,0:T(8,128)(2,1)S(1)}, u32[]{:S(2)}) copy-start(bf16[320,256]{1,0:T(8,128)(2,1)S(1)} %get-tuple-element.82) | copy-start | bytes 491524
  132.2 1.0 copy-start.2
  132.7 1.2 copy-start.4
  133.9 1.1 copy-start.7
  136.8 5.0 %copy-start.29 = (f32[320]{0:T(512)S(1)}, f32[320]{0:T(512)}, u32[]{:S(2)}) copy-start(f32[320]{0:T(512)} %copy-done.28) | copy-start | bytes 3844
  136.8 5.1 %copy-start.31 = (f32[320]{0:T(512)S(1)}, f32[320]{0:T(512)}, u32[]{:S(2)}) copy-start(f32[320]{0:T(512)} %copy-done.30) | copy-start | bytes 3844
  136.8 5.2 %copy-start.22 = (f32[384]{0:T(512)S(1)}, f32[384]{0:T(512)}, u32[]{:S(2)}) copy-start(f32[384]{0:T(512)} %param.9) | copy-start | bytes 4612
  136.8 28.3 %all-to-all-start.3 = ((bf16[32,16,768]{2,1,0:T(8,128)(2,1)}), bf16[32,16,768]{2,1,0:T(8,128)(2,1)S(1)}, u32[]{:S(2)}, u32[]{:S(2)}) async-start(bf16[32,16,768]{2,1,0:T(8,128)(2,1)} %pad_maximum_fusion.3), calls=%async_computation.3 | async-start | bytes 1572864 | tf_op jit(solution)/shard_map/all_to_all | solution.py:213
  142.0 2.9 %copy-start.11 = (bf16[320,256]{1,0:T(8,128)(2,1)S(1)}, bf16[320,256]{1,0:T(8,128)(2,1)}, u32[]{:S(2)}) copy-start(bf16[320,256]{1,0:T(8,128)(2,1)} %copy-done.10) | copy-start | bytes 491524
  142.5 2.4 %copy-start.15 = (bf16[320,256]{1,0:T(8,128)(2,1)S(1)}, bf16[320,256]{1,0:T(8,128)(2,1)}, u32[]{:S(2)}) copy-start(bf16[320,256]{1,0:T(8,128)(2,1)} %copy-done.14) | copy-start | bytes 491524
  144.8 1.4 copy-start.13
  146.2 19.7 %copy-start.17 = (bf16[10,384]{1,0:T(8,128)(2,1)S(1)}, bf16[10,384]{1,0:T(8,128)(2,1)}, u32[]{:S(2)}) copy-start(bf16[10,384]{1,0:T(8,128)(2,1)} %param.8) | copy-start | bytes 23044
  146.2 19.7 %copy-start.18 = (bf16[10,384]{1,0:T(8,128)(2,1)S(1)}, bf16[10,384]{1,0:T(8,128)(2,1)}, u32[]{:S(2)}) copy-start(bf16[10,384]{1,0:T(8,128)(2,1)} %param.15) | copy-start | bytes 23044

commit v2 on v1

v2 whole, which is shorter than its diff:
```python
import jax
import jax.numpy as jnp
from jax import lax
from jax.experimental import pallas as pl
from jax.experimental.pallas import tpu as pltpu
from jax.sharding import Mesh
from jax.sharding import PartitionSpec as P

HEAD = 128
QUARTER = 256
WIDE = 1024
EXTRA = 8
PACK = WIDE + HEAD
EPS = 1e-06
ROW = ("z", "core")
COL = ("x", "y")
F32 = jnp.float32
BF16 = jnp.bfloat16

NN = (((1,), (0,)), ((), ()))
NT = (((1,), (1,)), ((), ()))
TN = (((0,), (0,)), ((), ()))


def dot(a, b, dims):
    return lax.dot_general(a, b, dims, preferred_element_type=F32)


def split(values, parts):
    out = []
    for _ in range(parts):
        high = values.astype(BF16).astype(F32)
        out.append(high)
        values = values - high
    return out


def one_hot(rows, lanes, first):
    lane = lax.broadcasted_iota(jnp.int32, (rows, lanes), 1)
    return lane == lax.broadcasted_iota(jnp.int32, (rows, lanes), 0) + first


def to_column(row, hot):
    return jnp.sum(jnp.where(hot, row, 0.0), 1, keepdims=True)


def to_row(column, hot):
    return jnp.sum(jnp.where(hot, column, 0.0), 0, keepdims=True)


def call(kernel, outs, scratch, *args):
    return pl.pallas_call(
        kernel,
        out_shape=outs,
        in_specs=[pl.BlockSpec(memory_space=pltpu.VMEM)] * len(args),
        out_specs=[pl.BlockSpec(memory_space=pltpu.VMEM)] * len(outs),
        scratch_shapes=scratch,
        compiler_params=pltpu.CompilerParams(vmem_limit_bytes=40 * 2**20),
    )(*args)


def shape(dims, dtype=BF16):
    return jax.ShapeDtypeStruct(dims, dtype)


def spread_kernel(x_ref, cot_ref, out_ref, block):
    rows = x_ref.shape[0]
    block[...] = jnp.zeros_like(block)
    block[0:rows] = x_ref[...].astype(F32)
    block[rows : 2 * rows] = cot_ref[...].astype(F32)
    out_ref[...] = jnp.broadcast_to(block[...].astype(BF16)[None], out_ref.shape)


def product_kernel(
    got_ref, gain_ref, wq_ref, wu_ref, wa_ref, wd_ref, own_ref, other_ref, x_ref, cot_ref, xs, cs, lay
):
    n_col, rows = got_ref.shape[0], x_ref.shape[0] // got_ref.shape[0]
    tokens = x_ref.shape[0]
    for c in range(n_col):
        both = got_ref[c].astype(F32)
        xs[c * rows : (c + 1) * rows, :] = both[0:rows]
        cs[c * rows : (c + 1) * rows, :] = both[rows : 2 * rows]
    x = xs[0:tokens, :]
    gain = gain_ref[...]
    xs[tokens:, :] = jnp.concatenate(split(gain, 3) + [jnp.zeros((5, gain.shape[1]), F32)], 0)
    x_low = x.astype(BF16)
    x_ref[...] = x_low
    cot = cs[...].astype(BF16)
    cot_ref[...] = cot
    xg = jnp.concatenate([x * gain, xs[tokens:, :]], 0).astype(BF16)
    core = lax.axis_index("core")

    p = dot(xg, wq_ref[...], NN)
    lay[0, 0:tokens, 0 : 3 * HEAD] = p[0:tokens]
    c_qkv = jnp.sum(p[tokens:], 0, keepdims=True)
    p = dot(xg, wu_ref[...], NN)
    lay[0, 0:tokens, 512:768] = p[0:tokens, 0:256]
    lay[1, 0:tokens, 0:256] = p[0:tokens, 256:512]
    lay[1, 0:tokens, 512:768] = p[0:tokens, 512:768]
    c_up = jnp.sum(p[tokens:], 0, keepdims=True)
    lay[0, 0:tokens, 384:512] = dot(cot, wa_ref[...], NT)
    p = dot(cot, wd_ref[...], NT)
    lay[0, 0:tokens, 768:1024] = p[:, 0:256]
    lay[1, 0:tokens, 256:512] = p[:, 256:512]
    lay[1, 0:tokens, 768:1024] = p[:, 512:768]

    ones = jnp.ones((8, x.shape[1]), BF16)
    square = x * x
    high = square.astype(BF16)
    low = (square - high.astype(F32)).astype(BF16)
    s_1 = dot(ones, x_low, NT)[0:1]
    s_2 = (dot(ones, high, NT) + dot(ones, low, NT))[0:1]
    fill = jnp.zeros((1, 512 - tokens), F32)
    blank = jnp.zeros((1, 256), F32)
    mixed = jnp.concatenate([s_1, fill, c_qkv, blank[:, 0:128]], 1)
    s_2 = jnp.concatenate([s_2, fill, blank, blank], 1)
    c_0 = jnp.concatenate([c_qkv, blank[:, 0:128], c_up[:, 0:256], blank], 1)
    c_1 = jnp.concatenate([c_up[:, 256:512], blank, c_up[:, 512:768], blank], 1)
    zeros = jnp.zeros((5, WIDE), F32)
    lay[0, tokens:, :] = jnp.concatenate([c_0, mixed, s_2, zeros], 0)
    lay[1, tokens:, :] = jnp.concatenate([c_1, mixed, s_2, zeros], 0)
    own_ref[...] = lay[core]
    other_ref[0:tokens, :] = lay[1 - core, 0:tokens, :].astype(BF16)
    c_other = lay[1 - core, tokens : tokens + 1, :]
    other_ref[tokens:, :] = jnp.concatenate(
        split(c_other, 2) + split(mixed, 3) + split(s_2, 3), 0
    ).astype(BF16)


def half_kernel(own_ref, came_ref, out_ref):
    n_z, rows = out_ref.shape[0], out_ref.shape[1] - EXTRA
    tokens = n_z * rows
    parts = came_ref[tokens:, :].astype(F32)
    own = own_ref[tokens:, :]
    c_vec = own[0:1] + parts[0:1] + parts[1:2]
    mixed = own[1:2] + jnp.sum(parts[2:5], 0, keepdims=True)
    s_2 = own[2:3] + jnp.sum(parts[5:8], 0, keepdims=True)
    extra = jnp.concatenate(split(c_vec, 2) + split(mixed, 3) + split(s_2, 3), 0).astype(BF16)
    for d in range(n_z):
        at = pl.ds(d * rows, rows)
        out_ref[d, 0:rows, :] = (own_ref[at, :] + came_ref[at, :].astype(F32)).astype(BF16)
        out_ref[d, rows:, :] = extra


def gelu_parts(x):
    c = 0.7978845608028654
    t = jnp.tanh(c * (x + 0.044715 * (x * x * x)))
    half = 0.5 * (1.0 + t)
    slope = half + 0.5 * x * (1.0 - t * t) * (c * (1.0 + 3 * 0.044715 * (x * x)))
    return x * half, slope


def row_kernel(model_width, got_ref, qk_gain_ref, out_ref, stats_ref):
    n_z, rows = got_ref.shape[0], got_ref.shape[1] - EXTRA
    total = got_ref[0].astype(F32)
    for d in range(1, n_z):
        total = total + got_ref[d].astype(F32)
    c_tot = jnp.sum(total[rows : rows + 2], 0, keepdims=True)
    mixed = jnp.sum(total[rows + 2 : rows + 5], 0, keepdims=True)
    mean = mixed[:, 0:384] / model_width
    var = jnp.sum(total[rows + 5 :, 0:384], 0, keepdims=True) / model_width - mean * mean
    inv = lax.rsqrt(var + EPS)
    stats_ref[...] = jnp.concatenate([mean, inv, mixed[:, 512:896], jnp.zeros((5, 384), F32)], 0)
    hot = one_hot(rows, 384, lax.axis_index("z") * rows)
    mean_z, inv_z = to_column(mean, hot), to_column(inv, hot)
    total = total[0:rows]

    def columns(at, size):
        return (total[:, at : at + size] - mean_z * c_tot[:, at : at + size]) * inv_z

    def mlp(at):
        up = columns(at, 256)
        hidden, slope = gelu_parts(up)
        d_up = (total[:, at + 256 : at + 512].astype(BF16).astype(F32) * slope).astype(BF16)
        d_f = d_up.astype(F32)
        return (
            hidden.astype(BF16),
            d_up,
            jnp.sum(d_f * c_tot[:, at : at + 256], 1, keepdims=True),
            jnp.sum(d_f * up, 1, keepdims=True),
        )

    def norm(at, g):
        values = columns(at, HEAD)
        average = jnp.mean(values, -1, keepdims=True)
        centred = values - average
        rstd = lax.rsqrt(jnp.mean(centred * centred, -1, keepdims=True) + EPS)
        return (centred * rstd * g).astype(BF16), rstd, average

    lane = lax.broadcasted_iota(jnp.int32, (rows, HEAD), 1)

    def pack(values):
        out = jnp.zeros((rows, HEAD), F32)
        for i, v in enumerate(values):
            high = v.astype(BF16).astype(F32)
            out = jnp.where(lane == i, high, out)
            out = jnp.where(lane == i + 8, v - high, out)
        return out.astype(BF16)

    def store(at, value):
        out_ref[:, :, at : at + value.shape[1]] = jnp.broadcast_to(value[None], (n_z, *value.shape))

    hidden, d_up, s1_b, s2_b = mlp(512)
    store(512, hidden)
    store(768, d_up)
    core = lax.axis_index("core")

    @pl.when(core == 0)
    def _():
        q, rstd_q, mean_q = norm(0, qk_gain_ref[0:1])
        k, rstd_k, mean_k = norm(HEAD, qk_gain_ref[1:2])
        store(0, q)
        store(HEAD, k)
        store(2 * HEAD, columns(2 * HEAD, HEAD).astype(BF16))
        store(3 * HEAD, total[:, 3 * HEAD : 4 * HEAD].astype(BF16))
        store(WIDE, pack([rstd_q, rstd_k, mean_q, mean_k, s1_b, s2_b]))

    @pl.when(core != 0)
    def _():
        hidden, d_up, s1_a, s2_a = mlp(0)
        store(0, hidden)
        store(256, d_up)
        none = jnp.zeros_like(s1_a)
        store(WIDE, pack([none, none, none, none, s1_a + s1_b, s2_a + s2_b]))


def attention_kernel(
    mine_ref, theirs_ref, stats_ref, x_ref, gain_ref, qk_gain_ref, wq_ref, wu_ref, wa_ref, wd_ref,
    send_ref, d_gain_ref, hidden_ref, d_up_ref, att_ref, d_qkv_ref, normed_ref, both, block
):
    n_col = send_ref.shape[0]
    tokens, width = x_ref.shape
    rows = tokens // n_col
    core = lax.axis_index("core")
    both[core] = mine_ref[...]
    both[1 - core] = theirs_ref[...]
    hidden_ref[:, 0:256] = both[0, :, 512:768]
    hidden_ref[:, 256:512] = both[1, :, 0:256]
    hidden_ref[:, 512:768] = both[1, :, 512:768]
    d_up_ref[:, 0:256] = both[0, :, 768:1024]
    d_up_ref[:, 256:512] = both[1, :, 256:512]
    d_up_ref[:, 512:768] = both[1, :, 768:1024]
    scale = HEAD ** (-0.5)
    q, k, v, d_att = (both[0, :, i * HEAD : (i + 1) * HEAD] for i in range(4))
    e = both[0, :, WIDE:].astype(F32)
    e1 = both[1, :, WIDE:].astype(F32)

    def scalar(i):
        return e[:, i : i + 1] + e[:, i + 8 : i + 9]

    def scalar1(i):
        return e1[:, i : i + 1] + e1[:, i + 8 : i + 9]

    scores = dot(q, k, NT) * scale
    top = jnp.max(scores, -1, keepdims=True)
    probs = jnp.exp(scores - top)
    probs = probs / jnp.sum(probs, -1, keepdims=True)
    low = probs.astype(BF16)
    attended = dot(low, v, NN).astype(BF16)
    att_ref[...] = attended
    branch = dot(attended, wa_ref[...], NN) + dot(hidden_ref[...], wd_ref[...], NN)
    d_probs = dot(d_att, v, NT)
    delta = jnp.sum(probs * d_probs, -1, keepdims=True)
    d_scores = (probs * (d_probs - delta)).astype(BF16)
    d_qn = dot(d_scores, k, NN) * scale
    d_kn = dot(d_scores, q, TN) * scale
    d_v = dot(low, d_att, TN).astype(BF16)

    def back(rows_low, rstd, average, g, d_rows):
        unit = rows_low.astype(F32) / g
        d_unit = d_rows * g
        d_values = (
            d_unit
            - jnp.mean(d_unit, -1, keepdims=True)
            - unit * jnp.mean(d_unit * unit, -1, keepdims=True)
        ) * rstd
        return d_values.astype(BF16), jnp.sum(d_rows * unit, 0, keepdims=True), unit / rstd + average

    d_q, g_q, query = back(q, scalar(0), scalar(2), qk_gain_ref[0:1], d_qn)
    d_k, g_k, key = back(k, scalar(1), scalar(3), qk_gain_ref[1:2], d_kn)
    d_gain_ref[0:1, :] = g_q
    d_gain_ref[1:2, :] = g_k
    d_qkv_ref[:, 0:HEAD] = d_q
    d_qkv_ref[:, HEAD : 2 * HEAD] = d_k
    d_qkv_ref[:, 2 * HEAD :] = d_v
    d_normed = dot(d_qkv_ref[...], wq_ref[...], NT) + dot(d_up_ref[...], wu_ref[...], NT)

    c_h = stats_ref[2:3]
    d_qf, d_kf, d_vf = d_q.astype(F32), d_k.astype(F32), d_v.astype(F32)
    t_1 = scalar(4) + scalar1(4)
    t_1 += jnp.sum(d_qf * c_h[:, 0:HEAD] + d_kf * c_h[:, HEAD : 2 * HEAD] + d_vf * c_h[:, 2 * HEAD :], 1, keepdims=True)
    t_2 = scalar(5) + scalar1(5)
    t_2 += jnp.sum(d_qf * query + d_kf * key + d_vf * v.astype(F32), 1, keepdims=True)
    hot = one_hot(tokens, 384, 0)
    mean, inv = to_column(stats_ref[0:1], hot), to_column(stats_ref[1:2], hot)
    xhat = (x_ref[...].astype(F32) - mean) * inv
    normed_ref[...] = (xhat * gain_ref[...]).astype(BF16)
    part = split(jnp.sum(d_normed * xhat, 0, keepdims=True), 2)
    tail = jnp.concatenate(part + [to_row(t_1, hot), to_row(t_2, hot)], 0)
    block[0] = branch
    block[1] = d_normed
    for c in range(n_col):
        at = pl.ds(c * rows, rows)
        send_ref[c] = jnp.concatenate([block[0, at, :], block[1, at, :], tail], 0).astype(BF16)


def finish_kernel(
    model_width, got_ref, stats_ref, x_ref, cot_ref, gain_ref, out_ref, grad_ref, d_gain_ref
):
    rows = x_ref.shape[0]
    total = got_ref[0].astype(F32)
    for c in range(1, got_ref.shape[0]):
        total = total + got_ref[c].astype(F32)
    x = x_ref[...].astype(F32)
    out_ref[...] = (x + total[0:rows]).astype(BF16)
    d_gain_ref[...] = total[2 * rows : 2 * rows + 1] + total[2 * rows + 1 : 2 * rows + 2]
    col = lax.axis_index("x") * lax.axis_size("y") + lax.axis_index("y")
    hot = one_hot(rows, 384, col * rows)
    t_1 = to_column(total[2 * rows + 2 : 2 * rows + 3], hot)
    t_2 = to_column(total[2 * rows + 3 : 2 * rows + 4], hot)
    mean, inv = to_column(stats_ref[0:1], hot), to_column(stats_ref[1:2], hot)
    xhat = (x - mean) * inv
    d_xhat = total[rows : 2 * rows] * gain_ref[...]
    grad = (d_xhat - t_1 / model_width - xhat * t_2 / model_width) * inv
    grad_ref[...] = (cot_ref[...].astype(F32) + grad).astype(BF16)


def shards(tokens_in, gain, w_qkv, qk_gain, w_up, w_attn_out, w_down, cotangent):
    rows_c, width = tokens_in.shape
    n_col = lax.axis_size(COL)
    n_z = lax.axis_size("z")
    tokens = rows_c * n_col
    rows_z = tokens // n_z
    model_width = width * lax.axis_size(ROW)
    swap = [(0, 1), (1, 0)]
    hidden_w = w_up.shape[1]
    gain_row = gain.reshape(1, width)
    w_qkv2 = w_qkv.reshape(width, 3 * HEAD)
    chunk = 2 * rows_c + 4

    (spread,) = call(
        spread_kernel,
        [shape((n_col, chunk, width))],
        [pltpu.VMEM((chunk, width), F32)],
        tokens_in,
        cotangent,
    )
    got = lax.all_to_all(spread, COL, 0, 0)

    own, other, x_all, cot_all = call(
        product_kernel,
        [
            shape((tokens + EXTRA, WIDE), F32),
            shape((tokens + EXTRA, WIDE)),
            shape((tokens, width)),
            shape((tokens, width)),
        ],
        [
            pltpu.VMEM((tokens + EXTRA, width), F32),
            pltpu.VMEM((tokens, width), F32),
            pltpu.VMEM((2, tokens + EXTRA, WIDE), F32),
        ],
        got,
        gain_row,
        w_qkv2,
        w_up,
        w_attn_out,
        w_down,
    )
    came = lax.ppermute(other, "core", swap)
    (half,) = call(half_kernel, [shape((n_z, rows_z + EXTRA, WIDE))], [], own, came)
    got = lax.all_to_all(half, "z", 0, 0)

    packed, stats = call(
        lambda *refs: row_kernel(model_width, *refs),
        [shape((n_z, rows_z, PACK)), shape((8, width), F32)],
        [],
        got,
        qk_gain,
    )
    mine = lax.all_to_all(packed, "z", 0, 0).reshape(tokens, PACK)
    theirs = lax.ppermute(mine, "core", swap)

    send, d_qk_gain, hidden, d_up, attended, d_qkv, normed = call(
        attention_kernel,
        [
            shape((n_col, chunk, width)),
            shape((2, HEAD), F32),
            shape((tokens, hidden_w)),
            shape((tokens, hidden_w)),
            shape((tokens, HEAD)),
            shape((tokens, 3 * HEAD)),
            shape((tokens, width)),
        ],
        [pltpu.VMEM((2, tokens, PACK), BF16), pltpu.VMEM((2, tokens, width), F32)],
        mine,
        theirs,
        stats,
        x_all,
        gain_row,
        qk_gain,
        w_qkv2,
        w_up,
        w_attn_out,
        w_down,
    )
    got = lax.all_to_all(send, COL, 0, 0)
    d_w_qkv = dot(normed, d_qkv, TN).astype(BF16).reshape(w_qkv.shape)
    d_w_up = dot(normed, d_up, TN).astype(BF16)
    d_w_attn_out = dot(attended, cot_all, TN).astype(BF16)
    d_w_down = dot(hidden, cot_all, TN).astype(BF16)
    layer_out, token_grad, d_gain = call(
        lambda *refs: finish_kernel(model_width, *refs),
        [shape((rows_c, width)), shape((rows_c, width)), shape((1, width), F32)],
        [],
        got,
        stats,
        tokens_in,
        cotangent,
        gain_row,
    )
    return (
        layer_out,
        token_grad,
        d_gain.reshape(width),
        d_w_qkv,
        d_qk_gain,
        d_w_up,
        d_w_attn_out,
        d_w_down,
    )


def solution(mesh):
    fine = Mesh(mesh.devices.reshape(-1, 2, 4, 8), ("z", "core", "x", "y"))
    in_specs = (
        P(COL, ROW),
        P(ROW),
        P(ROW, None, COL),
        P(None, COL),
        P(ROW, COL),
        P(COL, ROW),
        P(COL, ROW),
        P(COL, ROW),
    )
    out_specs = (
        P(COL, ROW),
        P(COL, ROW),
        P(ROW),
        P(ROW, None, COL),
        P(None, COL),
        P(ROW, COL),
        P(COL, ROW),
        P(COL, ROW),
    )
    return jax.shard_map(shards, mesh=fine, in_specs=in_specs, out_specs=out_specs, check_vma=False)
```

time: 168 us -> 130 us (0.77)
  blocking collectives: 24.9 us -> 57.1 us
  waiting for transfers between devices: 63.4 us -> 37.2 us
  local copies, waits for them, and re-layouts: 21.8 us -> 3.56 us
  other arithmetic: 16.7 us -> 0.6 us
  starting transfers between devices: 29.4 us -> 19 us
  Pallas kernels: 0 us -> 7.28 us
  matrix products: 8.76 us -> 3.99 us
    all_to_all x1 -> x2, blocking collectives: 24.9 us -> 57.1 us  [the longest x1 33.5 us: shards(): got = lax.all_to_all(half, 'z', 0, 0)]
    all_to_all x3 -> x2, waiting for transfers between devices: 58.8 us -> 33 us  [the longest x1 18.5 us: shards(): got = lax.all_to_all(spread, COL, 0, 0)]
    convert_element_type x28 -> x0, other arithmetic: 10.5 us -> none  [the longest x17 5.22 us: split(): out.append(high.astype(BF16))]
    all_to_all x3 -> x2, starting transfers between devices: 25.6 us -> 15.2 us  [the longest x1 10.3 us: shards(): got = lax.all_to_all(spread, COL, 0, 0)]
    another operation x25 -> x0, local copies, waits for them, and re-layouts: 8.68 us -> none  [the longest x13 8.56 us: extras(): return jnp.stack(rows)]
    pallas_call x0 -> x6, Pallas kernels: none -> 7.28 us  [call(): pl.pallas_call(kernel, out_shape=outs, in_specs=[pl.BlockSpec(memory_spac...]
    concatenate x8 -> x0, local copies, waits for them, and re-layouts: 6.38 us -> none  [the longest x1 4.98 us: shards(): sent = jnp.concatenate([other, extras(c_other, sum_1, sum_2, c_qkv)], 0)]
    dot_general x18 -> x4, matrix products: 8.76 us -> 3.99 us  [dot(): return lax.dot_general(a, b, dims, preferred_element_type=F32)]
  transfers between devices with their start and end apart: 5 -> 4, of which waited for: 5 -> 4; matrix products, arithmetic and copies ran while one was open for 4% -> 4% of each run, Pallas kernels for 0% -> 0%
where the time goes in v2:
time: 130 us
  blocking collectives  57.1 us (44%)
  waiting for transfers between devices  37.2 us (29%)
  starting transfers between devices  19 us (15%)
  Pallas kernels  7.28 us (6%)
  matrix products  3.99 us (3%)
  local copies, waits for them, and re-layouts  3.56 us (3%)
    all_to_all x1, blocking collectives, shards(): got = lax.all_to_all(half, 'z', 0, 0)  33.5 us
    all_to_all x1, blocking collectives, shards(): mine = lax.all_to_all(packed, 'z', 0, 0).reshape(tokens, PACK)  23.6 us
    all_to_all x1, waiting for transfers between devices, shards(): got = lax.all_to_all(spread, COL, 0, 0)  18.5 us
    all_to_all x1, waiting for transfers between devices, shards(): got = lax.all_to_all(send, COL, 0, 0)  14.4 us
    all_to_all x1, starting transfers between devices, shards(): got = lax.all_to_all(spread, COL, 0, 0)  10.3 us
    pallas_call x6, Pallas kernels, call(): pl.pallas_call(kernel, out_shape=outs, in_specs=[pl.BlockSpec(memory_spac...  7.28 us
    all_to_all x1, starting transfers between devices, shards(): got = lax.all_to_all(send, COL, 0, 0)  4.87 us
    dot_general x4, matrix products, dot(): return lax.dot_general(a, b, dims, preferred_element_type=F32)  3.99 us
  transfers between devices with their start and end apart: 4, of which 4 were waited for; matrix products, arithmetic and copies ran while one was open for 4% of the time, Pallas kernels for 0%

profile of v2, /device:TPU:8, one launch (start us, length us, event | category | flops | bytes accessed | tf_op | source)
XLA Modules:
  0.0 129.5 jit_solution(7637585645930163432)
XLA Ops:
  0.6 0.0 copy-start.3
  0.6 0.7 copy-done.3
  1.3 0.0 copy-start.5
  1.3 0.7 copy-done.5
  2.1 0.0 copy-start.11
  2.1 0.0 copy-start.10
  2.1 0.9 shard_map.143
  2.9 0.0 copy-start
  2.9 0.0 copy-start.1
  2.9 0.0 copy-start.2
  2.9 10.3 %all-to-all-start = ((bf16[32,24,384]{2,1,0:T(8,128)(2,1)}), bf16[32,24,384]{2,1,0:T(8,128)(2,1)S(1)}, u32[]{:S(2)}, u32[]{:S(2)}) async-start(bf16[32,24,384]{2,1,0:T(8,128)(2,1)} %shard_map.143), calls=%async_computation | async-start | bytes 1179648 | tf_op jit(solution)/shard_map/all_to_all | solution.py:348
  13.2 0.0 copy-done.11
  13.3 0.0 copy-done.10
  13.3 0.2 copy.18
  13.5 0.2 copy.19.wq_ref
  13.7 18.5 %all-to-all-done.got_ref = bf16[32,24,384]{2,1,0:T(8,128)(2,1)S(1)} async-done(((bf16[32,24,384]{2,1,0:T(8,128)(2,1)}), bf16[32,24,384]{2,1,0:T(8,128)(2,1)S(1)}, u32[]{:S(2)}, u32[]{:S(2)}) %all-to-all-start) | async-done | bytes 589856 | tf_op jit(solution)/shard_map/all_to_all | solution.py:348
  32.2 0.0 copy-done
  32.3 0.0 copy-done.1
  32.3 0.0 copy-done.2
  32.3 1.7 %shard_map.144 = (f32[328,1024]{1,0:T(8,128)S(1)}, bf16[328,1024]{1,0:T(8,128)(2,1)S(1)}, bf16[320,384]{1,0:T(8,128)(2,1)S(1)}, bf16[320,384]{1,0:T(8,128)(2,1)S(1)}) custom-call(bf16[32,24,384]{2,1,0:T(8,128)(2,1)S(1)} %all-to-all-done.got_ref, f32[1,384]{1,0:T(1,128)S(1)} %reshape.31.gain_ref.refs_4_, bf16[384,384]{1,0:T(8,128)(2,1)S(1)} %copy.19.wq_ref, ...), custom_call_target="tpu_custom_call" | custom-call | tf_op jit(solution)/shard_map/pallas_call | solution.py:52
  34.0 1.9 %collective-permute-start = (bf16[328,1024]{1,0:T(8,128)(2,1)S(1)}, bf16[328,1024]{1,0:T(8,128)(2,1)S(1)}, u32[]{:S(2)}, u32[]{:S(2)}) collective-permute-start(bf16[328,1024]{1,0:T(8,128)(2,1)S(1)} %get-tuple-element.25), channel_id=1, source_target_pairs={{0,32},{32,0},{1,33},{33,1},{2,34},{34,2},{3,35},{35,3},{4,36},{36... | collective-permute-start | bytes 2015240 | tf_op jit(solution)/shard_map/ppermute | solution.py:370
  35.9 2.1 %collective-permute-done.came_ref = bf16[328,1024]{1,0:T(8,128)(2,1)S(1)} collective-permute-done((bf16[328,1024]{1,0:T(8,128)(2,1)S(1)}, bf16[328,1024]{1,0:T(8,128)(2,1)S(1)}, u32[]{:S(2)}, u32[]{:S(2)}) %collective-permute-start) | collective-permute-done | bytes 671776 | tf_op jit(solution)/shard_map/ppermute | solution.py:370
  38.0 0.2 shard_map.145
  38.2 0.0 copy-start.7
  38.2 33.5 %all_to_all.20.refs_0_ = bf16[8,48,1024]{2,1,0:T(8,128)(2,1)S(1)} all-to-all(bf16[8,48,1024]{2,1,0:T(8,128)(2,1)S(1)} %shard_map.145), channel_id=1, replica_groups=mesh['z'=8,'core'=2,'x'=4,'y'=8] {'z'}, dimensions={0} | all-to-all | bytes 1572864 | tf_op jit(solution)/shard_map/all_to_all | solution.py:372
  71.7 0.0 copy-done.7
  71.7 0.4 shard_map.146
  72.2 23.6 %all_to_all.21 = bf16[8,40,1152]{2,1,0:T(8,128)(2,1)S(1)} all-to-all(bf16[8,40,1152]{2,1,0:T(8,128)(2,1)S(1)} %get-tuple-element.26), channel_id=1, replica_groups=mesh['z'=8,'core'=2,'x'=4,'y'=8] {'z'}, dimensions={0} | all-to-all | bytes 1474560 | tf_op jit(solution)/shard_map/all_to_all | solution.py:381
  95.8 1.9 %collective-permute-start.1 = (bf16[320,1152]{1,0:T(8,128)(2,1)S(1)}, bf16[320,1152]{1,0:T(8,128)(2,1)S(1)}, u32[]{:S(2)}, u32[]{:S(2)}) collective-permute-start(bf16[320,1152]{1,0:T(8,128)(2,1)S(1)} %bitcast.11), channel_id=1, source_target_pairs={{0,32},{32,0},{1,33},{33,1},{2,34},{34,2},{3,35},{35,3},{4,36},{36... | collective-permute-start | bytes 2211848 | tf_op jit(solution)/shard_map/ppermute | solution.py:382
  97.7 2.2 %collective-permute-done.1.theirs_ref = bf16[320,1152]{1,0:T(8,128)(2,1)S(1)} collective-permute-done((bf16[320,1152]{1,0:T(8,128)(2,1)S(1)}, bf16[320,1152]{1,0:T(8,128)(2,1)S(1)}, u32[]{:S(2)}, u32[]{:S(2)}) %collective-permute-start.1) | collective-permute-done | bytes 737312 | tf_op jit(solution)/shard_map/ppermute | solution.py:382
  99.9 3.3 %shard_map.147 = (bf16[32,24,384]{2,1,0:T(8,128)(2,1)}, f32[2,128]{1,0:T(2,128)}, bf16[320,768]{1,0:T(8,128)(2,1)S(1)}, bf16[320,768]{1,0:T(8,128)(2,1)S(1)}, bf...) custom-call(bf16[320,1152]{1,0:T(8,128)(2,1)S(1)} %bitcast.12, ...), custom_call_target="tpu_custom_call" | custom-call | tf_op jit(solution)/shard_map/pallas_call | solution.py:52
  103.2 0.0 copy-start.8
  103.2 0.8 copy-done.8
  104.0 4.9 %all-to-all-start.3 = ((bf16[32,24,384]{2,1,0:T(8,128)(2,1)}), bf16[32,24,384]{2,1,0:T(8,128)(2,1)S(1)}, u32[]{:S(2)}, u32[]{:S(2)}) async-start(bf16[32,24,384]{2,1,0:T(8,128)(2,1)} %get-tuple-element.29), calls=%async_computation.3 | async-start | bytes 1179648 | tf_op jit(solution)/shard_map/all_to_all | solution.py:407
  108.9 0.0 copy-start.9
  108.9 0.4 convolution_convert_fusion.2
  109.3 0.9 copy.21
  110.2 0.9 convolution_convert_fusion.3
  111.1 0.0 copy-done.9
  111.1 0.0 copy-start.4
  111.1 0.0 copy-start.6
  111.1 1.4 %convolution_convert_fusion = bf16[768,384]{1,0:T(8,128)(2,1)} fusion(bf16[320,768]{1,0:T(8,128)(2,1)S(1)} %copy-done.9, bf16[320,384]{1,0:T(8,128)(2,1)S(1)} %get-tuple-element.38), kind=kOutput, calls=%fused_computation | convolution fusion | flops 189038592 | bytes 1327104 | tf_op jit(solution)/shard_map/dot_general | solution.py:26
  112.5 1.3 %convolution_convert_fusion.1 = bf16[384,768]{1,0:T(8,128)(2,1)} fusion(bf16[320,384]{1,0:T(8,128)(2,1)S(1)} %get-tuple-element.33, bf16[320,768]{1,0:T(8,128)(2,1)S(1)} %get-tuple-element.36), kind=kOutput, calls=%fused_computation.1 | convolution fusion | flops 189038592 | bytes 1327104 | tf_op jit(solution)/shard_map/dot_general | solution.py:26
  113.8 14.4 %all-to-all-done.3.refs_0_ = bf16[32,24,384]{2,1,0:T(8,128)(2,1)S(1)} async-done(((bf16[32,24,384]{2,1,0:T(8,128)(2,1)}), bf16[32,24,384]{2,1,0:T(8,128)(2,1)S(1)}, u32[]{:S(2)}, u32[]{:S(2)}) %all-to-all-start.3) | async-done | bytes 589856 | tf_op jit(solution)/shard_map/all_to_all | solution.py:407
  128.2 0.0 copy-done.4
  128.2 0.0 copy-done.6
  128.2 0.7 shard_map.148
  129.0 0.6 reduce
  (1 shorter events, 0.0 us)
Async XLA Ops:
  0.6 0.7 copy-start.3
  1.3 0.7 copy-start.5
  2.1 11.2 %copy-start.11 = (f32[384]{0:T(512)S(1)}, f32[384]{0:T(512)}, u32[]{:S(2)}) copy-start(f32[384]{0:T(512)} %param.9) | copy-start | bytes 4612
  2.1 11.2 %copy-start.10 = (bf16[384,3,128]{2,0,1:T(8,128)(2,1)S(1)}, bf16[384,3,128]{2,0,1:T(8,128)(2,1)}, u32[]{:S(2)}) copy-start(bf16[384,3,128]{2,0,1:T(8,128)(2,1)} %param.10) | copy-start | bytes 884740
  2.9 29.3 %copy-start = (bf16[384,768]{1,0:T(8,128)(2,1)S(1)}, bf16[384,768]{1,0:T(8,128)(2,1)}, u32[]{:S(2)}) copy-start(bf16[384,768]{1,0:T(8,128)(2,1)} %wu_ref.3) | copy-start | bytes 1769476
  2.9 29.3 %copy-start.1 = (bf16[768,384]{1,0:T(8,128)(2,1)S(1)}, bf16[768,384]{1,0:T(8,128)(2,1)}, u32[]{:S(2)}) copy-start(bf16[768,384]{1,0:T(8,128)(2,1)} %wd_ref.3) | copy-start | bytes 1769476
  2.9 29.3 %copy-start.2 = (bf16[128,384]{1,0:T(8,128)(2,1)S(1)}, bf16[128,384]{1,0:T(8,128)(2,1)}, u32[]{:S(2)}) copy-start(bf16[128,384]{1,0:T(8,128)(2,1)} %wa_ref.3) | copy-start | bytes 294916
  2.9 29.3 %all-to-all-start = ((bf16[32,24,384]{2,1,0:T(8,128)(2,1)}), bf16[32,24,384]{2,1,0:T(8,128)(2,1)S(1)}, u32[]{:S(2)}, u32[]{:S(2)}) async-start(bf16[32,24,384]{2,1,0:T(8,128)(2,1)} %shard_map.143), calls=%async_computation | async-start | bytes 1179648 | tf_op jit(solution)/shard_map/all_to_all | solution.py:348
  34.0 4.0 %collective-permute-start = (bf16[328,1024]{1,0:T(8,128)(2,1)S(1)}, bf16[328,1024]{1,0:T(8,128)(2,1)S(1)}, u32[]{:S(2)}, u32[]{:S(2)}) collective-permute-start(bf16[328,1024]{1,0:T(8,128)(2,1)S(1)} %get-tuple-element.25), channel_id=1, source_target_pairs={{0,32},{32,0},{1,33},{33,1},{2,34},{34,2},{3,35},{35,3},{4,36},{36... | collective-permute-start | bytes 2015240 | tf_op jit(solution)/shard_map/ppermute | solution.py:370
  38.2 33.5 %copy-start.7 = (f32[2,128]{1,0:T(2,128)S(1)}, f32[2,128]{1,0:T(2,128)}, u32[]{:S(2)}) copy-start(f32[2,128]{1,0:T(2,128)} %qk_gain_ref.1) | copy-start | bytes 3076
  95.8 4.1 %collective-permute-start.1 = (bf16[320,1152]{1,0:T(8,128)(2,1)S(1)}, bf16[320,1152]{1,0:T(8,128)(2,1)S(1)}, u32[]{:S(2)}, u32[]{:S(2)}) collective-permute-start(bf16[320,1152]{1,0:T(8,128)(2,1)S(1)} %bitcast.11), channel_id=1, source_target_pairs={{0,32},{32,0},{1,33},{33,1},{2,34},{34,2},{3,35},{35,3},{4,36},{36... | collective-permute-start | bytes 2211848 | tf_op jit(solution)/shard_map/ppermute | solution.py:382
  103.2 0.8 copy-start.8
  104.0 24.2 %all-to-all-start.3 = ((bf16[32,24,384]{2,1,0:T(8,128)(2,1)}), bf16[32,24,384]{2,1,0:T(8,128)(2,1)S(1)}, u32[]{:S(2)}, u32[]{:S(2)}) async-start(bf16[32,24,384]{2,1,0:T(8,128)(2,1)} %get-tuple-element.29), calls=%async_computation.3 | async-start | bytes 1179648 | tf_op jit(solution)/shard_map/all_to_all | solution.py:407
  108.9 2.2 %copy-start.9 = (bf16[320,768]{1,0:T(8,128)(2,1)S(1)}, bf16[320,768]{1,0:T(8,128)(2,1)}, u32[]{:S(2)}) copy-start(bf16[320,768]{1,0:T(8,128)(2,1)} %copy-done.8) | copy-start | bytes 1474564
  111.1 17.1 %copy-start.4 = (bf16[10,384]{1,0:T(8,128)(2,1)S(1)}, bf16[10,384]{1,0:T(8,128)(2,1)}, u32[]{:S(2)}) copy-start(bf16[10,384]{1,0:T(8,128)(2,1)} %refs_2_.1) | copy-start | bytes 23044
  111.1 17.1 %copy-start.6 = (bf16[10,384]{1,0:T(8,128)(2,1)S(1)}, bf16[10,384]{1,0:T(8,128)(2,1)}, u32[]{:S(2)}) copy-start(bf16[10,384]{1,0:T(8,128)(2,1)} %refs_3_.1) | copy-start | bytes 23044

commit v3 on v2

v3 whole, which is shorter than its diff:
```python
import jax
import jax.numpy as jnp
from jax import lax
from jax.experimental import pallas as pl
from jax.experimental.pallas import tpu as pltpu
from jax.sharding import Mesh
from jax.sharding import PartitionSpec as P

LANES = 128
EPS = 1e-06
ROW = ("z", "core")
COL = ("x", "y")
F32 = jnp.float32
BF16 = jnp.bfloat16

NN = (((1,), (0,)), ((), ()))
NT = (((1,), (1,)), ((), ()))
TN = (((0,), (0,)), ((), ()))


def dot(a, b, dims):
    return lax.dot_general(a, b, dims, preferred_element_type=F32)


def split(values, parts):
    out = []
    for _ in range(parts):
        high = values.astype(BF16).astype(F32)
        out.append(high)
        values = values - high
    return out


def one_hot(rows, lanes, first):
    lane = lax.broadcasted_iota(jnp.int32, (rows, lanes), 1)
    return lane == lax.broadcasted_iota(jnp.int32, (rows, lanes), 0) + first


def to_column(row, hot):
    return jnp.sum(jnp.where(hot, row, 0.0), 1, keepdims=True)


def to_row(column, hot):
    return jnp.sum(jnp.where(hot, column, 0.0), 0, keepdims=True)


def two_to_row(a, b, rows):
    out = jnp.zeros((1, LANES), F32)
    for at, part in zip((0, 32, 64, 96), split(a, 2) + split(b, 2)):
        out = out + to_row(part, one_hot(rows, LANES, at))
    return out


def two_to_columns(row, rows):
    first = one_hot(rows, LANES, 0) | one_hot(rows, LANES, 32)
    second = one_hot(rows, LANES, 64) | one_hot(rows, LANES, 96)
    return to_column(row, first), to_column(row, second)


def tile(j):
    return slice(j * LANES, (j + 1) * LANES)


def call(kernel, outs, scratch, *args):
    return pl.pallas_call(
        kernel,
        out_shape=outs,
        in_specs=[pl.BlockSpec(memory_space=pltpu.VMEM)] * len(args),
        out_specs=[pl.BlockSpec(memory_space=pltpu.VMEM)] * len(outs),
        scratch_shapes=scratch,
        compiler_params=pltpu.CompilerParams(vmem_limit_bytes=40 * 2**20),
    )(*args)


def shape(dims, dtype=BF16):
    return jax.ShapeDtypeStruct(dims, dtype)


def spread_kernel(x_any, cot_any, out_ref, x_ref, cot_ref, block, sems):
    copies = [
        pltpu.make_async_copy(x_any, x_ref, sems.at[0]),
        pltpu.make_async_copy(cot_any, cot_ref, sems.at[1]),
    ]
    for copy in copies:
        copy.start()
    block[...] = jnp.zeros_like(block)
    rows, width = x_ref.shape
    at = 0
    for copy, ref in zip(copies, (x_ref, cot_ref)):
        copy.wait()
        values = ref[...].astype(F32)
        for j in range(width // LANES):
            block[at : at + rows, :] = values[:, tile(j)]
            at += rows
    out_ref[...] = jnp.broadcast_to(block[...].astype(BF16)[None], out_ref.shape)


def product_kernel(
    got_ref, gain_ref, wq_ref, wu_ref, wa_ref, wd_ref,
    own_ref, other_ref, x_ref, cot_ref, xs, cs, ps, gs, st, lay
):
    tokens, width = x_ref.shape
    n_z = own_ref.shape[0]
    rows_c = tokens // got_ref.shape[0]
    rows = tokens // (2 * n_z)
    f_tiles, b_tiles = ps.shape[1] // LANES, gs.shape[1] // LANES
    f_sum = f_tiles * (rows + 1) + 3
    w_tiles = width // LANES
    for c in range(got_ref.shape[0]):
        values = got_ref[c].astype(F32)
        here = slice(c * rows_c, (c + 1) * rows_c)
        for j in range(w_tiles):
            xs[here, tile(j)] = values[j * rows_c : (j + 1) * rows_c]
            cs[here, tile(j)] = values[(w_tiles + j) * rows_c : (w_tiles + j + 1) * rows_c]
    x = xs[0:tokens, :]
    x_ref[...] = x.astype(BF16)
    cot = cs[...].astype(BF16)
    cot_ref[...] = cot
    gain = gain_ref[...]
    xs[tokens:, :] = jnp.concatenate(split(gain, 3) + [jnp.zeros((5, width), F32)], 0)
    xg = jnp.concatenate([x * gain, xs[tokens:, :]], 0).astype(BF16)
    ps[:, 0 : wq_ref.shape[1]] = dot(xg, wq_ref[...], NN)
    ps[:, wq_ref.shape[1] :] = dot(xg, wu_ref[...], NN)
    gs[:, 0 : wa_ref.shape[0]] = dot(cot, wa_ref[...], NT)
    gs[:, wa_ref.shape[0] :] = dot(cot, wd_ref[...], NT)
    c_vec = jnp.sum(ps[tokens:, :], 0, keepdims=True)
    s_1 = jnp.sum(x, 1, keepdims=True)
    s_2 = jnp.sum(x * x, 1, keepdims=True)
    lane = lax.broadcasted_iota(jnp.int32, (tokens, LANES), 1)
    place = lax.rem(lax.broadcasted_iota(jnp.int32, (tokens, LANES), 0), rows)
    st[...] = jnp.where(lane == place, s_1, 0.0) + jnp.where(lane == place + 32, s_2, 0.0)
    c_rows = jnp.concatenate([c_vec[:, tile(j)] for j in range(f_tiles)], 0)
    fill = jnp.zeros((lay.shape[2] - f_sum - b_tiles * rows, LANES), F32)
    for h in range(2):
        for d in range(n_z):
            at = slice((h * n_z + d) * rows, (h * n_z + d + 1) * rows)
            for j in range(f_tiles):
                lay[h, d, j * rows : (j + 1) * rows, :] = ps[at, tile(j)]
            stat = jnp.sum(st[at, :], 0, keepdims=True)
            lay[h, d, f_tiles * rows : f_sum, :] = jnp.concatenate([c_rows] + split(stat, 3), 0)
            for j in range(b_tiles):
                lay[h, d, f_sum + j * rows : f_sum + (j + 1) * rows, :] = gs[at, tile(j)]
            lay[h, d, f_sum + b_tiles * rows :, :] = fill
    core = lax.axis_index("core")
    own_ref[...] = lay[core]
    other_ref[...] = lay[1 - core].astype(BF16)


def add_kernel(f_sum, own_ref, came_ref, out_ref, block):
    for d in range(own_ref.shape[0]):
        block[...] = own_ref[d] + came_ref[d].astype(F32)
        stat = jnp.sum(block[f_sum - 3 : f_sum, :], 0, keepdims=True)
        block[f_sum - 3 : f_sum, :] = jnp.concatenate(split(stat, 3), 0)
        out_ref[d] = block[...].astype(BF16)


def gelu_parts(x):
    c = 0.7978845608028654
    t = jnp.tanh(c * (x + 0.044715 * (x * x * x)))
    half = 0.5 * (1.0 + t)
    slope = half + 0.5 * x * (1.0 - t * t) * (c * (1.0 + 3 * 0.044715 * (x * x)))
    return x * half, slope


def sum_blocks(got_ref, tot):
    total = got_ref[0].astype(F32)
    for d in range(1, got_ref.shape[0]):
        total = total + got_ref[d].astype(F32)
    tot[...] = total


def row_kernel(model_width, rows, f_sum, got_ref, qk_gain_ref, out_ref, c_ref, tot, block):
    sum_blocks(got_ref, tot)
    tiles = (f_sum - 3) // (rows + 1)
    c_ref[0:tiles, :] = tot[tiles * rows : tiles * rows + tiles, :]
    c_ref[tiles:, :] = jnp.zeros((c_ref.shape[0] - tiles, LANES), F32)
    stat = jnp.sum(tot[f_sum - 3 : f_sum, :], 0, keepdims=True)
    mean = to_column(stat, one_hot(rows, LANES, 0)) / model_width
    var = to_column(stat, one_hot(rows, LANES, 32)) / model_width - mean * mean
    inv = lax.rsqrt(var + EPS)

    def merged(j):
        return (tot[j * rows : (j + 1) * rows, :] - mean * c_ref[j : j + 1, :]) * inv

    def norm(j):
        values = merged(j)
        average = jnp.mean(values, -1, keepdims=True)
        centred = values - average
        rstd = lax.rsqrt(jnp.mean(centred * centred, -1, keepdims=True) + EPS)
        return centred * rstd * qk_gain_ref[j : j + 1], rstd, average

    block[0:rows, :], rstd_q, mean_q = norm(0)
    block[rows : 2 * rows, :], rstd_k, mean_k = norm(1)
    block[2 * rows : 3 * rows, :] = merged(2)
    back = tiles * rows
    block[back : back + rows, :] = tot[f_sum : f_sum + rows, :]
    s_1 = jnp.zeros((rows, LANES), F32)
    s_2 = jnp.zeros((rows, LANES), F32)
    for j in range(3, tiles):
        up = merged(j)
        hidden, slope = gelu_parts(up)
        block[j * rows : (j + 1) * rows, :] = hidden
        at = (j - 2) * rows
        d_hidden = tot[f_sum + at : f_sum + at + rows, :].astype(BF16).astype(F32)
        d_up = (d_hidden * slope).astype(BF16).astype(F32)
        block[back + at : back + at + rows, :] = d_up
        s_1 = s_1 + d_up * c_ref[j : j + 1, :]
        s_2 = s_2 + d_up * up
    s_1 = jnp.sum(s_1, 1, keepdims=True)
    s_2 = jnp.sum(s_2, 1, keepdims=True)
    last = (2 * tiles - 2) * rows
    pairs = ((rstd_q, rstd_k), (mean_q, mean_k), (mean, inv), (s_1, s_2))
    block[last:, :] = jnp.concatenate(
        [two_to_row(a, b, rows) for a, b in pairs]
        + [jnp.zeros((block.shape[0] - last - len(pairs), LANES), F32)],
        0,
    )
    out_ref[...] = jnp.broadcast_to(block[...].astype(BF16)[None], out_ref.shape)


def attention_kernel(
    rows, mine_ref, theirs_ref, c_ref, x_ref, gain_ref, qk_gain_ref, wq_ref, wu_ref, wa_ref, wd_ref,
    send_ref, d_gain_ref, att_ref, hidden_ref, d_qkv_ref, d_up_ref, normed_ref, stats_ref,
    both, cols, block
):
    n_z = mine_ref.shape[0]
    tokens, width = x_ref.shape
    half = tokens // 2
    core = lax.axis_index("core")
    tiles = both.shape[2] // LANES
    f_width = 3 * LANES + hidden_ref.shape[1]
    lane = lax.broadcasted_iota(jnp.int32, (rows, LANES), 1)
    for ref, h in ((mine_ref, core), (theirs_ref, 1 - core)):
        for d in range(n_z):
            values = ref[d].astype(F32)
            at = slice(d * rows, (d + 1) * rows)
            for j in range(tiles):
                both[h, at, tile(j)] = values[j * rows : (j + 1) * rows]
            scalars = jnp.zeros((rows, LANES), F32)
            for i in range(4):
                a, b = two_to_columns(values[tiles * rows + i : tiles * rows + i + 1], rows)
                scalars = jnp.where(lane == 2 * i, a, scalars)
                scalars = jnp.where(lane == 2 * i + 1, b, scalars)
            cols[h, at, :] = scalars

    def whole(at, size):
        return jnp.concatenate([both[h, :, at : at + size].astype(BF16) for h in range(2)], 0)

    def scalar(i):
        return jnp.concatenate([cols[h, :, i : i + 1] for h in range(2)], 0)

    hidden_ref[...] = whole(3 * LANES, hidden_ref.shape[1])
    d_up_ref[...] = whole(f_width + LANES, d_up_ref.shape[1])
    q, k, v = (whole(j * LANES, LANES) for j in range(3))
    d_att = whole(f_width, LANES)
    mean, inv = scalar(4), scalar(5)
    hot = one_hot(tokens, stats_ref.shape[1], 0)
    stats_ref[...] = jnp.concatenate([to_row(mean, hot), to_row(inv, hot)], 0)

    scale = LANES ** (-0.5)
    scores = dot(q, k, NT) * scale
    probs = jnp.exp(scores - jnp.max(scores, -1, keepdims=True))
    probs = probs / jnp.sum(probs, -1, keepdims=True)
    low = probs.astype(BF16)
    attended = dot(low, v, NN).astype(BF16)
    att_ref[...] = attended
    branch = dot(attended, wa_ref[...], NN) + dot(hidden_ref[...], wd_ref[...], NN)
    both[0, :, 0:width] = branch[0:half]
    both[1, :, 0:width] = branch[half:]
    d_probs = dot(d_att, v, NT)
    delta = jnp.sum(probs * d_probs, -1, keepdims=True)
    d_scores = (probs * (d_probs - delta)).astype(BF16)
    d_qn = dot(d_scores, k, NN) * scale
    d_kn = dot(d_scores, q, TN) * scale
    d_v = dot(low, d_att, TN).astype(BF16)

    def back(rows_low, i, g, d_rows):
        rstd, average = scalar(i), scalar(i + 2)
        unit = rows_low.astype(F32) / g
        d_unit = d_rows * g
        d_values = (
            d_unit
            - jnp.mean(d_unit, -1, keepdims=True)
            - unit * jnp.mean(d_unit * unit, -1, keepdims=True)
        ) * rstd
        return d_values.astype(BF16), jnp.sum(d_rows * unit, 0, keepdims=True), unit / rstd + average

    d_q, g_q, query = back(q, 0, qk_gain_ref[0:1], d_qn)
    d_k, g_k, key = back(k, 1, qk_gain_ref[1:2], d_kn)
    d_gain_ref[0:1, :] = g_q
    d_gain_ref[1:2, :] = g_k
    d_qkv_ref[:, tile(0)] = d_q
    d_qkv_ref[:, tile(1)] = d_k
    d_qkv_ref[:, tile(2)] = d_v
    d_normed = dot(d_qkv_ref[...], wq_ref[...], NT) + dot(d_up_ref[...], wu_ref[...], NT)
    both[0, :, width : 2 * width] = d_normed[0:half]
    both[1, :, width : 2 * width] = d_normed[half:]
    d_qf, d_kf, d_vf = d_q.astype(F32), d_k.astype(F32), d_v.astype(F32)
    t_1 = scalar(6)
    t_1 += jnp.sum(d_qf * c_ref[0:1] + d_kf * c_ref[1:2] + d_vf * c_ref[2:3], 1, keepdims=True)
    t_2 = scalar(7)
    t_2 += jnp.sum(d_qf * query + d_kf * key + d_vf * v.astype(F32), 1, keepdims=True)
    xhat = (x_ref[...].astype(F32) - mean) * inv
    normed_ref[...] = (xhat * gain_ref[...]).astype(BF16)
    part = jnp.sum(d_normed * xhat, 0, keepdims=True)
    n_col = send_ref.shape[0]
    rows_c = tokens // n_col
    lane = lax.broadcasted_iota(jnp.int32, (tokens, LANES), 1)
    place = lax.rem(lax.broadcasted_iota(jnp.int32, (tokens, LANES), 0), rows_c)
    ts = jnp.where(lane == place, t_1, 0.0) + jnp.where(lane == place + 32, t_2, 0.0)
    cols[0] = ts[0:half]
    cols[1] = ts[half:]

    w_tiles = width // LANES
    used = 2 * w_tiles * rows_c
    part = jnp.concatenate([part[:, tile(j)] for j in range(w_tiles)], 0)
    for c in range(n_col):
        h, at = divmod(c * rows_c, half)
        at = slice(at, at + rows_c)
        for j in range(2 * w_tiles):
            block[c, j * rows_c : (j + 1) * rows_c, :] = both[h, at, tile(j)]
        t_row = jnp.sum(cols[h, at, :], 0, keepdims=True)
        block[c, used : used + w_tiles + 1, :] = jnp.concatenate([part, t_row], 0)
    send_ref[...] = block[...].astype(BF16)


def finish_kernel(
    model_width, got_ref, stats_ref, x_ref, cot_ref, gain_ref, d_qk_ref,
    out_ref, grad_ref, d_gain_ref, d_qk_out, tot
):
    d_qk_out[...] = d_qk_ref[...]
    sum_blocks(got_ref, tot)
    rows, width = x_ref.shape
    tiles = width // LANES
    last = 2 * rows * tiles
    t_row = tot[last + tiles : last + tiles + 1, :]
    t_1 = to_column(t_row, one_hot(rows, LANES, 0))
    t_2 = to_column(t_row, one_hot(rows, LANES, 32))
    col = lax.axis_index("x") * lax.axis_size("y") + lax.axis_index("y")
    hot = one_hot(rows, stats_ref.shape[1], col * rows)
    mean, inv = to_column(stats_ref[0:1], hot), to_column(stats_ref[1:2], hot)
    for j in range(tiles):
        d_gain_ref[:, tile(j)] = tot[last + j : last + j + 1, :]
        x = x_ref[:, tile(j)].astype(F32)
        out_ref[:, tile(j)] = (x + tot[j * rows : (j + 1) * rows, :]).astype(BF16)
        xhat = (x - mean) * inv
        d_xhat = tot[(tiles + j) * rows : (tiles + j + 1) * rows, :] * gain_ref[:, tile(j)]
        grad = (d_xhat - t_1 / model_width - xhat * t_2 / model_width) * inv
        grad_ref[:, tile(j)] = (cot_ref[:, tile(j)].astype(F32) + grad).astype(BF16)


def shards(tokens_in, gain, w_qkv, qk_gain, w_up, w_attn_out, w_down, cotangent):
    rows_c, width = tokens_in.shape
    n_col = lax.axis_size(COL)
    n_z = lax.axis_size("z")
    tokens = rows_c * n_col
    rows = tokens // (2 * n_z)
    model_width = width * lax.axis_size(ROW)
    swap = [(0, 1), (1, 0)]
    hidden_w = w_up.shape[1]
    gain_row = gain.reshape(1, width)
    w_qkv2 = w_qkv.reshape(width, 3 * LANES)
    in_w, out_w = 3 * LANES + hidden_w, LANES + hidden_w
    tiles = (in_w + out_w) // LANES
    f_sum = in_w // LANES * (rows + 1) + 3
    sum_rows = f_sum + -(-out_w // LANES * rows // 16) * 16
    row_rows = tiles * rows + 8
    col_rows = 2 * width // LANES * rows_c + width // LANES + 1

    def scratch(*dims):
        return pltpu.VMEM(dims, F32)

    (sent,) = pl.pallas_call(
        spread_kernel,
        out_shape=[shape((n_col, col_rows, LANES))],
        in_specs=[pl.BlockSpec(memory_space=pl.ANY)] * 2,
        out_specs=[pl.BlockSpec(memory_space=pltpu.VMEM)],
        scratch_shapes=[
            pltpu.VMEM((rows_c, width), BF16),
            pltpu.VMEM((rows_c, width), BF16),
            scratch(col_rows, LANES),
            pltpu.SemaphoreType.DMA((2,)),
        ],
    )(tokens_in, cotangent)
    got = lax.all_to_all(sent, COL, 0, 0)

    own, other, x_all, cot_all = call(
        product_kernel,
        [
            shape((n_z, sum_rows, LANES), F32),
            shape((n_z, sum_rows, LANES)),
            shape((tokens, width)),
            shape((tokens, width)),
        ],
        [
            scratch(tokens + 8, width),
            scratch(tokens, width),
            scratch(tokens + 8, in_w),
            scratch(tokens, out_w),
            scratch(tokens, LANES),
            scratch(2, n_z, sum_rows, LANES),
        ],
        got,
        gain_row,
        w_qkv2,
        w_up,
        w_attn_out,
        w_down,
    )
    (half,) = call(
        lambda *refs: add_kernel(f_sum, *refs),
        [shape((n_z, sum_rows, LANES))],
        [scratch(sum_rows, LANES)],
        own,
        lax.ppermute(other, "core", swap),
    )
    got = lax.all_to_all(half, "z", 0, 0)

    sent, c_vec = call(
        lambda *refs: row_kernel(model_width, rows, f_sum, *refs),
        [shape((n_z, row_rows, LANES)), shape((16, LANES), F32)],
        [scratch(sum_rows, LANES), scratch(row_rows, LANES)],
        got,
        qk_gain,
    )
    mine = lax.all_to_all(sent, "z", 0, 0)
    theirs = lax.ppermute(mine, "core", swap)

    sent, d_qk_gain, attended, hidden, d_qkv, d_up, normed, stats = call(
        lambda *refs: attention_kernel(rows, *refs),
        [
            shape((n_col, col_rows, LANES)),
            shape((2, LANES), F32),
            shape((tokens, LANES)),
            shape((tokens, hidden_w)),
            shape((tokens, 3 * LANES)),
            shape((tokens, hidden_w)),
            shape((tokens, width)),
            shape((2, width), F32),
        ],
        [
            scratch(2, tokens // 2, in_w + out_w),
            scratch(2, tokens // 2, LANES),
            scratch(n_col, col_rows, LANES),
        ],
        mine,
        theirs,
        c_vec,
        x_all,
        gain_row,
        qk_gain,
        w_qkv2,
        w_up,
        w_attn_out,
        w_down,
    )
    got = lax.all_to_all(sent, COL, 0, 0)
    d_w_attn_out = dot(attended, cot_all, TN).astype(BF16)
    d_w_down = dot(hidden, cot_all, TN).astype(BF16)
    d_w_qkv = dot(normed, d_qkv, TN).astype(BF16).reshape(w_qkv.shape)
    d_w_up = dot(normed, d_up, TN).astype(BF16)
    layer_out, token_grad, d_gain, d_qk_gain = call(
        lambda *refs: finish_kernel(model_width, *refs),
        [
            shape((rows_c, width)),
            shape((rows_c, width)),
            shape((1, width), F32),
            shape((2, LANES), F32),
        ],
        [scratch(col_rows, LANES)],
        got,
        stats,
        tokens_in,
        cotangent,
        gain_row,
        d_qk_gain,
    )
    return (
        layer_out,
        token_grad,
        d_gain.reshape(width),
        d_w_qkv,
        d_qk_gain,
        d_w_up,
        d_w_attn_out,
        d_w_down,
    )


def solution(mesh):
    fine = Mesh(mesh.devices.reshape(-1, 2, 4, 8), ("z", "core", "x", "y"))
    in_specs = (
        P(COL, ROW),
        P(ROW),
        P(ROW, None, COL),
        P(None, COL),
        P(ROW, COL),
        P(COL, ROW),
        P(COL, ROW),
        P(COL, ROW),
    )
    out_specs = (
        P(COL, ROW),
        P(COL, ROW),
        P(ROW),
        P(ROW, None, COL),
        P(None, COL),
        P(ROW, COL),
        P(COL, ROW),
        P(COL, ROW),
    )
    return jax.shard_map(shards, mesh=fine, in_specs=in_specs, out_specs=out_specs, check_vma=False)
```

time: 130 us -> 123 us (0.946)
  blocking collectives: 57.1 us -> 53.8 us
  waiting for transfers between devices: 37.2 us -> 34.4 us
  local copies, waits for them, and re-layouts: 3.56 us -> 1.38 us
    all_to_all x2, waiting for transfers between devices: 33 us -> 30.2 us  [shards(): got = lax.all_to_all(sent, COL, 0, 0)]
    unnamed x26 -> x18, local copies, waits for them, and re-layouts: 3.34 us -> 1.16 us
    all_to_all x1, blocking collectives: 33.5 us -> 31.6 us  [shards(): got = lax.all_to_all(half, 'z', 0, 0)]
    pallas_call x0 -> x1, Pallas kernels: none -> 1.63 us  [shards(): pl.pallas_call(spread_kernel, out_shape=[shape((n_col, col_rows, LANES))]...]
    all_to_all x1, blocking collectives: 23.6 us -> 22.3 us  [shards(): mine = lax.all_to_all(sent, 'z', 0, 0)]
    pallas_call x6 -> x5, Pallas kernels: 7.28 us -> 6.64 us  [call(): pl.pallas_call(kernel, out_shape=outs, in_specs=[pl.BlockSpec(memory_spac...]
where the time goes in v3:
time: 123 us; the launch traced here: 122 us
  blocking collectives  53.8 us (44%)
  waiting for transfers between devices  34.4 us (28%)
  starting transfers between devices  19 us (15%)
  Pallas kernels  8.27 us (7%)
  matrix products  3.99 us (3%)
  local copies, waits for them, and re-layouts  1.38 us (1%)
    all_to_all x1, blocking collectives, shards(): got = lax.all_to_all(half, 'z', 0, 0)  31.6 us
    all_to_all x2, waiting for transfers between devices, shards(): got = lax.all_to_all(sent, COL, 0, 0)  30.2 us
    all_to_all x1, blocking collectives, shards(): mine = lax.all_to_all(sent, 'z', 0, 0)  22.3 us
    all_to_all x2, starting transfers between devices, shards(): got = lax.all_to_all(sent, COL, 0, 0)  15.2 us
    pallas_call x5, Pallas kernels, call(): pl.pallas_call(kernel, out_shape=outs, in_specs=[pl.BlockSpec(memory_spac...  6.64 us
    dot_general x4, matrix products, dot(): return lax.dot_general(a, b, dims, preferred_element_type=F32)  3.99 us
  transfers between devices with their start and end apart: 4, of which 4 were waited for; matrix products, arithmetic and copies ran while one was open for 4% of the time, Pallas kernels for 0%

profile of v3, /device:TPU:8, one launch (start us, length us, event | category | flops | bytes accessed | tf_op | source)
XLA Modules:
  0.0 122.2 jit_solution(8788154746492247899)
XLA Ops:
  0.6 0.0 copy-start.7
  0.6 0.0 copy-start.6
  0.7 1.6 %shard_map.143 = bf16[32,64,128]{2,1,0:T(8,128)(2,1)} custom-call(bf16[10,384]{1,0:T(8,128)(2,1)} %refs_2_.1, bf16[10,384]{1,0:T(8,128)(2,1)} %refs_3_.1), custom_call_target="tpu_custom_call" | custom-call | tf_op jit(solution)/shard_map/pallas_call | solution.py:373
  2.3 0.0 copy-start
  2.3 0.0 copy-start.1
  2.3 0.0 copy-start.2
  2.3 10.3 %all-to-all-start = ((bf16[32,64,128]{2,1,0:T(8,128)(2,1)}), bf16[32,64,128]{2,1,0:T(8,128)(2,1)S(1)}, u32[]{:S(2)}, u32[]{:S(2)}) async-start(bf16[32,64,128]{2,1,0:T(8,128)(2,1)} %shard_map.143), calls=%async_computation | async-start | bytes 1048576 | tf_op jit(solution)/shard_map/all_to_all | solution.py:385
  12.6 0.0 copy-done.7
  12.7 0.0 copy-done.6
  12.7 0.2 copy.18
  12.9 0.2 copy.19.wq_ref.refs_6_
  13.1 17.1 %all-to-all-done.got_ref = bf16[32,64,128]{2,1,0:T(8,128)(2,1)S(1)} async-done(((bf16[32,64,128]{2,1,0:T(8,128)(2,1)}), bf16[32,64,128]{2,1,0:T(8,128)(2,1)S(1)}, u32[]{:S(2)}, u32[]{:S(2)}) %all-to-all-start) | async-done | bytes 524320 | tf_op jit(solution)/shard_map/all_to_all | solution.py:385
  30.3 0.0 copy-done
  30.3 0.0 copy-done.1
  30.3 0.0 copy-done.2
  30.3 1.5 %shard_map.144 = (f32[8,336,128]{2,1,0:T(8,128)S(1)}, bf16[8,336,128]{2,1,0:T(8,128)(2,1)S(1)}, bf16[320,384]{1,0:T(8,128)(2,1)S(1)}, bf16[320,384]{1,0:T(8,128)(2,1)S(1)}) custom-call(bf16[32,64,128]{2,1,0:T(8,128)(2,1)S(1)} %all-to-all-done.got_ref, f32[1,384]{1,0:T(1,128)S(1)} %reshape.28.gain_ref.refs_4_, bf16[384,384]{1,0:T(8,128)(2,1)S(1)} %copy.19.wq_ref.refs_6_, ...), custom_call_target="tpu_custom_call" | custom-call | tf_op jit(solution)/shard_map/pallas_call | solution.py:65
  31.8 1.9 %collective-permute-start = (bf16[8,336,128]{2,1,0:T(8,128)(2,1)S(1)}, bf16[8,336,128]{2,1,0:T(8,128)(2,1)S(1)}, u32[]{:S(2)}, u32[]{:S(2)}) collective-permute-start(bf16[8,336,128]{2,1,0:T(8,128)(2,1)S(1)} %get-tuple-element.27), channel_id=1, source_target_pairs={{0,32},{32,0},{1,33},{33,1},{2,34},{34,2},{3,35},{35,3},{4,36},{36... | collective-permute-start | bytes 2064392 | tf_op jit(solution)/shard_map/ppermute | solution.py:415
  33.7 2.1 %collective-permute-done.refs_1_ = bf16[8,336,128]{2,1,0:T(8,128)(2,1)S(1)} collective-permute-done((bf16[8,336,128]{2,1,0:T(8,128)(2,1)S(1)}, bf16[8,336,128]{2,1,0:T(8,128)(2,1)S(1)}, u32[]{:S(2)}, u32[]{:S(2)}) %collective-permute-start) | collective-permute-done | bytes 688160 | tf_op jit(solution)/shard_map/ppermute | solution.py:415
  35.9 0.2 shard_map.145
  36.1 0.0 copy-start.5
  36.1 31.6 %all_to_all.20.refs_0_ = bf16[8,336,128]{2,1,0:T(8,128)(2,1)S(1)} all-to-all(bf16[8,336,128]{2,1,0:T(8,128)(2,1)S(1)} %shard_map.145), channel_id=1, replica_groups=mesh['z'=8,'core'=2,'x'=4,'y'=8] {'z'}, dimensions={0} | all-to-all | bytes 1376256 | tf_op jit(solution)/shard_map/all_to_all | solution.py:417
  67.7 0.0 copy-done.5
  67.7 0.3 shard_map.146
  68.0 22.3 %all_to_all.21.refs_0_ = bf16[8,328,128]{2,1,0:T(8,128)(2,1)S(1)} all-to-all(bf16[8,328,128]{2,1,0:T(8,128)(2,1)S(1)} %get-tuple-element.28), channel_id=1, replica_groups=mesh['z'=8,'core'=2,'x'=4,'y'=8] {'z'}, dimensions={0} | all-to-all | bytes 1343488 | tf_op jit(solution)/shard_map/all_to_all | solution.py:426
  90.2 1.9 %collective-permute-start.1 = (bf16[8,328,128]{2,1,0:T(8,128)(2,1)S(1)}, bf16[8,328,128]{2,1,0:T(8,128)(2,1)S(1)}, u32[]{:S(2)}, u32[]{:S(2)}) collective-permute-start(bf16[8,328,128]{2,1,0:T(8,128)(2,1)S(1)} %all_to_all.21.refs_0_), channel_id=1, source_target_pairs={{0,32},{32,0},{1,33},{33,1},{2,34},{34,2},{3,35},{35,3},{4,36},{36... | collective-permute-start | bytes 2015240 | tf_op jit(solution)/shard_map/ppermute | solution.py:427
  92.2 2.1 %collective-permute-done.1.refs_1_ = bf16[8,328,128]{2,1,0:T(8,128)(2,1)S(1)} collective-permute-done((bf16[8,328,128]{2,1,0:T(8,128)(2,1)S(1)}, bf16[8,328,128]{2,1,0:T(8,128)(2,1)S(1)}, u32[]{:S(2)}, u32[]{:S(2)}) %collective-permute-start.1) | collective-permute-done | bytes 671776 | tf_op jit(solution)/shard_map/ppermute | solution.py:427
  94.3 3.8 %shard_map.147 = (bf16[32,64,128]{2,1,0:T(8,128)(2,1)}, f32[2,128]{1,0:T(2,128)S(1)}, bf16[320,128]{1,0:T(8,128)(2,1)S(1)}, bf16[320,768]{1,0:T(8,128)(2,1)S(1)}...) custom-call(bf16[8,328,128]{2,1,0:T(8,128)(2,1)S(1)} %all_to_all.21., ...), custom_call_target="tpu_custom_call" | custom-call | tf_op jit(solution)/shard_map/pallas_call | solution.py:65
  98.0 4.9 %all-to-all-start.3 = ((bf16[32,64,128]{2,1,0:T(8,128)(2,1)}), bf16[32,64,128]{2,1,0:T(8,128)(2,1)S(1)}, u32[]{:S(2)}, u32[]{:S(2)}) async-start(bf16[32,64,128]{2,1,0:T(8,128)(2,1)} %get-tuple-element.31), calls=%async_computation.3 | async-start | bytes 1048576 | tf_op jit(solution)/shard_map/all_to_all | solution.py:457
  102.9 0.4 convolution_convert_fusion.2
  103.3 0.9 copy.21
  104.2 0.9 convolution_convert_fusion.3
  105.1 0.0 copy-start.3
  105.1 0.0 copy-start.4
  105.1 1.4 %convolution_convert_fusion = bf16[768,384]{1,0:T(8,128)(2,1)} fusion(bf16[320,768]{1,0:T(8,128)(2,1)S(1)} %get-tuple-element.43, bf16[320,384]{1,0:T(8,128)(2,1)S(1)} %get-tuple-element.42), kind=kOutput, calls=%fused_computation | convolution fusion | flops 189038592 | bytes 1327104 | tf_op jit(solution)/shard_map/dot_general | solution.py:22
  106.5 1.3 %convolution_convert_fusion.1 = bf16[384,768]{1,0:T(8,128)(2,1)} fusion(bf16[320,384]{1,0:T(8,128)(2,1)S(1)} %get-tuple-element.37, bf16[320,768]{1,0:T(8,128)(2,1)S(1)} %get-tuple-element.40), kind=kOutput, calls=%fused_computation.1 | convolution fusion | flops 189038592 | bytes 1327104 | tf_op jit(solution)/shard_map/dot_general | solution.py:22
  107.8 13.1 %all-to-all-done.3.refs_0_ = bf16[32,64,128]{2,1,0:T(8,128)(2,1)S(1)} async-done(((bf16[32,64,128]{2,1,0:T(8,128)(2,1)}), bf16[32,64,128]{2,1,0:T(8,128)(2,1)S(1)}, u32[]{:S(2)}, u32[]{:S(2)}) %all-to-all-start.3) | async-done | bytes 524320 | tf_op jit(solution)/shard_map/all_to_all | solution.py:457
  120.9 0.0 copy-done.3
  120.9 0.0 copy-done.4
  120.9 0.7 shard_map.148
  121.6 0.6 reduce
  (1 shorter events, 0.0 us)
Async XLA Ops:
  0.6 12.0 %copy-start.7 = (f32[384]{0:T(512)S(1)}, f32[384]{0:T(512)}, u32[]{:S(2)}) copy-start(f32[384]{0:T(512)} %param.9) | copy-start | bytes 4612
  0.6 12.0 %copy-start.6 = (bf16[384,3,128]{2,0,1:T(8,128)(2,1)S(1)}, bf16[384,3,128]{2,0,1:T(8,128)(2,1)}, u32[]{:S(2)}) copy-start(bf16[384,3,128]{2,0,1:T(8,128)(2,1)} %param.10) | copy-start | bytes 884740
  2.3 28.0 %copy-start = (bf16[384,768]{1,0:T(8,128)(2,1)S(1)}, bf16[384,768]{1,0:T(8,128)(2,1)}, u32[]{:S(2)}) copy-start(bf16[384,768]{1,0:T(8,128)(2,1)} %refs_7_.1) | copy-start | bytes 1769476
  2.3 28.0 %copy-start.1 = (bf16[768,384]{1,0:T(8,128)(2,1)S(1)}, bf16[768,384]{1,0:T(8,128)(2,1)}, u32[]{:S(2)}) copy-start(bf16[768,384]{1,0:T(8,128)(2,1)} %refs_9_.1) | copy-start | bytes 1769476
  2.3 28.0 %copy-start.2 = (bf16[128,384]{1,0:T(8,128)(2,1)S(1)}, bf16[128,384]{1,0:T(8,128)(2,1)}, u32[]{:S(2)}) copy-start(bf16[128,384]{1,0:T(8,128)(2,1)} %refs_8_.1) | copy-start | bytes 294916
  2.3 27.9 %all-to-all-start = ((bf16[32,64,128]{2,1,0:T(8,128)(2,1)}), bf16[32,64,128]{2,1,0:T(8,128)(2,1)S(1)}, u32[]{:S(2)}, u32[]{:S(2)}) async-start(bf16[32,64,128]{2,1,0:T(8,128)(2,1)} %shard_map.143), calls=%async_computation | async-start | bytes 1048576 | tf_op jit(solution)/shard_map/all_to_all | solution.py:385
  31.8 4.0 %collective-permute-start = (bf16[8,336,128]{2,1,0:T(8,128)(2,1)S(1)}, bf16[8,336,128]{2,1,0:T(8,128)(2,1)S(1)}, u32[]{:S(2)}, u32[]{:S(2)}) collective-permute-start(bf16[8,336,128]{2,1,0:T(8,128)(2,1)S(1)} %get-tuple-element.27), channel_id=1, source_target_pairs={{0,32},{32,0},{1,33},{33,1},{2,34},{34,2},{3,35},{35,3},{4,36},{36... | collective-permute-start | bytes 2064392 | tf_op jit(solution)/shard_map/ppermute | solution.py:415
  36.1 31.6 %copy-start.5 = (f32[2,128]{1,0:T(2,128)S(1)}, f32[2,128]{1,0:T(2,128)}, u32[]{:S(2)}) copy-start(f32[2,128]{1,0:T(2,128)} %refs_5_.1) | copy-start | bytes 3076
  90.2 4.0 %collective-permute-start.1 = (bf16[8,328,128]{2,1,0:T(8,128)(2,1)S(1)}, bf16[8,328,128]{2,1,0:T(8,128)(2,1)S(1)}, u32[]{:S(2)}, u32[]{:S(2)}) collective-permute-start(bf16[8,328,128]{2,1,0:T(8,128)(2,1)S(1)} %all_to_all.21.refs_0_), channel_id=1, source_target_pairs={{0,32},{32,0},{1,33},{33,1},{2,34},{34,2},{3,35},{35,3},{4,36},{36... | collective-permute-start | bytes 2015240 | tf_op jit(solution)/shard_map/ppermute | solution.py:427
  98.0 22.8 %all-to-all-start.3 = ((bf16[32,64,128]{2,1,0:T(8,128)(2,1)}), bf16[32,64,128]{2,1,0:T(8,128)(2,1)S(1)}, u32[]{:S(2)}, u32[]{:S(2)}) async-start(bf16[32,64,128]{2,1,0:T(8,128)(2,1)} %get-tuple-element.31), calls=%async_computation.3 | async-start | bytes 1048576 | tf_op jit(solution)/shard_map/all_to_all | solution.py:457
  105.1 15.8 %copy-start.3 = (bf16[10,384]{1,0:T(8,128)(2,1)S(1)}, bf16[10,384]{1,0:T(8,128)(2,1)}, u32[]{:S(2)}) copy-start(bf16[10,384]{1,0:T(8,128)(2,1)} %refs_2_.1) | copy-start | bytes 23044
  105.1 15.8 %copy-start.4 = (bf16[10,384]{1,0:T(8,128)(2,1)S(1)}, bf16[10,384]{1,0:T(8,128)(2,1)}, u32[]{:S(2)}) copy-start(bf16[10,384]{1,0:T(8,128)(2,1)} %refs_3_.1) | copy-start | bytes 23044

commit v4 on v3

--- a/solution.py
+++ b/solution.py
@@ -68,7 +68,7 @@
         in_specs=[pl.BlockSpec(memory_space=pltpu.VMEM)] * len(args),
         out_specs=[pl.BlockSpec(memory_space=pltpu.VMEM)] * len(outs),
         scratch_shapes=scratch,
-        compiler_params=pltpu.CompilerParams(vmem_limit_bytes=40 * 2**20),
+        compiler_params=pltpu.CompilerParams(vmem_limit_bytes=16 * 2**20),
     )(*args)
 
 
@@ -76,10 +76,10 @@
     return jax.ShapeDtypeStruct(dims, dtype)
 
 
-def spread_kernel(x_any, cot_any, out_ref, x_ref, cot_ref, block, sems):
+def spread_kernel(x_hbm, cot_hbm, out_ref, x_ref, cot_ref, block, sems):
     copies = [
-        pltpu.make_async_copy(x_any, x_ref, sems.at[0]),
-        pltpu.make_async_copy(cot_any, cot_ref, sems.at[1]),
+        pltpu.make_async_copy(x_hbm, x_ref, sems.at[0]),
+        pltpu.make_async_copy(cot_hbm, cot_ref, sems.at[1]),
     ]
     for copy in copies:
         copy.start()
@@ -95,60 +95,98 @@
     out_ref[...] = jnp.broadcast_to(block[...].astype(BF16)[None], out_ref.shape)
 
 
-def product_kernel(
-    got_ref, gain_ref, wq_ref, wu_ref, wa_ref, wd_ref,
-    own_ref, other_ref, x_ref, cot_ref, xs, cs, ps, gs, st, lay
+def gather_kernel(got_ref, x_ref, cot_ref, xs, cs):
+    n_col, width = got_ref.shape[0], x_ref.shape[1]
+    rows = x_ref.shape[0] // n_col
+    tiles = width // LANES
+    for c in range(n_col):
+        values = got_ref[c].astype(F32)
+        here = slice(c * rows, (c + 1) * rows)
+        for j in range(tiles):
+            xs[here, tile(j)] = values[j * rows : (j + 1) * rows]
+            cs[here, tile(j)] = values[(tiles + j) * rows : (tiles + j + 1) * rows]
+    x_ref[...] = xs[...].astype(BF16)
+    cot_ref[...] = cs[...].astype(BF16)
+
+
+def products(
+    which, rows, x_ref, cot_ref, gain_ref, wq_ref, wu_ref, wa_ref, wd_ref, out_ref, ps, fs, gs, st, lay
 ):
-    tokens, width = x_ref.shape
-    n_z = own_ref.shape[0]
-    rows_c = tokens // got_ref.shape[0]
-    rows = tokens // (2 * n_z)
+    width = x_ref.shape[1]
+    n_z = out_ref.shape[0]
+    half = n_z * rows
+    mine = pl.ds(pl.multiple_of(which * half, 16), half)
+    x = x_ref[mine, :].astype(F32)
+    cot = cot_ref[mine, :]
     f_tiles, b_tiles = ps.shape[1] // LANES, gs.shape[1] // LANES
     f_sum = f_tiles * (rows + 1) + 3
-    w_tiles = width // LANES
-    for c in range(got_ref.shape[0]):
-        values = got_ref[c].astype(F32)
-        here = slice(c * rows_c, (c + 1) * rows_c)
-        for j in range(w_tiles):
-            xs[here, tile(j)] = values[j * rows_c : (j + 1) * rows_c]
-            cs[here, tile(j)] = values[(w_tiles + j) * rows_c : (w_tiles + j + 1) * rows_c]
-    x = xs[0:tokens, :]
-    x_ref[...] = x.astype(BF16)
-    cot = cs[...].astype(BF16)
-    cot_ref[...] = cot
-    gain = gain_ref[...]
-    xs[tokens:, :] = jnp.concatenate(split(gain, 3) + [jnp.zeros((5, width), F32)], 0)
-    xg = jnp.concatenate([x * gain, xs[tokens:, :]], 0).astype(BF16)
-    ps[:, 0 : wq_ref.shape[1]] = dot(xg, wq_ref[...], NN)
-    ps[:, wq_ref.shape[1] :] = dot(xg, wu_ref[...], NN)
+    gain = gain_ref[...].reshape(1, width)
+    gains = jnp.concatenate(split(gain, 3) + [jnp.zeros((5, width), F32)], 0)
+    scaled = jnp.concatenate([x * gain, gains], 0)
+    xg = scaled.astype(BF16)
+    xg_low = (scaled - xg.astype(F32)).astype(BF16)
+    fine = []
+    for j in range(2):
+        p = dot(xg, wq_ref[j], NN) + dot(xg_low, wq_ref[j], NN)
+        ps[:, tile(j)] = p.astype(BF16).astype(F32)
+        fs[:, tile(j)] = p - ps[:, tile(j)]
+        fine.append(jnp.sum(p[half:], 0, keepdims=True))
+    ps[:, tile(2)] = dot(xg, wq_ref[2], NN)
+    ps[:, 3 * LANES :] = dot(xg, wu_ref[...], NN)
     gs[:, 0 : wa_ref.shape[0]] = dot(cot, wa_ref[...], NT)
     gs[:, wa_ref.shape[0] :] = dot(cot, wd_ref[...], NT)
-    c_vec = jnp.sum(ps[tokens:, :], 0, keepdims=True)
+    c_vec = jnp.sum(ps[half:, :], 0, keepdims=True)
     s_1 = jnp.sum(x, 1, keepdims=True)
     s_2 = jnp.sum(x * x, 1, keepdims=True)
-    lane = lax.broadcasted_iota(jnp.int32, (tokens, LANES), 1)
-    place = lax.rem(lax.broadcasted_iota(jnp.int32, (tokens, LANES), 0), rows)
+    lane = lax.broadcasted_iota(jnp.int32, (half, LANES), 1)
+    place = lax.rem(lax.broadcasted_iota(jnp.int32, (half, LANES), 0), rows)
     st[...] = jnp.where(lane == place, s_1, 0.0) + jnp.where(lane == place + 32, s_2, 0.0)
-    c_rows = jnp.concatenate([c_vec[:, tile(j)] for j in range(f_tiles)], 0)
-    fill = jnp.zeros((lay.shape[2] - f_sum - b_tiles * rows, LANES), F32)
-    for h in range(2):
-        for d in range(n_z):
-            at = slice((h * n_z + d) * rows, (h * n_z + d + 1) * rows)
-            for j in range(f_tiles):
-                lay[h, d, j * rows : (j + 1) * rows, :] = ps[at, tile(j)]
-            stat = jnp.sum(st[at, :], 0, keepdims=True)
-            lay[h, d, f_tiles * rows : f_sum, :] = jnp.concatenate([c_rows] + split(stat, 3), 0)
-            for j in range(b_tiles):
-                lay[h, d, f_sum + j * rows : f_sum + (j + 1) * rows, :] = gs[at, tile(j)]
-            lay[h, d, f_sum + b_tiles * rows :, :] = fill
+    c_rows = jnp.concatenate(fine + [c_vec[:, tile(j)] for j in range(2, f_tiles)], 0)
+    c_rows, c_low = split(c_rows, 2)
+    low_at = f_sum + b_tiles * rows
+    fill = jnp.zeros((lay.shape[1] - low_at - 2 * rows - f_tiles, LANES), F32)
+    c_low = jnp.concatenate([c_low, fill], 0)
+    for d in range(n_z):
+        at = slice(d * rows, (d + 1) * rows)
+        for j in range(f_tiles):
+            lay[d, j * rows : (j + 1) * rows, :] = ps[at, tile(j)]
+        stat = jnp.sum(st[at, :], 0, keepdims=True)
+        lay[d, f_tiles * rows : f_sum, :] = jnp.concatenate([c_rows] + split(stat, 3), 0)
+        for j in range(b_tiles):
+            lay[d, f_sum + j * rows : f_sum + (j + 1) * rows, :] = gs[at, tile(j)]
+        for j in range(2):
+            lay[d, low_at + j * rows : low_at + (j + 1) * rows, :] = fs[at, tile(j)]
+        lay[d, low_at + 2 * rows :, :] = c_low
+    out_ref[...] = lay[...].astype(out_ref.dtype)
+
+
+def other_kernel(rows, got_ref, gain_ref, wq_ref, wu_ref, wa_ref, wd_ref, out_ref, x_ref, cot_ref, xs, cs, *scr):
+    gather_kernel(got_ref, x_ref, cot_ref, xs, cs)
+    other = 1 - lax.axis_index("core")
+    products(other, rows, x_ref, cot_ref, gain_ref, wq_ref, wu_ref, wa_ref, wd_ref, out_ref, *scr)
+
+
+def own_kernel(rows, x_ref, cot_ref, gain_ref, wq_ref, wu_ref, wa_ref, wd_ref, out_ref, *scr):
     core = lax.axis_index("core")
-    own_ref[...] = lay[core]
-    other_ref[...] = lay[1 - core].astype(BF16)
-
-
-def add_kernel(f_sum, own_ref, came_ref, out_ref, block):
+    products(core, rows, x_ref, cot_ref, gain_ref, wq_ref, wu_ref, wa_ref, wd_ref, out_ref, *scr)
+
+
+def fine_pairs(rows, f_sum, low_at):
+    tiles = f_sum // (rows + 1)
+    c_at, c_low_at = tiles * rows, low_at + 2 * rows
+    return (
+        (slice(0, 2 * rows), slice(low_at, low_at + 2 * rows)),
+        (slice(c_at, c_at + tiles), slice(c_low_at, c_low_at + tiles)),
+    )
+
+
+def add_kernel(rows, f_sum, low_at, own_ref, came_ref, out_ref, block):
     for d in range(own_ref.shape[0]):
         block[...] = own_ref[d] + came_ref[d].astype(F32)
+        for high, low in fine_pairs(rows, f_sum, low_at):
+            whole = block[high, :] + block[low, :]
+            block[high, :] = whole.astype(BF16).astype(F32)
+            block[low, :] = whole - block[high, :]
         stat = jnp.sum(block[f_sum - 3 : f_sum, :], 0, keepdims=True)
         block[f_sum - 3 : f_sum, :] = jnp.concatenate(split(stat, 3), 0)
         out_ref[d] = block[...].astype(BF16)
@@ -169,8 +207,12 @@
     tot[...] = total
 
 
-def row_kernel(model_width, rows, f_sum, got_ref, qk_gain_ref, out_ref, c_ref, tot, block):
+def row_kernel(
+    model_width, rows, f_sum, low_at, got_ref, qk_gain_ref, out_ref, c_ref, tot, block
+):
     sum_blocks(got_ref, tot)
+    for high, low in fine_pairs(rows, f_sum, low_at):
+        tot[high, :] = tot[high, :] + tot[low, :]
     tiles = (f_sum - 3) // (rows + 1)
     c_ref[0:tiles, :] = tot[tiles * rows : tiles * rows + tiles, :]
     c_ref[tiles:, :] = jnp.zeros((c_ref.shape[0] - tiles, LANES), F32)
@@ -292,7 +334,9 @@
     d_qkv_ref[:, tile(0)] = d_q
     d_qkv_ref[:, tile(1)] = d_k
     d_qkv_ref[:, tile(2)] = d_v
-    d_normed = dot(d_qkv_ref[...], wq_ref[...], NT) + dot(d_up_ref[...], wu_ref[...], NT)
+    d_normed = dot(d_up_ref[...], wu_ref[...], NT)
+    for j, d_j in enumerate((d_q, d_k, d_v)):
+        d_normed += dot(d_j, wq_ref[j], NT)
     both[0, :, width : 2 * width] = d_normed[0:half]
     both[1, :, width : 2 * width] = d_normed[half:]
     d_qf, d_kf, d_vf = d_q.astype(F32), d_k.astype(F32), d_v.astype(F32)
@@ -301,7 +345,7 @@
     t_2 = scalar(7)
     t_2 += jnp.sum(d_qf * query + d_kf * key + d_vf * v.astype(F32), 1, keepdims=True)
     xhat = (x_ref[...].astype(F32) - mean) * inv
-    normed_ref[...] = (xhat * gain_ref[...]).astype(BF16)
+    normed_ref[...] = (xhat * gain_ref[...].reshape(1, width)).astype(BF16)
     part = jnp.sum(d_normed * xhat, 0, keepdims=True)
     n_col = send_ref.shape[0]
     rows_c = tokens // n_col
@@ -328,6 +372,7 @@
     model_width, got_ref, stats_ref, x_ref, cot_ref, gain_ref, d_qk_ref,
     out_ref, grad_ref, d_gain_ref, d_qk_out, tot
 ):
+    gain = gain_ref[...].reshape(1, x_ref.shape[1])
     d_qk_out[...] = d_qk_ref[...]
     sum_blocks(got_ref, tot)
     rows, width = x_ref.shape
@@ -340,11 +385,11 @@
     hot = one_hot(rows, stats_ref.shape[1], col * rows)
     mean, inv = to_column(stats_ref[0:1], hot), to_column(stats_ref[1:2], hot)
     for j in range(tiles):
-        d_gain_ref[:, tile(j)] = tot[last + j : last + j + 1, :]
+        d_gain_ref[tile(j)] = tot[last + j, :]
         x = x_ref[:, tile(j)].astype(F32)
         out_ref[:, tile(j)] = (x + tot[j * rows : (j + 1) * rows, :]).astype(BF16)
         xhat = (x - mean) * inv
-        d_xhat = tot[(tiles + j) * rows : (tiles + j + 1) * rows, :] * gain_ref[:, tile(j)]
+        d_xhat = tot[(tiles + j) * rows : (tiles + j + 1) * rows, :] * gain[:, tile(j)]
         grad = (d_xhat - t_1 / model_width - xhat * t_2 / model_width) * inv
         grad_ref[:, tile(j)] = (cot_ref[:, tile(j)].astype(F32) + grad).astype(BF16)
 
@@ -358,12 +403,12 @@
     model_width = width * lax.axis_size(ROW)
     swap = [(0, 1), (1, 0)]
     hidden_w = w_up.shape[1]
-    gain_row = gain.reshape(1, width)
-    w_qkv2 = w_qkv.reshape(width, 3 * LANES)
+    w_qkv3 = jnp.transpose(w_qkv, (1, 0, 2))
     in_w, out_w = 3 * LANES + hidden_w, LANES + hidden_w
     tiles = (in_w + out_w) // LANES
     f_sum = in_w // LANES * (rows + 1) + 3
-    sum_rows = f_sum + -(-out_w // LANES * rows // 16) * 16
+    low_at = f_sum + out_w // LANES * rows
+    sum_rows = -(-(low_at + 2 * rows + in_w // LANES) // 16) * 16
     row_rows = tiles * rows + 8
     col_rows = 2 * width // LANES * rows_c + width // LANES + 1
 
@@ -373,7 +418,7 @@
     (sent,) = pl.pallas_call(
         spread_kernel,
         out_shape=[shape((n_col, col_rows, LANES))],
-        in_specs=[pl.BlockSpec(memory_space=pl.ANY)] * 2,
+        in_specs=[pl.BlockSpec(memory_space=pltpu.HBM)] * 2,
         out_specs=[pl.BlockSpec(memory_space=pltpu.VMEM)],
         scratch_shapes=[
             pltpu.VMEM((rows_c, width), BF16),
@@ -384,31 +429,31 @@
     )(tokens_in, cotangent)
     got = lax.all_to_all(sent, COL, 0, 0)
 
-    own, other, x_all, cot_all = call(
-        product_kernel,
-        [
-            shape((n_z, sum_rows, LANES), F32),
-            shape((n_z, sum_rows, LANES)),
-            shape((tokens, width)),
-            shape((tokens, width)),
-        ],
-        [
-            scratch(tokens + 8, width),
-            scratch(tokens, width),
-            scratch(tokens + 8, in_w),
-            scratch(tokens, out_w),
-            scratch(tokens, LANES),
-            scratch(2, n_z, sum_rows, LANES),
-        ],
+    weights = (gain, w_qkv3, w_up, w_attn_out, w_down)
+    work = [
+        scratch(tokens // 2 + 8, in_w),
+        scratch(tokens // 2 + 8, 2 * LANES),
+        scratch(tokens // 2, out_w),
+        scratch(tokens // 2, LANES),
+        scratch(n_z, sum_rows, LANES),
+    ]
+    other, x_all, cot_all = call(
+        lambda *refs: other_kernel(rows, *refs),
+        [shape((n_z, sum_rows, LANES)), shape((tokens, width)), shape((tokens, width))],
+        [scratch(tokens, width), scratch(tokens, width)] + work,
         got,
-        gain_row,
-        w_qkv2,
-        w_up,
-        w_attn_out,
-        w_down,
+        *weights,
+    )
+    (own,) = call(
+        lambda *refs: own_kernel(rows, *refs),
+        [shape((n_z, sum_rows, LANES), F32)],
+        work,
+        x_all,
+        cot_all,
+        *weights,
     )
     (half,) = call(
-        lambda *refs: add_kernel(f_sum, *refs),
+        lambda *refs: add_kernel(rows, f_sum, low_at, *refs),
         [shape((n_z, sum_rows, LANES))],
         [scratch(sum_rows, LANES)],
         own,
@@ -417,7 +462,7 @@
     got = lax.all_to_all(half, "z", 0, 0)
 
     sent, c_vec = call(
-        lambda *refs: row_kernel(model_width, rows, f_sum, *refs),
+        lambda *refs: row_kernel(model_width, rows, f_sum, low_at, *refs),
         [shape((n_z, row_rows, LANES)), shape((16, LANES), F32)],
         [scratch(sum_rows, LANES), scratch(row_rows, LANES)],
         got,
@@ -447,9 +492,9 @@
         theirs,
         c_vec,
         x_all,
-        gain_row,
+        gain,
         qk_gain,
-        w_qkv2,
+        w_qkv3,
         w_up,
         w_attn_out,
         w_down,
@@ -464,7 +509,7 @@
         [
             shape((rows_c, width)),
             shape((rows_c, width)),
-            shape((1, width), F32),
+            shape((width,), F32),
             shape((2, LANES), F32),
         ],
         [scratch(col_rows, LANES)],
@@ -472,13 +517,13 @@
         stats,
         tokens_in,
         cotangent,
-        gain_row,
+        gain,
         d_qk_gain,
     )
     return (
         layer_out,
         token_grad,
-        d_gain.reshape(width),
+        d_gain,
         d_w_qkv,
         d_qk_gain,
         d_w_up,

time: 123 us -> 124 us (level)
  blocking collectives: 53.8 us -> 83.6 us
  waiting for transfers between devices: 34.4 us -> 16.5 us
  starting transfers between devices: 19 us -> 8.7 us
    all_to_all x0 -> x1, blocking collectives: none -> 27.8 us  [shards(): got = lax.all_to_all(sent, COL, 0, 0)]
    all_to_all x2 -> x1, waiting for transfers between devices: 30.2 us -> 13 us  [shards(): got = lax.all_to_all(sent, COL, 0, 0)]
    all_to_all x2 -> x1, starting transfers between devices: 15.2 us -> 4.87 us  [shards(): got = lax.all_to_all(sent, COL, 0, 0)]
    all_to_all x1, blocking collectives: 31.6 us -> 33.5 us  [shards(): got = lax.all_to_all(half, 'z', 0, 0)]
    pallas_call x5 -> x6, Pallas kernels: 6.64 us -> 7.04 us  [call(): pl.pallas_call(kernel, out_shape=outs, in_specs=[pl.BlockSpec(memory_spac...]
  transfers between devices with their start and end apart: 4 -> 3, of which waited for: 4 -> 3; matrix products, arithmetic and copies ran while one was open for 4% -> 4% of each run, Pallas kernels for 0% -> 1%
where the time goes in v4:
time: 124 us; the launch traced here: 123 us
  blocking collectives  83.6 us (67%)
  waiting for transfers between devices  16.5 us (13%)
  Pallas kernels  8.74 us (7%)
  starting transfers between devices  8.7 us (7%)
  matrix products  3.99 us (3%)
    all_to_all x1, blocking collectives, shards(): got = lax.all_to_all(half, 'z', 0, 0)  33.5 us
    all_to_all x1, blocking collectives, shards(): got = lax.all_to_all(sent, COL, 0, 0)  27.8 us
    all_to_all x1, blocking collectives, shards(): mine = lax.all_to_all(sent, 'z', 0, 0)  22.3 us
    all_to_all x1, waiting for transfers between devices, shards(): got = lax.all_to_all(sent, COL, 0, 0)  13 us
    pallas_call x6, Pallas kernels, call(): pl.pallas_call(kernel, out_shape=outs, in_specs=[pl.BlockSpec(memory_spac...  7.04 us
    all_to_all x1, starting transfers between devices, shards(): got = lax.all_to_all(sent, COL, 0, 0)  4.87 us
    dot_general x4, matrix products, dot(): return lax.dot_general(a, b, dims, preferred_element_type=F32)  3.99 us
  transfers between devices with their start and end apart: 3, of which 3 were waited for; matrix products, arithmetic and copies ran while one was open for 4% of the time, Pallas kernels for 1%

profile of v4, /device:TPU:8, one launch (start us, length us, event | category | flops | bytes accessed | tf_op | source)
XLA Modules:
  0.0 123.2 jit_solution(5232284278446700759)
XLA Ops:
  0.6 0.0 copy-start.6
  0.6 0.0 copy-start.1
  0.7 0.0 copy-start.3
  0.7 0.0 copy-start
  0.7 0.0 copy-start.2
  0.7 1.7 %shard_map.143 = bf16[32,64,128]{2,1,0:T(8,128)(2,1)} custom-call(bf16[10,384]{1,0:T(8,128)(2,1)} %refs_2_.3, bf16[10,384]{1,0:T(8,128)(2,1)} %refs_3_.3), custom_call_target="tpu_custom_call" | custom-call | tf_op jit(solution)/shard_map/pallas_call | solution.py:418
  2.4 27.8 %all_to_all.20.refs_0_ = bf16[32,64,128]{2,1,0:T(8,128)(2,1)S(1)} all-to-all(bf16[32,64,128]{2,1,0:T(8,128)(2,1)} %shard_map.143), channel_id=1, replica_groups=mesh['z'=8,'core'=2,'x'=4,'y'=8] {'x','y'}, dimensions={0} | all-to-all | bytes 1048576 | tf_op jit(solution)/shard_map/all_to_all | solution.py:430
  30.2 0.0 copy-done.6
  30.2 0.0 copy-done.1
  30.2 0.0 copy-done.3
  30.2 0.0 copy-done
  30.2 0.0 copy-done.2
  30.2 1.0 shard_map.144
  31.3 1.9 %collective-permute-start = (bf16[8,384,128]{2,1,0:T(8,128)(2,1)S(1)}, bf16[8,384,128]{2,1,0:T(8,128)(2,1)S(1)}, u32[]{:S(2)}, u32[]{:S(2)}) collective-permute-start(bf16[8,384,128]{2,1,0:T(8,128)(2,1)S(1)} %get-tuple-element.27), channel_id=1, source_target_pairs={{0,32},{32,0},{1,33},{33,1},{2,34},{34,2},{3,35},{35,3},{4,36},{36... | collective-permute-start | bytes 2359304 | tf_op jit(solution)/shard_map/ppermute | solution.py:460
  33.2 0.9 shard_map.145.refs_0_
  34.1 1.4 %collective-permute-done.refs_1_ = bf16[8,384,128]{2,1,0:T(8,128)(2,1)S(1)} collective-permute-done((bf16[8,384,128]{2,1,0:T(8,128)(2,1)S(1)}, bf16[8,384,128]{2,1,0:T(8,128)(2,1)S(1)}, u32[]{:S(2)}, u32[]{:S(2)}) %collective-permute-start) | collective-permute-done | bytes 786464 | tf_op jit(solution)/shard_map/ppermute | solution.py:460
  35.4 0.3 shard_map.146
  35.7 0.0 copy-start.7
  35.7 33.5 %all_to_all.21.refs_0_ = bf16[8,384,128]{2,1,0:T(8,128)(2,1)S(1)} all-to-all(bf16[8,384,128]{2,1,0:T(8,128)(2,1)S(1)} %shard_map.146), channel_id=1, replica_groups=mesh['z'=8,'core'=2,'x'=4,'y'=8] {'z'}, dimensions={0} | all-to-all | bytes 1572864 | tf_op jit(solution)/shard_map/all_to_all | solution.py:462
  69.3 0.0 copy-done.7
  69.3 0.3 shard_map.147
  69.6 22.3 %all_to_all.22.refs_0_ = bf16[8,328,128]{2,1,0:T(8,128)(2,1)S(1)} all-to-all(bf16[8,328,128]{2,1,0:T(8,128)(2,1)S(1)} %get-tuple-element.28), channel_id=1, replica_groups=mesh['z'=8,'core'=2,'x'=4,'y'=8] {'z'}, dimensions={0} | all-to-all | bytes 1343488 | tf_op jit(solution)/shard_map/all_to_all | solution.py:471
  91.9 1.9 %collective-permute-start.1 = (bf16[8,328,128]{2,1,0:T(8,128)(2,1)S(1)}, bf16[8,328,128]{2,1,0:T(8,128)(2,1)S(1)}, u32[]{:S(2)}, u32[]{:S(2)}) collective-permute-start(bf16[8,328,128]{2,1,0:T(8,128)(2,1)S(1)} %all_to_all.22.refs_0_), channel_id=1, source_target_pairs={{0,32},{32,0},{1,33},{33,1},{2,34},{34,2},{3,35},{35,3},{4,36},{36... | collective-permute-start | bytes 2015240 | tf_op jit(solution)/shard_map/ppermute | solution.py:472
  93.8 2.1 %collective-permute-done.1.refs_1_ = bf16[8,328,128]{2,1,0:T(8,128)(2,1)S(1)} collective-permute-done((bf16[8,328,128]{2,1,0:T(8,128)(2,1)S(1)}, bf16[8,328,128]{2,1,0:T(8,128)(2,1)S(1)}, u32[]{:S(2)}, u32[]{:S(2)}) %collective-permute-start.1) | collective-permute-done | bytes 671776 | tf_op jit(solution)/shard_map/ppermute | solution.py:472
  95.9 3.8 %shard_map.148 = (bf16[32,64,128]{2,1,0:T(8,128)(2,1)}, f32[2,128]{1,0:T(2,128)S(1)}, bf16[320,128]{1,0:T(8,128)(2,1)S(1)}, bf16[320,768]{1,0:T(8,128)(2,1)S(1)}...) custom-call(bf16[8,328,128]{2,1,0:T(8,128)(2,1)S(1)} %all_to_all.22., ...), custom_call_target="tpu_custom_call" | custom-call | tf_op jit(solution)/shard_map/pallas_call | solution.py:65
  99.6 4.9 %all-to-all-start.3 = ((bf16[32,64,128]{2,1,0:T(8,128)(2,1)}), bf16[32,64,128]{2,1,0:T(8,128)(2,1)S(1)}, u32[]{:S(2)}, u32[]{:S(2)}) async-start(bf16[32,64,128]{2,1,0:T(8,128)(2,1)} %get-tuple-element.30), calls=%async_computation.3 | async-start | bytes 1048576 | tf_op jit(solution)/shard_map/all_to_all | solution.py:502
  104.5 0.4 convolution_convert_fusion.2
  104.9 0.9 copy.16
  105.8 0.9 convolution_convert_fusion.3
  106.7 0.0 copy-start.4
  106.7 0.0 copy-start.5
  106.7 1.4 %convolution_convert_fusion = bf16[768,384]{1,0:T(8,128)(2,1)} fusion(bf16[320,768]{1,0:T(8,128)(2,1)S(1)} %get-tuple-element.41, bf16[320,384]{1,0:T(8,128)(2,1)S(1)} %get-tuple-element.26.refs_1_), kind=kOutput, calls=%fused_computation | convolution fusion | flops 189038592 | bytes 1327104 | tf_op jit(solution)/shard_map/dot_general | solution.py:22
  108.1 1.3 %convolution_convert_fusion.1 = bf16[384,768]{1,0:T(8,128)(2,1)} fusion(bf16[320,384]{1,0:T(8,128)(2,1)S(1)} %get-tuple-element.36, bf16[320,768]{1,0:T(8,128)(2,1)S(1)} %get-tuple-element.39), kind=kOutput, calls=%fused_computation.1 | convolution fusion | flops 189038592 | bytes 1327104 | tf_op jit(solution)/shard_map/dot_general | solution.py:22
  109.4 13.0 %all-to-all-done.3.refs_0_ = bf16[32,64,128]{2,1,0:T(8,128)(2,1)S(1)} async-done(((bf16[32,64,128]{2,1,0:T(8,128)(2,1)}), bf16[32,64,128]{2,1,0:T(8,128)(2,1)S(1)}, u32[]{:S(2)}, u32[]{:S(2)}) %all-to-all-start.3) | async-done | bytes 524320 | tf_op jit(solution)/shard_map/all_to_all | solution.py:502
  122.4 0.0 copy-done.4
  122.4 0.0 copy-done.5
  122.4 0.7 shard_map.149
Async XLA Ops:
  0.6 29.6 %copy-start.6 = (f32[384]{0:T(512)S(1)}, f32[384]{0:T(512)}, u32[]{:S(2)}) copy-start(f32[384]{0:T(512)} %refs_4_.7) | copy-start | bytes 4612
  0.6 29.5 %copy-start.1 = (bf16[768,384]{1,0:T(8,128)(2,1)S(1)}, bf16[768,384]{1,0:T(8,128)(2,1)}, u32[]{:S(2)}) copy-start(bf16[768,384]{1,0:T(8,128)(2,1)} %refs_9_.1) | copy-start | bytes 1769476
  0.7 29.5 %copy-start.3 = (bf16[128,384]{1,0:T(8,128)(2,1)S(1)}, bf16[128,384]{1,0:T(8,128)(2,1)}, u32[]{:S(2)}) copy-start(bf16[128,384]{1,0:T(8,128)(2,1)} %refs_8_.1) | copy-start | bytes 294916
  0.7 29.5 %copy-start = (bf16[384,768]{1,0:T(8,128)(2,1)S(1)}, bf16[384,768]{1,0:T(8,128)(2,1)}, u32[]{:S(2)}) copy-start(bf16[384,768]{1,0:T(8,128)(2,1)} %refs_7_.1) | copy-start | bytes 1769476
  0.7 29.5 %copy-start.2 = (bf16[384,3,128]{2,0,1:T(8,128)(2,1)S(1)}, bf16[384,3,128]{2,0,1:T(8,128)(2,1)}, u32[]{:S(2)}) copy-start(bf16[384,3,128]{2,0,1:T(8,128)(2,1)} %param.10) | copy-start | bytes 884740
  31.3 4.2 %collective-permute-start = (bf16[8,384,128]{2,1,0:T(8,128)(2,1)S(1)}, bf16[8,384,128]{2,1,0:T(8,128)(2,1)S(1)}, u32[]{:S(2)}, u32[]{:S(2)}) collective-permute-start(bf16[8,384,128]{2,1,0:T(8,128)(2,1)S(1)} %get-tuple-element.27), channel_id=1, source_target_pairs={{0,32},{32,0},{1,33},{33,1},{2,34},{34,2},{3,35},{35,3},{4,36},{36... | collective-permute-start | bytes 2359304 | tf_op jit(solution)/shard_map/ppermute | solution.py:460
  35.7 33.5 %copy-start.7 = (f32[2,128]{1,0:T(2,128)S(1)}, f32[2,128]{1,0:T(2,128)}, u32[]{:S(2)}) copy-start(f32[2,128]{1,0:T(2,128)} %refs_5_.5) | copy-start | bytes 3076
  91.9 4.0 %collective-permute-start.1 = (bf16[8,328,128]{2,1,0:T(8,128)(2,1)S(1)}, bf16[8,328,128]{2,1,0:T(8,128)(2,1)S(1)}, u32[]{:S(2)}, u32[]{:S(2)}) collective-permute-start(bf16[8,328,128]{2,1,0:T(8,128)(2,1)S(1)} %all_to_all.22.refs_0_), channel_id=1, source_target_pairs={{0,32},{32,0},{1,33},{33,1},{2,34},{34,2},{3,35},{35,3},{4,36},{36... | collective-permute-start | bytes 2015240 | tf_op jit(solution)/shard_map/ppermute | solution.py:472
  99.6 22.8 %all-to-all-start.3 = ((bf16[32,64,128]{2,1,0:T(8,128)(2,1)}), bf16[32,64,128]{2,1,0:T(8,128)(2,1)S(1)}, u32[]{:S(2)}, u32[]{:S(2)}) async-start(bf16[32,64,128]{2,1,0:T(8,128)(2,1)} %get-tuple-element.30), calls=%async_computation.3 | async-start | bytes 1048576 | tf_op jit(solution)/shard_map/all_to_all | solution.py:502
  106.7 15.8 %copy-start.4 = (bf16[10,384]{1,0:T(8,128)(2,1)S(1)}, bf16[10,384]{1,0:T(8,128)(2,1)}, u32[]{:S(2)}) copy-start(bf16[10,384]{1,0:T(8,128)(2,1)} %refs_2_.3) | copy-start | bytes 23044
  106.7 15.8 %copy-start.5 = (bf16[10,384]{1,0:T(8,128)(2,1)S(1)}, bf16[10,384]{1,0:T(8,128)(2,1)}, u32[]{:S(2)}) copy-start(bf16[10,384]{1,0:T(8,128)(2,1)} %refs_3_.3) | copy-start | bytes 23044

commit v5 on v4

--- a/solution.py
+++ b/solution.py
@@ -260,36 +260,58 @@
     out_ref[...] = jnp.broadcast_to(block[...].astype(BF16)[None], out_ref.shape)
 
 
+def unpack(rows, ref, half, cols):
+    tiles = half.shape[-1] // LANES
+    lane = lax.broadcasted_iota(jnp.int32, (rows, LANES), 1)
+    for d in range(ref.shape[0]):
+        values = ref[d].astype(F32)
+        at = slice(d * rows, (d + 1) * rows)
+        for j in range(tiles):
+            half[at, tile(j)] = values[j * rows : (j + 1) * rows]
+        scalars = jnp.zeros((rows, LANES), F32)
+        for i in range(4):
+            a, b = two_to_columns(values[tiles * rows + i : tiles * rows + i + 1], rows)
+            scalars = jnp.where(lane == 2 * i, a, scalars)
+            scalars = jnp.where(lane == 2 * i + 1, b, scalars)
+        cols[at, :] = scalars
+
+
+def mlp_products(values, wd_ref, wu_ref, part_ref, at):
+    hidden_w, width = wd_ref.shape
+    f_width = 3 * LANES + hidden_w
+    part_ref[at, 0:width] = dot(values[:, 3 * LANES : f_width], wd_ref[...], NN)
+    part_ref[at, width:] = dot(values[:, f_width + LANES :], wu_ref[...], NT)
+
+
+def unpack_kernel(rows, mine_ref, wd_ref, wu_ref, out_ref, cols_ref, part_ref, half):
+    unpack(rows, mine_ref, half, cols_ref)
+    out_ref[...] = half[...].astype(BF16)
+    mlp_products(out_ref[...], wd_ref, wu_ref, part_ref, slice(None))
+
+
 def attention_kernel(
-    rows, mine_ref, theirs_ref, c_ref, x_ref, gain_ref, qk_gain_ref, wq_ref, wu_ref, wa_ref, wd_ref,
+    rows, half_ref, half_cols_ref, half_part_ref, theirs_ref, c_ref, x_ref, gain_ref, qk_gain_ref, wq_ref, wu_ref, wa_ref, wd_ref,
     send_ref, d_gain_ref, att_ref, hidden_ref, d_qkv_ref, d_up_ref, normed_ref, stats_ref,
-    both, cols, block
+    full, wide, block, cols, cols_ref, mlp
 ):
-    n_z = mine_ref.shape[0]
     tokens, width = x_ref.shape
     half = tokens // 2
     core = lax.axis_index("core")
-    tiles = both.shape[2] // LANES
     f_width = 3 * LANES + hidden_ref.shape[1]
-    lane = lax.broadcasted_iota(jnp.int32, (rows, LANES), 1)
-    for ref, h in ((mine_ref, core), (theirs_ref, 1 - core)):
-        for d in range(n_z):
-            values = ref[d].astype(F32)
-            at = slice(d * rows, (d + 1) * rows)
-            for j in range(tiles):
-                both[h, at, tile(j)] = values[j * rows : (j + 1) * rows]
-            scalars = jnp.zeros((rows, LANES), F32)
-            for i in range(4):
-                a, b = two_to_columns(values[tiles * rows + i : tiles * rows + i + 1], rows)
-                scalars = jnp.where(lane == 2 * i, a, scalars)
-                scalars = jnp.where(lane == 2 * i + 1, b, scalars)
-            cols[h, at, :] = scalars
+    unpack(rows, theirs_ref, wide, cols)
+    for h, values, scalars in ((core, half_ref, half_cols_ref), (1 - core, wide, cols)):
+        at = pl.ds(pl.multiple_of(h * half, 16), half)
+        full[at, :] = values[...].astype(BF16)
+        cols_ref[at, :] = scalars[...]
+    mlp[pl.ds(pl.multiple_of(core * half, 16), half), :] = half_part_ref[...]
+    other = pl.ds(pl.multiple_of((1 - core) * half, 16), half)
+    mlp_products(wide[...].astype(BF16), wd_ref, wu_ref, mlp, other)
 
     def whole(at, size):
-        return jnp.concatenate([both[h, :, at : at + size].astype(BF16) for h in range(2)], 0)
+        return full[:, at : at + size]
 
     def scalar(i):
-        return jnp.concatenate([cols[h, :, i : i + 1] for h in range(2)], 0)
+        return cols_ref[:, i : i + 1]
 
     hidden_ref[...] = whole(3 * LANES, hidden_ref.shape[1])
     d_up_ref[...] = whole(f_width + LANES, d_up_ref.shape[1])
@@ -306,9 +328,9 @@
     low = probs.astype(BF16)
     attended = dot(low, v, NN).astype(BF16)
     att_ref[...] = attended
-    branch = dot(attended, wa_ref[...], NN) + dot(hidden_ref[...], wd_ref[...], NN)
-    both[0, :, 0:width] = branch[0:half]
-    both[1, :, 0:width] = branch[half:]
+    branch = dot(attended, wa_ref[...], NN) + mlp[:, 0:width]
+    wide[:, 0:width] = branch[0:half]
+    wide[:, width : 2 * width] = branch[half:]
     d_probs = dot(d_att, v, NT)
     delta = jnp.sum(probs * d_probs, -1, keepdims=True)
     d_scores = (probs * (d_probs - delta)).astype(BF16)
@@ -334,11 +356,11 @@
     d_qkv_ref[:, tile(0)] = d_q
     d_qkv_ref[:, tile(1)] = d_k
     d_qkv_ref[:, tile(2)] = d_v
-    d_normed = dot(d_up_ref[...], wu_ref[...], NT)
+    d_normed = mlp[:, width:]
     for j, d_j in enumerate((d_q, d_k, d_v)):
         d_normed += dot(d_j, wq_ref[j], NT)
-    both[0, :, width : 2 * width] = d_normed[0:half]
-    both[1, :, width : 2 * width] = d_normed[half:]
+    wide[:, 2 * width : 3 * width] = d_normed[0:half]
+    wide[:, 3 * width : 4 * width] = d_normed[half:]
     d_qf, d_kf, d_vf = d_q.astype(F32), d_k.astype(F32), d_v.astype(F32)
     t_1 = scalar(6)
     t_1 += jnp.sum(d_qf * c_ref[0:1] + d_kf * c_ref[1:2] + d_vf * c_ref[2:3], 1, keepdims=True)
@@ -352,8 +374,7 @@
     lane = lax.broadcasted_iota(jnp.int32, (tokens, LANES), 1)
     place = lax.rem(lax.broadcasted_iota(jnp.int32, (tokens, LANES), 0), rows_c)
     ts = jnp.where(lane == place, t_1, 0.0) + jnp.where(lane == place + 32, t_2, 0.0)
-    cols[0] = ts[0:half]
-    cols[1] = ts[half:]
+    cols[...] = ts[0:half] + pltpu.roll(ts[half:], 64, 1)
 
     w_tiles = width // LANES
     used = 2 * w_tiles * rows_c
@@ -361,9 +382,11 @@
     for c in range(n_col):
         h, at = divmod(c * rows_c, half)
         at = slice(at, at + rows_c)
-        for j in range(2 * w_tiles):
-            block[c, j * rows_c : (j + 1) * rows_c, :] = both[h, at, tile(j)]
-        t_row = jnp.sum(cols[h, at, :], 0, keepdims=True)
+        for i in range(2):
+            for j in range(w_tiles):
+                to = (i * w_tiles + j) * rows_c
+                block[c, to : to + rows_c, :] = wide[at, tile((2 * i + h) * w_tiles + j)]
+        t_row = jnp.sum(cols[at, :], 0, keepdims=True)
         block[c, used : used + w_tiles + 1, :] = jnp.concatenate([part, t_row], 0)
     send_ref[...] = block[...].astype(BF16)
 
@@ -379,9 +402,10 @@
     tiles = width // LANES
     last = 2 * rows * tiles
     t_row = tot[last + tiles : last + tiles + 1, :]
-    t_1 = to_column(t_row, one_hot(rows, LANES, 0))
-    t_2 = to_column(t_row, one_hot(rows, LANES, 32))
     col = lax.axis_index("x") * lax.axis_size("y") + lax.axis_index("y")
+    upper = jnp.where(col * 2 >= lax.axis_size("x") * lax.axis_size("y"), 64, 0)
+    t_1 = to_column(t_row, one_hot(rows, LANES, upper))
+    t_2 = to_column(t_row, one_hot(rows, LANES, upper + 32))
     hot = one_hot(rows, stats_ref.shape[1], col * rows)
     mean, inv = to_column(stats_ref[0:1], hot), to_column(stats_ref[1:2], hot)
     for j in range(tiles):
@@ -470,6 +494,18 @@
     )
     mine = lax.all_to_all(sent, "z", 0, 0)
     theirs = lax.ppermute(mine, "core", swap)
+    half, half_cols, half_part = call(
+        lambda *refs: unpack_kernel(rows, *refs),
+        [
+            shape((tokens // 2, in_w + out_w)),
+            shape((tokens // 2, LANES), F32),
+            shape((tokens // 2, 2 * width), F32),
+        ],
+        [scratch(tokens // 2, in_w + out_w)],
+        mine,
+        w_down,
+        w_up,
+    )
 
     sent, d_qk_gain, attended, hidden, d_qkv, d_up, normed, stats = call(
         lambda *refs: attention_kernel(rows, *refs),
@@ -484,11 +520,16 @@
             shape((2, width), F32),
         ],
         [
-            scratch(2, tokens // 2, in_w + out_w),
-            scratch(2, tokens // 2, LANES),
+            pltpu.VMEM((tokens, in_w + out_w), BF16),
+            scratch(tokens // 2, in_w + out_w),
             scratch(n_col, col_rows, LANES),
+            scratch(tokens // 2, LANES),
+            scratch(tokens, LANES),
+            scratch(tokens, 2 * width),
         ],
-        mine,
+        half,
+        half_cols,
+        half_part,
         theirs,
         c_vec,
         x_all,

time: 124 us -> 123 us (level)
    pallas_call x6 -> x7, Pallas kernels: 7.04 us -> 7.09 us  [call(): pl.pallas_call(kernel, out_shape=outs, in_specs=[pl.BlockSpec(memory_spac...]
where the time goes in v5:
time: 123 us
  blocking collectives  83.6 us (68%)
  waiting for transfers between devices  16 us (13%)
  Pallas kernels  8.79 us (7%)
  starting transfers between devices  8.69 us (7%)
  matrix products  3.98 us (3%)
    all_to_all x1, blocking collectives, shards(): got = lax.all_to_all(half, 'z', 0, 0)  33.5 us
    all_to_all x1, blocking collectives, shards(): got = lax.all_to_all(sent, COL, 0, 0)  27.8 us
    all_to_all x1, blocking collectives, shards(): mine = lax.all_to_all(sent, 'z', 0, 0)  22.3 us
    all_to_all x1, waiting for transfers between devices, shards(): got = lax.all_to_all(sent, COL, 0, 0)  13.1 us
    pallas_call x7, Pallas kernels, call(): pl.pallas_call(kernel, out_shape=outs, in_specs=[pl.BlockSpec(memory_spac...  7.09 us
    all_to_all x1, starting transfers between devices, shards(): got = lax.all_to_all(sent, COL, 0, 0)  4.86 us
    dot_general x4, matrix products, dot(): return lax.dot_general(a, b, dims, preferred_element_type=F32)  3.98 us
  transfers between devices with their start and end apart: 3, of which 3 were waited for; matrix products, arithmetic and copies ran while one was open for 4% of the time, Pallas kernels for 1%

profile of v5, /device:TPU:8, one launch (start us, length us, event | category | flops | bytes accessed | tf_op | source)
XLA Modules:
  0.0 122.7 jit_solution(3846484951614985290)
XLA Ops:
  0.6 0.0 copy-start.1
  0.6 0.0 copy-start
  0.7 0.0 copy-start.6
  0.7 0.0 copy-start.3
  0.7 0.0 copy-start.2
  0.7 1.7 %shard_map.143 = bf16[32,64,128]{2,1,0:T(8,128)(2,1)} custom-call(bf16[10,384]{1,0:T(8,128)(2,1)} %refs_2_.5, bf16[10,384]{1,0:T(8,128)(2,1)} %refs_3_.3), custom_call_target="tpu_custom_call" | custom-call | tf_op jit(solution)/shard_map/pallas_call | solution.py:442
  2.4 27.8 %all_to_all.20.refs_0_ = bf16[32,64,128]{2,1,0:T(8,128)(2,1)S(1)} all-to-all(bf16[32,64,128]{2,1,0:T(8,128)(2,1)} %shard_map.143), channel_id=1, replica_groups=mesh['z'=8,'core'=2,'x'=4,'y'=8] {'x','y'}, dimensions={0} | all-to-all | bytes 1048576 | tf_op jit(solution)/shard_map/all_to_all | solution.py:454
  30.2 0.0 copy-done.1
  30.2 0.0 copy-done
  30.2 0.0 copy-done.6
  30.2 0.0 copy-done.3
  30.2 0.0 copy-done.2
  30.2 1.0 shard_map.144
  31.2 1.9 %collective-permute-start = (bf16[8,384,128]{2,1,0:T(8,128)(2,1)S(1)}, bf16[8,384,128]{2,1,0:T(8,128)(2,1)S(1)}, u32[]{:S(2)}, u32[]{:S(2)}) collective-permute-start(bf16[8,384,128]{2,1,0:T(8,128)(2,1)S(1)} %get-tuple-element.30), channel_id=1, source_target_pairs={{0,32},{32,0},{1,33},{33,1},{2,34},{34,2},{3,35},{35,3},{4,36},{36... | collective-permute-start | bytes 2359304 | tf_op jit(solution)/shard_map/ppermute | solution.py:484
  33.2 0.9 shard_map.145.refs_0_
  34.1 1.4 %collective-permute-done.refs_1_ = bf16[8,384,128]{2,1,0:T(8,128)(2,1)S(1)} collective-permute-done((bf16[8,384,128]{2,1,0:T(8,128)(2,1)S(1)}, bf16[8,384,128]{2,1,0:T(8,128)(2,1)S(1)}, u32[]{:S(2)}, u32[]{:S(2)}) %collective-permute-start) | collective-permute-done | bytes 786464 | tf_op jit(solution)/shard_map/ppermute | solution.py:484
  35.4 0.3 shard_map.146
  35.7 0.0 copy-start.7
  35.7 33.5 %all_to_all.21.refs_0_ = bf16[8,384,128]{2,1,0:T(8,128)(2,1)S(1)} all-to-all(bf16[8,384,128]{2,1,0:T(8,128)(2,1)S(1)} %shard_map.146), channel_id=1, replica_groups=mesh['z'=8,'core'=2,'x'=4,'y'=8] {'z'}, dimensions={0} | all-to-all | bytes 1572864 | tf_op jit(solution)/shard_map/all_to_all | solution.py:486
  69.3 0.0 copy-done.7
  69.3 0.3 shard_map.147
  69.6 22.3 %all_to_all.22.refs_0_ = bf16[8,328,128]{2,1,0:T(8,128)(2,1)S(1)} all-to-all(bf16[8,328,128]{2,1,0:T(8,128)(2,1)S(1)} %get-tuple-element.31), channel_id=1, replica_groups=mesh['z'=8,'core'=2,'x'=4,'y'=8] {'z'}, dimensions={0} | all-to-all | bytes 1343488 | tf_op jit(solution)/shard_map/all_to_all | solution.py:495
  91.9 1.9 %collective-permute-start.1 = (bf16[8,328,128]{2,1,0:T(8,128)(2,1)S(1)}, bf16[8,328,128]{2,1,0:T(8,128)(2,1)S(1)}, u32[]{:S(2)}, u32[]{:S(2)}) collective-permute-start(bf16[8,328,128]{2,1,0:T(8,128)(2,1)S(1)} %all_to_all.22.refs_0_), channel_id=1, source_target_pairs={{0,32},{32,0},{1,33},{33,1},{2,34},{34,2},{3,35},{35,3},{4,36},{36... | collective-permute-start | bytes 2015240 | tf_op jit(solution)/shard_map/ppermute | solution.py:496
  93.8 0.5 shard_map.148
  94.3 1.6 %collective-permute-done.1.refs_3_ = bf16[8,328,128]{2,1,0:T(8,128)(2,1)S(1)} collective-permute-done((bf16[8,328,128]{2,1,0:T(8,128)(2,1)S(1)}, bf16[8,328,128]{2,1,0:T(8,128)(2,1)S(1)}, u32[]{:S(2)}, u32[]{:S(2)}) %collective-permute-start.1) | collective-permute-done | bytes 671776 | tf_op jit(solution)/shard_map/ppermute | solution.py:496
  95.9 3.3 %shard_map.149 = (bf16[32,64,128]{2,1,0:T(8,128)(2,1)}, f32[2,128]{1,0:T(2,128)S(1)}, bf16[320,128]{1,0:T(8,128)(2,1)S(1)}, bf16[320,768]{1,0:T(8,128)(2,1)S(1)}...) custom-call(bf16[160,2048]{1,0:T(8,128)(2,1)S(1)} %get-tuple-element, ...), custom_call_target="tpu_custom_call" | custom-call | tf_op jit(solution)/shard_map/pallas_call | solution.py:65
  99.2 4.9 %all-to-all-start.3 = ((bf16[32,64,128]{2,1,0:T(8,128)(2,1)}), bf16[32,64,128]{2,1,0:T(8,128)(2,1)S(1)}, u32[]{:S(2)}, u32[]{:S(2)}) async-start(bf16[32,64,128]{2,1,0:T(8,128)(2,1)} %get-tuple-element.36), calls=%async_computation.3 | async-start | bytes 1048576 | tf_op jit(solution)/shard_map/all_to_all | solution.py:543
  104.0 0.4 convolution_convert_fusion.2
  104.4 0.9 copy.16
  105.3 0.9 convolution_convert_fusion.3
  106.2 0.0 copy-start.4
  106.2 0.0 copy-start.5
  106.2 1.4 %convolution_convert_fusion = bf16[768,384]{1,0:T(8,128)(2,1)} fusion(bf16[320,768]{1,0:T(8,128)(2,1)S(1)} %get-tuple-element.47, bf16[320,384]{1,0:T(8,128)(2,1)S(1)} %get-tuple-element.29.refs_1_), kind=kOutput, calls=%fused_computation | convolution fusion | flops 189038592 | bytes 1327104 | tf_op jit(solution)/shard_map/dot_general | solution.py:22
  107.6 1.3 %convolution_convert_fusion.1 = bf16[384,768]{1,0:T(8,128)(2,1)} fusion(bf16[320,384]{1,0:T(8,128)(2,1)S(1)} %get-tuple-element.42, bf16[320,768]{1,0:T(8,128)(2,1)S(1)} %get-tuple-element.45), kind=kOutput, calls=%fused_computation.1 | convolution fusion | flops 189038592 | bytes 1327104 | tf_op jit(solution)/shard_map/dot_general | solution.py:22
  108.9 13.1 %all-to-all-done.3.refs_0_ = bf16[32,64,128]{2,1,0:T(8,128)(2,1)S(1)} async-done(((bf16[32,64,128]{2,1,0:T(8,128)(2,1)}), bf16[32,64,128]{2,1,0:T(8,128)(2,1)S(1)}, u32[]{:S(2)}, u32[]{:S(2)}) %all-to-all-start.3) | async-done | bytes 524320 | tf_op jit(solution)/shard_map/all_to_all | solution.py:543
  122.0 0.0 copy-done.4
  122.0 0.0 copy-done.5
  122.0 0.7 shard_map.150
Async XLA Ops:
  0.6 29.5 %copy-start.1 = (bf16[768,384]{1,0:T(8,128)(2,1)S(1)}, bf16[768,384]{1,0:T(8,128)(2,1)}, u32[]{:S(2)}) copy-start(bf16[768,384]{1,0:T(8,128)(2,1)} %refs_11_.1) | copy-start | bytes 1769476
  0.6 29.5 %copy-start = (bf16[384,768]{1,0:T(8,128)(2,1)S(1)}, bf16[384,768]{1,0:T(8,128)(2,1)}, u32[]{:S(2)}) copy-start(bf16[384,768]{1,0:T(8,128)(2,1)} %refs_9_.1) | copy-start | bytes 1769476
  0.7 29.5 %copy-start.6 = (f32[384]{0:T(512)S(1)}, f32[384]{0:T(512)}, u32[]{:S(2)}) copy-start(f32[384]{0:T(512)} %refs_4_.5) | copy-start | bytes 4612
  0.7 29.5 %copy-start.3 = (bf16[128,384]{1,0:T(8,128)(2,1)S(1)}, bf16[128,384]{1,0:T(8,128)(2,1)}, u32[]{:S(2)}) copy-start(bf16[128,384]{1,0:T(8,128)(2,1)} %refs_10_.1) | copy-start | bytes 294916
  0.7 29.5 %copy-start.2 = (bf16[384,3,128]{2,0,1:T(8,128)(2,1)S(1)}, bf16[384,3,128]{2,0,1:T(8,128)(2,1)}, u32[]{:S(2)}) copy-start(bf16[384,3,128]{2,0,1:T(8,128)(2,1)} %param.10) | copy-start | bytes 884740
  31.2 4.2 %collective-permute-start = (bf16[8,384,128]{2,1,0:T(8,128)(2,1)S(1)}, bf16[8,384,128]{2,1,0:T(8,128)(2,1)S(1)}, u32[]{:S(2)}, u32[]{:S(2)}) collective-permute-start(bf16[8,384,128]{2,1,0:T(8,128)(2,1)S(1)} %get-tuple-element.30), channel_id=1, source_target_pairs={{0,32},{32,0},{1,33},{33,1},{2,34},{34,2},{3,35},{35,3},{4,36},{36... | collective-permute-start | bytes 2359304 | tf_op jit(solution)/shard_map/ppermute | solution.py:484
  35.7 33.5 %copy-start.7 = (f32[2,128]{1,0:T(2,128)S(1)}, f32[2,128]{1,0:T(2,128)}, u32[]{:S(2)}) copy-start(f32[2,128]{1,0:T(2,128)} %refs_7_.1) | copy-start | bytes 3076
  91.9 4.0 %collective-permute-start.1 = (bf16[8,328,128]{2,1,0:T(8,128)(2,1)S(1)}, bf16[8,328,128]{2,1,0:T(8,128)(2,1)S(1)}, u32[]{:S(2)}, u32[]{:S(2)}) collective-permute-start(bf16[8,328,128]{2,1,0:T(8,128)(2,1)S(1)} %all_to_all.22.refs_0_), channel_id=1, source_target_pairs={{0,32},{32,0},{1,33},{33,1},{2,34},{34,2},{3,35},{35,3},{4,36},{36... | collective-permute-start | bytes 2015240 | tf_op jit(solution)/shard_map/ppermute | solution.py:496
  99.2 22.8 %all-to-all-start.3 = ((bf16[32,64,128]{2,1,0:T(8,128)(2,1)}), bf16[32,64,128]{2,1,0:T(8,128)(2,1)S(1)}, u32[]{:S(2)}, u32[]{:S(2)}) async-start(bf16[32,64,128]{2,1,0:T(8,128)(2,1)} %get-tuple-element.36), calls=%async_computation.3 | async-start | bytes 1048576 | tf_op jit(solution)/shard_map/all_to_all | solution.py:543
  106.2 15.8 %copy-start.4 = (bf16[10,384]{1,0:T(8,128)(2,1)S(1)}, bf16[10,384]{1,0:T(8,128)(2,1)}, u32[]{:S(2)}) copy-start(bf16[10,384]{1,0:T(8,128)(2,1)} %refs_2_.5) | copy-start | bytes 23044
  106.2 15.8 %copy-start.5 = (bf16[10,384]{1,0:T(8,128)(2,1)S(1)}, bf16[10,384]{1,0:T(8,128)(2,1)}, u32[]{:S(2)}) copy-start(bf16[10,384]{1,0:T(8,128)(2,1)} %refs_3_.3) | copy-start | bytes 23044

commit v6 on v5

--- a/solution.py
+++ b/solution.py
@@ -142,9 +142,10 @@
     place = lax.rem(lax.broadcasted_iota(jnp.int32, (half, LANES), 0), rows)
     st[...] = jnp.where(lane == place, s_1, 0.0) + jnp.where(lane == place + 32, s_2, 0.0)
     c_rows = jnp.concatenate(fine + [c_vec[:, tile(j)] for j in range(2, f_tiles)], 0)
-    c_rows, c_low = split(c_rows, 2)
+    c_high, c_low = split(c_rows[0:3], 2)
+    c_rows = jnp.concatenate([c_high, c_rows[3:]], 0)
     low_at = f_sum + b_tiles * rows
-    fill = jnp.zeros((lay.shape[1] - low_at - 2 * rows - f_tiles, LANES), F32)
+    fill = jnp.zeros((lay.shape[1] - low_at - 2 * rows - 3, LANES), F32)
     c_low = jnp.concatenate([c_low, fill], 0)
     for d in range(n_z):
         at = slice(d * rows, (d + 1) * rows)
@@ -172,11 +173,10 @@
 
 
 def fine_pairs(rows, f_sum, low_at):
-    tiles = f_sum // (rows + 1)
-    c_at, c_low_at = tiles * rows, low_at + 2 * rows
+    c_at, c_low_at = f_sum // (rows + 1) * rows, low_at + 2 * rows
     return (
         (slice(0, 2 * rows), slice(low_at, low_at + 2 * rows)),
-        (slice(c_at, c_at + tiles), slice(c_low_at, c_low_at + tiles)),
+        (slice(c_at, c_at + 3), slice(c_low_at, c_low_at + 3)),
     )
 
 
@@ -324,7 +324,7 @@
     scale = LANES ** (-0.5)
     scores = dot(q, k, NT) * scale
     probs = jnp.exp(scores - jnp.max(scores, -1, keepdims=True))
-    probs = probs / jnp.sum(probs, -1, keepdims=True)
+    probs = probs * (1.0 / jnp.sum(probs, -1, keepdims=True))
     low = probs.astype(BF16)
     attended = dot(low, v, NN).astype(BF16)
     att_ref[...] = attended
@@ -340,14 +340,14 @@
 
     def back(rows_low, i, g, d_rows):
         rstd, average = scalar(i), scalar(i + 2)
-        unit = rows_low.astype(F32) / g
+        unit = rows_low.astype(F32) * (1.0 / g)
         d_unit = d_rows * g
         d_values = (
             d_unit
             - jnp.mean(d_unit, -1, keepdims=True)
             - unit * jnp.mean(d_unit * unit, -1, keepdims=True)
         ) * rstd
-        return d_values.astype(BF16), jnp.sum(d_rows * unit, 0, keepdims=True), unit / rstd + average
+        return d_values.astype(BF16), jnp.sum(d_rows * unit, 0, keepdims=True), unit * (1.0 / rstd) + average
 
     d_q, g_q, query = back(q, 0, qk_gain_ref[0:1], d_qn)
     d_k, g_k, key = back(k, 1, qk_gain_ref[1:2], d_kn)
@@ -432,7 +432,7 @@
     tiles = (in_w + out_w) // LANES
     f_sum = in_w // LANES * (rows + 1) + 3
     low_at = f_sum + out_w // LANES * rows
-    sum_rows = -(-(low_at + 2 * rows + in_w // LANES) // 16) * 16
+    sum_rows = -(-(low_at + 2 * rows + 3) // 8) * 8
     row_rows = tiles * rows + 8
     col_rows = 2 * width // LANES * rows_c + width // LANES + 1
 

time: 123 us -> 123 us (level)
  no operation moved by 1% of the time
where the time goes in v6:
time: 123 us; the launch traced here: 122 us
  blocking collectives  83.3 us (68%)
  waiting for transfers between devices  15.9 us (13%)
  Pallas kernels  8.79 us (7%)
  starting transfers between devices  8.7 us (7%)
  matrix products  3.99 us (3%)
    all_to_all x1, blocking collectives, shards(): got = lax.all_to_all(half, 'z', 0, 0)  33.3 us
    all_to_all x1, blocking collectives, shards(): got = lax.all_to_all(sent, COL, 0, 0)  27.8 us
    all_to_all x1, blocking collectives, shards(): mine = lax.all_to_all(sent, 'z', 0, 0)  22.2 us
    all_to_all x1, waiting for transfers between devices, shards(): got = lax.all_to_all(sent, COL, 0, 0)  13 us
    pallas_call x7, Pallas kernels, call(): pl.pallas_call(kernel, out_shape=outs, in_specs=[pl.BlockSpec(memory_spac...  7.1 us
    all_to_all x1, starting transfers between devices, shards(): got = lax.all_to_all(sent, COL, 0, 0)  4.87 us
    dot_general x4, matrix products, dot(): return lax.dot_general(a, b, dims, preferred_element_type=F32)  3.99 us
  transfers between devices with their start and end apart: 3, of which 3 were waited for; matrix products, arithmetic and copies ran while one was open for 4% of the time, Pallas kernels for 1%

profile of v6, /device:TPU:8, one launch (start us, length us, event | category | flops | bytes accessed | tf_op | source)
XLA Modules:
  0.0 122.4 jit_solution(16055848553729548675)
XLA Ops:
  0.6 0.0 copy-start.1
  0.6 0.0 copy-start
  0.7 0.0 copy-start.6
  0.7 0.0 copy-start.3
  0.7 0.0 copy-start.2
  0.7 1.7 %shard_map.143 = bf16[32,64,128]{2,1,0:T(8,128)(2,1)} custom-call(bf16[10,384]{1,0:T(8,128)(2,1)} %refs_2_.5, bf16[10,384]{1,0:T(8,128)(2,1)} %refs_3_.3), custom_call_target="tpu_custom_call" | custom-call | tf_op jit(solution)/shard_map/pallas_call | solution.py:442
  2.4 27.8 %all_to_all.20.refs_0_ = bf16[32,64,128]{2,1,0:T(8,128)(2,1)S(1)} all-to-all(bf16[32,64,128]{2,1,0:T(8,128)(2,1)} %shard_map.143), channel_id=1, replica_groups=mesh['z'=8,'core'=2,'x'=4,'y'=8] {'x','y'}, dimensions={0} | all-to-all | bytes 1048576 | tf_op jit(solution)/shard_map/all_to_all | solution.py:454
  30.2 0.0 copy-done.1
  30.2 0.0 copy-done
  30.2 0.0 copy-done.6
  30.2 0.0 copy-done.3
  30.2 0.0 copy-done.2
  30.2 1.0 shard_map.144
  31.2 1.9 %collective-permute-start = (bf16[8,376,128]{2,1,0:T(8,128)(2,1)S(1)}, bf16[8,376,128]{2,1,0:T(8,128)(2,1)S(1)}, u32[]{:S(2)}, u32[]{:S(2)}) collective-permute-start(bf16[8,376,128]{2,1,0:T(8,128)(2,1)S(1)} %get-tuple-element.30), channel_id=1, source_target_pairs={{0,32},{32,0},{1,33},{33,1},{2,34},{34,2},{3,35},{35,3},{4,36},{36... | collective-permute-start | bytes 2310152 | tf_op jit(solution)/shard_map/ppermute | solution.py:484
  33.2 0.9 shard_map.145.refs_0_
  34.1 1.3 %collective-permute-done.refs_1_ = bf16[8,376,128]{2,1,0:T(8,128)(2,1)S(1)} collective-permute-done((bf16[8,376,128]{2,1,0:T(8,128)(2,1)S(1)}, bf16[8,376,128]{2,1,0:T(8,128)(2,1)S(1)}, u32[]{:S(2)}, u32[]{:S(2)}) %collective-permute-start) | collective-permute-done | bytes 770080 | tf_op jit(solution)/shard_map/ppermute | solution.py:484
  35.4 0.3 shard_map.146
  35.7 0.0 copy-start.7
  35.7 33.3 %all_to_all.21.refs_0_ = bf16[8,376,128]{2,1,0:T(8,128)(2,1)S(1)} all-to-all(bf16[8,376,128]{2,1,0:T(8,128)(2,1)S(1)} %shard_map.146), channel_id=1, replica_groups=mesh['z'=8,'core'=2,'x'=4,'y'=8] {'z'}, dimensions={0} | all-to-all | bytes 1540096 | tf_op jit(solution)/shard_map/all_to_all | solution.py:486
  69.0 0.0 copy-done.7
  69.0 0.3 shard_map.147
  69.3 22.2 %all_to_all.22.refs_0_ = bf16[8,328,128]{2,1,0:T(8,128)(2,1)S(1)} all-to-all(bf16[8,328,128]{2,1,0:T(8,128)(2,1)S(1)} %get-tuple-element.31), channel_id=1, replica_groups=mesh['z'=8,'core'=2,'x'=4,'y'=8] {'z'}, dimensions={0} | all-to-all | bytes 1343488 | tf_op jit(solution)/shard_map/all_to_all | solution.py:495
  91.5 1.9 %collective-permute-start.1 = (bf16[8,328,128]{2,1,0:T(8,128)(2,1)S(1)}, bf16[8,328,128]{2,1,0:T(8,128)(2,1)S(1)}, u32[]{:S(2)}, u32[]{:S(2)}) collective-permute-start(bf16[8,328,128]{2,1,0:T(8,128)(2,1)S(1)} %all_to_all.22.refs_0_), channel_id=1, source_target_pairs={{0,32},{32,0},{1,33},{33,1},{2,34},{34,2},{3,35},{35,3},{4,36},{36... | collective-permute-start | bytes 2015240 | tf_op jit(solution)/shard_map/ppermute | solution.py:496
  93.5 0.5 shard_map.148
  94.0 1.6 %collective-permute-done.1.refs_3_ = bf16[8,328,128]{2,1,0:T(8,128)(2,1)S(1)} collective-permute-done((bf16[8,328,128]{2,1,0:T(8,128)(2,1)S(1)}, bf16[8,328,128]{2,1,0:T(8,128)(2,1)S(1)}, u32[]{:S(2)}, u32[]{:S(2)}) %collective-permute-start.1) | collective-permute-done | bytes 671776 | tf_op jit(solution)/shard_map/ppermute | solution.py:496
  95.6 3.3 %shard_map.149 = (bf16[32,64,128]{2,1,0:T(8,128)(2,1)}, f32[2,128]{1,0:T(2,128)S(1)}, bf16[320,128]{1,0:T(8,128)(2,1)S(1)}, bf16[320,768]{1,0:T(8,128)(2,1)S(1)}...) custom-call(bf16[160,2048]{1,0:T(8,128)(2,1)S(1)} %get-tuple-element, ...), custom_call_target="tpu_custom_call" | custom-call | tf_op jit(solution)/shard_map/pallas_call | solution.py:65
  98.9 4.9 %all-to-all-start.3 = ((bf16[32,64,128]{2,1,0:T(8,128)(2,1)}), bf16[32,64,128]{2,1,0:T(8,128)(2,1)S(1)}, u32[]{:S(2)}, u32[]{:S(2)}) async-start(bf16[32,64,128]{2,1,0:T(8,128)(2,1)} %get-tuple-element.36), calls=%async_computation.3 | async-start | bytes 1048576 | tf_op jit(solution)/shard_map/all_to_all | solution.py:543
  103.7 0.4 convolution_convert_fusion.2
  104.1 0.9 copy.16
  105.0 0.9 convolution_convert_fusion.3
  105.9 0.0 copy-start.4
  105.9 0.0 copy-start.5
  105.9 1.4 %convolution_convert_fusion = bf16[768,384]{1,0:T(8,128)(2,1)} fusion(bf16[320,768]{1,0:T(8,128)(2,1)S(1)} %get-tuple-element.47, bf16[320,384]{1,0:T(8,128)(2,1)S(1)} %get-tuple-element.29.refs_1_), kind=kOutput, calls=%fused_computation | convolution fusion | flops 189038592 | bytes 1327104 | tf_op jit(solution)/shard_map/dot_general | solution.py:22
  107.3 1.3 %convolution_convert_fusion.1 = bf16[384,768]{1,0:T(8,128)(2,1)} fusion(bf16[320,384]{1,0:T(8,128)(2,1)S(1)} %get-tuple-element.42, bf16[320,768]{1,0:T(8,128)(2,1)S(1)} %get-tuple-element.45), kind=kOutput, calls=%fused_computation.1 | convolution fusion | flops 189038592 | bytes 1327104 | tf_op jit(solution)/shard_map/dot_general | solution.py:22
  108.6 13.0 %all-to-all-done.3.refs_0_ = bf16[32,64,128]{2,1,0:T(8,128)(2,1)S(1)} async-done(((bf16[32,64,128]{2,1,0:T(8,128)(2,1)}), bf16[32,64,128]{2,1,0:T(8,128)(2,1)S(1)}, u32[]{:S(2)}, u32[]{:S(2)}) %all-to-all-start.3) | async-done | bytes 524320 | tf_op jit(solution)/shard_map/all_to_all | solution.py:543
  121.7 0.0 copy-done.4
  121.7 0.0 copy-done.5
  121.7 0.7 shard_map.150
Async XLA Ops:
  0.6 29.5 %copy-start.1 = (bf16[768,384]{1,0:T(8,128)(2,1)S(1)}, bf16[768,384]{1,0:T(8,128)(2,1)}, u32[]{:S(2)}) copy-start(bf16[768,384]{1,0:T(8,128)(2,1)} %refs_11_.1) | copy-start | bytes 1769476
  0.6 29.5 %copy-start = (bf16[384,768]{1,0:T(8,128)(2,1)S(1)}, bf16[384,768]{1,0:T(8,128)(2,1)}, u32[]{:S(2)}) copy-start(bf16[384,768]{1,0:T(8,128)(2,1)} %refs_9_.1) | copy-start | bytes 1769476
  0.7 29.5 %copy-start.6 = (f32[384]{0:T(512)S(1)}, f32[384]{0:T(512)}, u32[]{:S(2)}) copy-start(f32[384]{0:T(512)} %refs_4_.5) | copy-start | bytes 4612
  0.7 29.5 %copy-start.3 = (bf16[128,384]{1,0:T(8,128)(2,1)S(1)}, bf16[128,384]{1,0:T(8,128)(2,1)}, u32[]{:S(2)}) copy-start(bf16[128,384]{1,0:T(8,128)(2,1)} %refs_10_.1) | copy-start | bytes 294916
  0.7 29.5 %copy-start.2 = (bf16[384,3,128]{2,0,1:T(8,128)(2,1)S(1)}, bf16[384,3,128]{2,0,1:T(8,128)(2,1)}, u32[]{:S(2)}) copy-start(bf16[384,3,128]{2,0,1:T(8,128)(2,1)} %param.10) | copy-start | bytes 884740
  31.2 4.2 %collective-permute-start = (bf16[8,376,128]{2,1,0:T(8,128)(2,1)S(1)}, bf16[8,376,128]{2,1,0:T(8,128)(2,1)S(1)}, u32[]{:S(2)}, u32[]{:S(2)}) collective-permute-start(bf16[8,376,128]{2,1,0:T(8,128)(2,1)S(1)} %get-tuple-element.30), channel_id=1, source_target_pairs={{0,32},{32,0},{1,33},{33,1},{2,34},{34,2},{3,35},{35,3},{4,36},{36... | collective-permute-start | bytes 2310152 | tf_op jit(solution)/shard_map/ppermute | solution.py:484
  35.7 33.3 %copy-start.7 = (f32[2,128]{1,0:T(2,128)S(1)}, f32[2,128]{1,0:T(2,128)}, u32[]{:S(2)}) copy-start(f32[2,128]{1,0:T(2,128)} %refs_7_.1) | copy-start | bytes 3076
  91.5 4.0 %collective-permute-start.1 = (bf16[8,328,128]{2,1,0:T(8,128)(2,1)S(1)}, bf16[8,328,128]{2,1,0:T(8,128)(2,1)S(1)}, u32[]{:S(2)}, u32[]{:S(2)}) collective-permute-start(bf16[8,328,128]{2,1,0:T(8,128)(2,1)S(1)} %all_to_all.22.refs_0_), channel_id=1, source_target_pairs={{0,32},{32,0},{1,33},{33,1},{2,34},{34,2},{3,35},{35,3},{4,36},{36... | collective-permute-start | bytes 2015240 | tf_op jit(solution)/shard_map/ppermute | solution.py:496
  98.9 22.8 %all-to-all-start.3 = ((bf16[32,64,128]{2,1,0:T(8,128)(2,1)}), bf16[32,64,128]{2,1,0:T(8,128)(2,1)S(1)}, u32[]{:S(2)}, u32[]{:S(2)}) async-start(bf16[32,64,128]{2,1,0:T(8,128)(2,1)} %get-tuple-element.36), calls=%async_computation.3 | async-start | bytes 1048576 | tf_op jit(solution)/shard_map/all_to_all | solution.py:543
  105.9 15.7 %copy-start.4 = (bf16[10,384]{1,0:T(8,128)(2,1)S(1)}, bf16[10,384]{1,0:T(8,128)(2,1)}, u32[]{:S(2)}) copy-start(bf16[10,384]{1,0:T(8,128)(2,1)} %refs_2_.5) | copy-start | bytes 23044
  105.9 15.7 %copy-start.5 = (bf16[10,384]{1,0:T(8,128)(2,1)S(1)}, bf16[10,384]{1,0:T(8,128)(2,1)}, u32[]{:S(2)}) copy-start(bf16[10,384]{1,0:T(8,128)(2,1)} %refs_3_.3) | copy-start | bytes 23044

commit v7 on v6

--- a/solution.py
+++ b/solution.py
@@ -145,7 +145,8 @@
     c_high, c_low = split(c_rows[0:3], 2)
     c_rows = jnp.concatenate([c_high, c_rows[3:]], 0)
     low_at = f_sum + b_tiles * rows
-    fill = jnp.zeros((lay.shape[1] - low_at - 2 * rows - 3, LANES), F32)
+    fine_at = lay.shape[1] - 2 * rows
+    fill = jnp.zeros((fine_at - low_at - 3, LANES), F32)
     c_low = jnp.concatenate([c_low, fill], 0)
     for d in range(n_z):
         at = slice(d * rows, (d + 1) * rows)
@@ -156,8 +157,8 @@
         for j in range(b_tiles):
             lay[d, f_sum + j * rows : f_sum + (j + 1) * rows, :] = gs[at, tile(j)]
         for j in range(2):
-            lay[d, low_at + j * rows : low_at + (j + 1) * rows, :] = fs[at, tile(j)]
-        lay[d, low_at + 2 * rows :, :] = c_low
+            lay[d, fine_at + j * rows : fine_at + (j + 1) * rows, :] = fs[at, tile(j)]
+        lay[d, low_at:fine_at, :] = c_low
     out_ref[...] = lay[...].astype(out_ref.dtype)
 
 
@@ -172,24 +173,23 @@
     products(core, rows, x_ref, cot_ref, gain_ref, wq_ref, wu_ref, wa_ref, wd_ref, out_ref, *scr)
 
 
-def fine_pairs(rows, f_sum, low_at):
-    c_at, c_low_at = f_sum // (rows + 1) * rows, low_at + 2 * rows
-    return (
-        (slice(0, 2 * rows), slice(low_at, low_at + 2 * rows)),
-        (slice(c_at, c_at + 3), slice(c_low_at, c_low_at + 3)),
-    )
+def gain_parts(rows, f_sum, low_at):
+    c_at = f_sum // (rows + 1) * rows
+    return slice(c_at, c_at + 3), slice(low_at, low_at + 3)
 
 
 def add_kernel(rows, f_sum, low_at, own_ref, came_ref, out_ref, block):
+    length = out_ref.shape[1]
+    high, low = gain_parts(rows, f_sum, low_at)
     for d in range(own_ref.shape[0]):
         block[...] = own_ref[d] + came_ref[d].astype(F32)
-        for high, low in fine_pairs(rows, f_sum, low_at):
-            whole = block[high, :] + block[low, :]
-            block[high, :] = whole.astype(BF16).astype(F32)
-            block[low, :] = whole - block[high, :]
+        block[0 : 2 * rows, :] = block[0 : 2 * rows, :] + block[length:, :]
+        whole = block[high, :] + block[low, :]
+        block[high, :] = whole.astype(BF16).astype(F32)
+        block[low, :] = whole - block[high, :]
         stat = jnp.sum(block[f_sum - 3 : f_sum, :], 0, keepdims=True)
         block[f_sum - 3 : f_sum, :] = jnp.concatenate(split(stat, 3), 0)
-        out_ref[d] = block[...].astype(BF16)
+        out_ref[d] = block[0:length, :].astype(BF16)
 
 
 def gelu_parts(x):
@@ -211,8 +211,8 @@
     model_width, rows, f_sum, low_at, got_ref, qk_gain_ref, out_ref, c_ref, tot, block
 ):
     sum_blocks(got_ref, tot)
-    for high, low in fine_pairs(rows, f_sum, low_at):
-        tot[high, :] = tot[high, :] + tot[low, :]
+    high, low = gain_parts(rows, f_sum, low_at)
+    tot[high, :] = tot[high, :] + tot[low, :]
     tiles = (f_sum - 3) // (rows + 1)
     c_ref[0:tiles, :] = tot[tiles * rows : tiles * rows + tiles, :]
     c_ref[tiles:, :] = jnp.zeros((c_ref.shape[0] - tiles, LANES), F32)
@@ -432,7 +432,8 @@
     tiles = (in_w + out_w) // LANES
     f_sum = in_w // LANES * (rows + 1) + 3
     low_at = f_sum + out_w // LANES * rows
-    sum_rows = -(-(low_at + 2 * rows + 3) // 8) * 8
+    z_rows = -(-(low_at + 3) // 16) * 16
+    sum_rows = z_rows + 2 * rows
     row_rows = tiles * rows + 8
     col_rows = 2 * width // LANES * rows_c + width // LANES + 1
 
@@ -478,7 +479,7 @@
     )
     (half,) = call(
         lambda *refs: add_kernel(rows, f_sum, low_at, *refs),
-        [shape((n_z, sum_rows, LANES))],
+        [shape((n_z, z_rows, LANES))],
         [scratch(sum_rows, LANES)],
         own,
         lax.ppermute(other, "core", swap),
@@ -488,7 +489,7 @@
     sent, c_vec = call(
         lambda *refs: row_kernel(model_width, rows, f_sum, low_at, *refs),
         [shape((n_z, row_rows, LANES)), shape((16, LANES), F32)],
-        [scratch(sum_rows, LANES), scratch(row_rows, LANES)],
+        [scratch(z_rows, LANES), scratch(row_rows, LANES)],
         got,
         qk_gain,
     )

time: 123 us -> 121 us (0.984)
  blocking collectives: 83.3 us -> 81.6 us
    all_to_all x1, blocking collectives: 33.3 us -> 31.6 us  [shards(): got = lax.all_to_all(half, 'z', 0, 0)]
where the time goes in v7:
time: 121 us
  blocking collectives  81.6 us (67%)
  waiting for transfers between devices  15.9 us (13%)
  Pallas kernels  8.78 us (7%)
  starting transfers between devices  8.7 us (7%)
  matrix products  3.99 us (3%)
    all_to_all x1, blocking collectives, shards(): got = lax.all_to_all(half, 'z', 0, 0)  31.6 us
    all_to_all x1, blocking collectives, shards(): got = lax.all_to_all(sent, COL, 0, 0)  27.8 us
    all_to_all x1, blocking collectives, shards(): mine = lax.all_to_all(sent, 'z', 0, 0)  22.3 us
    all_to_all x1, waiting for transfers between devices, shards(): got = lax.all_to_all(sent, COL, 0, 0)  13 us
    pallas_call x7, Pallas kernels, call(): pl.pallas_call(kernel, out_shape=outs, in_specs=[pl.BlockSpec(memory_spac...  7.08 us
    all_to_all x1, starting transfers between devices, shards(): got = lax.all_to_all(sent, COL, 0, 0)  4.87 us
    dot_general x4, matrix products, dot(): return lax.dot_general(a, b, dims, preferred_element_type=F32)  3.99 us
  transfers between devices with their start and end apart: 3, of which 3 were waited for; matrix products, arithmetic and copies ran while one was open for 4% of the time, Pallas kernels for 1%

profile of v7, /device:TPU:8, one launch (start us, length us, event | category | flops | bytes accessed | tf_op | source)
XLA Modules:
  0.0 120.7 jit_solution(17365040150032779431)
XLA Ops:
  0.6 0.0 copy-start.1
  0.6 0.0 copy-start
  0.7 0.0 copy-start.6
  0.7 0.0 copy-start.3
  0.7 0.0 copy-start.2
  0.7 1.7 %shard_map.143 = bf16[32,64,128]{2,1,0:T(8,128)(2,1)} custom-call(bf16[10,384]{1,0:T(8,128)(2,1)} %refs_2_.5, bf16[10,384]{1,0:T(8,128)(2,1)} %refs_3_.3), custom_call_target="tpu_custom_call" | custom-call | tf_op jit(solution)/shard_map/pallas_call | solution.py:443
  2.4 27.8 %all_to_all.20.refs_0_ = bf16[32,64,128]{2,1,0:T(8,128)(2,1)S(1)} all-to-all(bf16[32,64,128]{2,1,0:T(8,128)(2,1)} %shard_map.143), channel_id=1, replica_groups=mesh['z'=8,'core'=2,'x'=4,'y'=8] {'x','y'}, dimensions={0} | all-to-all | bytes 1048576 | tf_op jit(solution)/shard_map/all_to_all | solution.py:455
  30.2 0.0 copy-done.1
  30.2 0.0 copy-done
  30.2 0.0 copy-done.6
  30.2 0.0 copy-done.3
  30.2 0.0 copy-done.2
  30.2 1.0 shard_map.144
  31.2 1.9 %collective-permute-start = (bf16[8,376,128]{2,1,0:T(8,128)(2,1)S(1)}, bf16[8,376,128]{2,1,0:T(8,128)(2,1)S(1)}, u32[]{:S(2)}, u32[]{:S(2)}) collective-permute-start(bf16[8,376,128]{2,1,0:T(8,128)(2,1)S(1)} %get-tuple-element.30), channel_id=1, source_target_pairs={{0,32},{32,0},{1,33},{33,1},{2,34},{34,2},{3,35},{35,3},{4,36},{36... | collective-permute-start | bytes 2310152 | tf_op jit(solution)/shard_map/ppermute | solution.py:485
  33.2 0.9 shard_map.145.refs_0_
  34.1 1.3 %collective-permute-done.refs_1_ = bf16[8,376,128]{2,1,0:T(8,128)(2,1)S(1)} collective-permute-done((bf16[8,376,128]{2,1,0:T(8,128)(2,1)S(1)}, bf16[8,376,128]{2,1,0:T(8,128)(2,1)S(1)}, u32[]{:S(2)}, u32[]{:S(2)}) %collective-permute-start) | collective-permute-done | bytes 770080 | tf_op jit(solution)/shard_map/ppermute | solution.py:485
  35.4 0.3 shard_map.146
  35.7 0.0 copy-start.7
  35.7 31.6 %all_to_all.21.refs_0_ = bf16[8,336,128]{2,1,0:T(8,128)(2,1)S(1)} all-to-all(bf16[8,336,128]{2,1,0:T(8,128)(2,1)S(1)} %shard_map.146), channel_id=1, replica_groups=mesh['z'=8,'core'=2,'x'=4,'y'=8] {'z'}, dimensions={0} | all-to-all | bytes 1376256 | tf_op jit(solution)/shard_map/all_to_all | solution.py:487
  67.2 0.0 copy-done.7
  67.2 0.3 shard_map.147
  67.6 22.3 %all_to_all.22.refs_0_ = bf16[8,328,128]{2,1,0:T(8,128)(2,1)S(1)} all-to-all(bf16[8,328,128]{2,1,0:T(8,128)(2,1)S(1)} %get-tuple-element.31), channel_id=1, replica_groups=mesh['z'=8,'core'=2,'x'=4,'y'=8] {'z'}, dimensions={0} | all-to-all | bytes 1343488 | tf_op jit(solution)/shard_map/all_to_all | solution.py:496
  89.8 1.9 %collective-permute-start.1 = (bf16[8,328,128]{2,1,0:T(8,128)(2,1)S(1)}, bf16[8,328,128]{2,1,0:T(8,128)(2,1)S(1)}, u32[]{:S(2)}, u32[]{:S(2)}) collective-permute-start(bf16[8,328,128]{2,1,0:T(8,128)(2,1)S(1)} %all_to_all.22.refs_0_), channel_id=1, source_target_pairs={{0,32},{32,0},{1,33},{33,1},{2,34},{34,2},{3,35},{35,3},{4,36},{36... | collective-permute-start | bytes 2015240 | tf_op jit(solution)/shard_map/ppermute | solution.py:497
  91.8 0.5 shard_map.148
  92.3 1.6 %collective-permute-done.1.refs_3_ = bf16[8,328,128]{2,1,0:T(8,128)(2,1)S(1)} collective-permute-done((bf16[8,328,128]{2,1,0:T(8,128)(2,1)S(1)}, bf16[8,328,128]{2,1,0:T(8,128)(2,1)S(1)}, u32[]{:S(2)}, u32[]{:S(2)}) %collective-permute-start.1) | collective-permute-done | bytes 671776 | tf_op jit(solution)/shard_map/ppermute | solution.py:497
  93.8 3.3 %shard_map.149 = (bf16[32,64,128]{2,1,0:T(8,128)(2,1)}, f32[2,128]{1,0:T(2,128)S(1)}, bf16[320,128]{1,0:T(8,128)(2,1)S(1)}, bf16[320,768]{1,0:T(8,128)(2,1)S(1)}...) custom-call(bf16[160,2048]{1,0:T(8,128)(2,1)S(1)} %get-tuple-element, ...), custom_call_target="tpu_custom_call" | custom-call | tf_op jit(solution)/shard_map/pallas_call | solution.py:65
  97.1 4.9 %all-to-all-start.3 = ((bf16[32,64,128]{2,1,0:T(8,128)(2,1)}), bf16[32,64,128]{2,1,0:T(8,128)(2,1)S(1)}, u32[]{:S(2)}, u32[]{:S(2)}) async-start(bf16[32,64,128]{2,1,0:T(8,128)(2,1)} %get-tuple-element.36), calls=%async_computation.3 | async-start | bytes 1048576 | tf_op jit(solution)/shard_map/all_to_all | solution.py:544
  102.0 0.4 convolution_convert_fusion.2
  102.4 0.9 copy.16
  103.3 0.9 convolution_convert_fusion.3
  104.2 0.0 copy-start.4
  104.2 0.0 copy-start.5
  104.2 1.4 %convolution_convert_fusion = bf16[768,384]{1,0:T(8,128)(2,1)} fusion(bf16[320,768]{1,0:T(8,128)(2,1)S(1)} %get-tuple-element.47, bf16[320,384]{1,0:T(8,128)(2,1)S(1)} %get-tuple-element.29.refs_1_), kind=kOutput, calls=%fused_computation | convolution fusion | flops 189038592 | bytes 1327104 | tf_op jit(solution)/shard_map/dot_general | solution.py:22
  105.6 1.3 %convolution_convert_fusion.1 = bf16[384,768]{1,0:T(8,128)(2,1)} fusion(bf16[320,384]{1,0:T(8,128)(2,1)S(1)} %get-tuple-element.42, bf16[320,768]{1,0:T(8,128)(2,1)S(1)} %get-tuple-element.45), kind=kOutput, calls=%fused_computation.1 | convolution fusion | flops 189038592 | bytes 1327104 | tf_op jit(solution)/shard_map/dot_general | solution.py:22
  106.9 13.0 %all-to-all-done.3.refs_0_ = bf16[32,64,128]{2,1,0:T(8,128)(2,1)S(1)} async-done(((bf16[32,64,128]{2,1,0:T(8,128)(2,1)}), bf16[32,64,128]{2,1,0:T(8,128)(2,1)S(1)}, u32[]{:S(2)}, u32[]{:S(2)}) %all-to-all-start.3) | async-done | bytes 524320 | tf_op jit(solution)/shard_map/all_to_all | solution.py:544
  120.0 0.0 copy-done.4
  120.0 0.0 copy-done.5
  120.0 0.7 shard_map.150
Async XLA Ops:
  0.6 29.5 %copy-start.1 = (bf16[768,384]{1,0:T(8,128)(2,1)S(1)}, bf16[768,384]{1,0:T(8,128)(2,1)}, u32[]{:S(2)}) copy-start(bf16[768,384]{1,0:T(8,128)(2,1)} %refs_11_.1) | copy-start | bytes 1769476
  0.6 29.5 %copy-start = (bf16[384,768]{1,0:T(8,128)(2,1)S(1)}, bf16[384,768]{1,0:T(8,128)(2,1)}, u32[]{:S(2)}) copy-start(bf16[384,768]{1,0:T(8,128)(2,1)} %refs_9_.1) | copy-start | bytes 1769476
  0.7 29.5 %copy-start.6 = (f32[384]{0:T(512)S(1)}, f32[384]{0:T(512)}, u32[]{:S(2)}) copy-start(f32[384]{0:T(512)} %refs_4_.5) | copy-start | bytes 4612
  0.7 29.5 %copy-start.3 = (bf16[128,384]{1,0:T(8,128)(2,1)S(1)}, bf16[128,384]{1,0:T(8,128)(2,1)}, u32[]{:S(2)}) copy-start(bf16[128,384]{1,0:T(8,128)(2,1)} %refs_10_.1) | copy-start | bytes 294916
  0.7 29.5 %copy-start.2 = (bf16[384,3,128]{2,0,1:T(8,128)(2,1)S(1)}, bf16[384,3,128]{2,0,1:T(8,128)(2,1)}, u32[]{:S(2)}) copy-start(bf16[384,3,128]{2,0,1:T(8,128)(2,1)} %param.10) | copy-start | bytes 884740
  31.2 4.2 %collective-permute-start = (bf16[8,376,128]{2,1,0:T(8,128)(2,1)S(1)}, bf16[8,376,128]{2,1,0:T(8,128)(2,1)S(1)}, u32[]{:S(2)}, u32[]{:S(2)}) collective-permute-start(bf16[8,376,128]{2,1,0:T(8,128)(2,1)S(1)} %get-tuple-element.30), channel_id=1, source_target_pairs={{0,32},{32,0},{1,33},{33,1},{2,34},{34,2},{3,35},{35,3},{4,36},{36... | collective-permute-start | bytes 2310152 | tf_op jit(solution)/shard_map/ppermute | solution.py:485
  35.7 31.6 %copy-start.7 = (f32[2,128]{1,0:T(2,128)S(1)}, f32[2,128]{1,0:T(2,128)}, u32[]{:S(2)}) copy-start(f32[2,128]{1,0:T(2,128)} %refs_7_.1) | copy-start | bytes 3076
  89.8 4.0 %collective-permute-start.1 = (bf16[8,328,128]{2,1,0:T(8,128)(2,1)S(1)}, bf16[8,328,128]{2,1,0:T(8,128)(2,1)S(1)}, u32[]{:S(2)}, u32[]{:S(2)}) collective-permute-start(bf16[8,328,128]{2,1,0:T(8,128)(2,1)S(1)} %all_to_all.22.refs_0_), channel_id=1, source_target_pairs={{0,32},{32,0},{1,33},{33,1},{2,34},{34,2},{3,35},{35,3},{4,36},{36... | collective-permute-start | bytes 2015240 | tf_op jit(solution)/shard_map/ppermute | solution.py:497
  97.1 22.8 %all-to-all-start.3 = ((bf16[32,64,128]{2,1,0:T(8,128)(2,1)}), bf16[32,64,128]{2,1,0:T(8,128)(2,1)S(1)}, u32[]{:S(2)}, u32[]{:S(2)}) async-start(bf16[32,64,128]{2,1,0:T(8,128)(2,1)} %get-tuple-element.36), calls=%async_computation.3 | async-start | bytes 1048576 | tf_op jit(solution)/shard_map/all_to_all | solution.py:544
  104.2 15.7 %copy-start.4 = (bf16[10,384]{1,0:T(8,128)(2,1)S(1)}, bf16[10,384]{1,0:T(8,128)(2,1)}, u32[]{:S(2)}) copy-start(bf16[10,384]{1,0:T(8,128)(2,1)} %refs_2_.5) | copy-start | bytes 23044
  104.2 15.7 %copy-start.5 = (bf16[10,384]{1,0:T(8,128)(2,1)S(1)}, bf16[10,384]{1,0:T(8,128)(2,1)}, u32[]{:S(2)}) copy-start(bf16[10,384]{1,0:T(8,128)(2,1)} %refs_3_.3) | copy-start | bytes 23044
